TPU v7x, 128 devices: a whole 4x4x4 slice. The times are simulated.
128 devices in a mesh: seq: 16 (over y, z_hi, core), batch: 8 (over z_lo, x).
Axes of the slice: x: 4, y: 4, z: 4 (z_hi: 2, z_lo: 2; z = z_hi * 2 + z_lo), core: 2. Of those that a mesh axis runs over, the one named last changes fastest.
Arguments:
- base_codes: int32 [8, 2048], P('batch', 'seq'), may hold values from 0 to 3
- stem_weight: bfloat16 [15, 4, 768], replicated, may hold values from -1.5 to 1.5
- conv_weight: bfloat16 [3, 768, 768], replicated, may hold values from -0.125 to 0.125
- down_weight: bfloat16 [768, 1536], replicated, may hold values from -0.21875 to 0.21875
- norm_gain: float32 [1536], replicated, may hold values from 0.1 to 1.9
- query_weight: bfloat16 [1536, 1024], P(None, 'batch'), may hold values from -0.15625 to 0.15625
- key_weight: bfloat16 [1536, 1024], P(None, 'batch'), may hold values from -0.15625 to 0.15625
- value_weight: bfloat16 [1536, 1536], P(None, 'batch'), may hold values from -0.15625 to 0.15625
- output_weight: bfloat16 [1536, 1536], P('batch'), may hold values from -0.15625 to 0.15625
- up_weight: bfloat16 [1536, 768], replicated, may hold values from -0.15625 to 0.15625
- cotangent: bfloat16 [8, 2048, 768], P('batch', 'seq'), may hold values from -6 to 6
Outputs:
- features: bfloat16 [8, 2048, 768], P('batch', 'seq')
- grad_stem: float32 [15, 4, 768], P(None, None, ('seq', 'batch'))
- grad_conv: float32 [3, 768, 768], P(None, None, ('seq', 'batch'))
- grad_down: float32 [768, 1536], P(None, ('seq', 'batch'))
- grad_gain: float32 [1536], P(('seq', 'batch'))
- grad_up: float32 [1536, 768], P(None, ('seq', 'batch'))
- grad_query: float32 [1536, 1024], P('seq', 'batch')
- grad_key: float32 [1536, 1024], P('seq', 'batch')
- grad_value: float32 [1536, 1536], P('seq', 'batch')
- grad_out: float32 [1536, 1536], P('seq', 'batch')
All inputs are finite; a program needn't handle non-finite values.
Results may differ from a plain program's by a relative error of at most 0.035.
Values may be sent and summed in bfloat16 or wider, within the bound.
A program may use at most 128 MiB of HBM per device.

v0:
```python
import math

import jax
import jax.numpy as jnp
from jax import lax
from jax.sharding import PartitionSpec as P

HEADS = 8
DILATION = 8


EPSILON = 1e-06


def with_halo(block, sides, width):
    for axis, dim in sides:
        count = lax.axis_size(axis)
        forward = [(i, i + 1) for i in range(count - 1)]
        backward = [(target, source) for source, target in forward]
        low = lax.ppermute(
            lax.slice_in_dim(block, block.shape[dim] - width, None, axis=dim), axis, forward
        )
        high = lax.ppermute(lax.slice_in_dim(block, 0, width, axis=dim), axis, backward)
        block = jnp.concatenate([low, block, high], axis=dim)
    return block


def stem_embed(weights, padded_bases):
    tap_count = weights.shape[0]
    row_count = padded_bases.shape[1] - tap_count + 1
    codes = jnp.arange(1, 5, dtype=jnp.int32)
    windows = jnp.stack(
        [padded_bases[:, offset : offset + row_count] for offset in range(tap_count)], axis=2
    )
    one_hot = (windows[..., None] == codes).astype(jnp.bfloat16).reshape(-1, tap_count * 4)
    summed = jnp.dot(
        one_hot, weights.reshape(tap_count * 4, -1), preferred_element_type=jnp.float32
    )
    return summed.reshape(padded_bases.shape[0], row_count, -1).astype(jnp.bfloat16)


def conv_block(weights, padded):
    number, total, channel_count = padded.shape
    row_count = total - 2 * DILATION
    summed = jnp.zeros((number * row_count, channel_count), jnp.float32)
    for tap_index in range(3):
        shifted = padded[:, tap_index * DILATION : tap_index * DILATION + row_count].reshape(
            -1, channel_count
        )
        summed = summed + jnp.dot(shifted, weights[tap_index], preferred_element_type=jnp.float32)
    center = (
        padded[:, DILATION : DILATION + row_count].reshape(-1, channel_count).astype(jnp.float32)
    )
    return (
        (center + jax.nn.gelu(summed))
        .astype(jnp.bfloat16)
        .reshape(number, row_count, channel_count)
    )


def down_block(weights, gain_vector, towered):
    number, row_count, channel_count = towered.shape
    pairs = towered.reshape(number, row_count // 2, 2, channel_count).astype(jnp.float32)
    pooled = (
        (0.5 * (pairs[:, :, 0] + pairs[:, :, 1])).astype(jnp.bfloat16).reshape(-1, channel_count)
    )
    lifted = jnp.dot(pooled, weights, preferred_element_type=jnp.float32).astype(jnp.bfloat16)
    values_f = lifted.astype(jnp.float32)
    factor = lax.rsqrt(jnp.mean(values_f * values_f, axis=-1, keepdims=True) + EPSILON)
    normed = (values_f * factor * gain_vector).astype(jnp.bfloat16)
    return (lifted, normed)


def tail_block(weights, lifted, mixed, towered):
    number, row_count, channel_count = towered.shape
    updated = (lifted.astype(jnp.float32) + mixed).astype(jnp.bfloat16)
    lowered = jnp.dot(updated, weights, preferred_element_type=jnp.float32).reshape(
        number, row_count // 2, 1, channel_count
    )
    skipped = towered.reshape(number, row_count // 2, 2, channel_count).astype(jnp.float32)
    return (skipped + lowered).astype(jnp.bfloat16).reshape(number, row_count, channel_count)


def split_heads(array, heads):
    return array.reshape(array.shape[0], array.shape[1], heads, -1)


def head_scores(queries, keys, heads):
    query_heads = split_heads(queries, heads)
    factor = 1.0 / math.sqrt(query_heads.shape[-1])
    return (
        jnp.einsum(
            "nqhd,nkhd->nhqk",
            query_heads,
            split_heads(keys, heads),
            preferred_element_type=jnp.float32,
        )
        * factor
    )


def attend_rows(queries, keys, values, heads):
    scores = head_scores(queries, keys, heads)
    log_total = jnp.log(jnp.sum(jnp.exp(scores), axis=-1, keepdims=True))
    weights_b = jnp.exp(scores - log_total).astype(jnp.bfloat16)
    output = jnp.einsum(
        "nhqk,nkhd->nqhd", weights_b, split_heads(values, heads), preferred_element_type=jnp.float32
    )
    output = output.astype(jnp.bfloat16).reshape(queries.shape[0], queries.shape[1], -1)
    return (output, jnp.transpose(log_total[..., 0], (0, 2, 1)))


def query_grads(queries, keys, values, log_total, d_attended, heads):
    scores = head_scores(queries, keys, heads)
    softmax_weights = jnp.exp(scores - jnp.transpose(log_total, (0, 2, 1))[..., None])
    d_weights = jnp.einsum(
        "nqhd,nkhd->nhqk",
        split_heads(d_attended, heads),
        split_heads(values, heads),
        preferred_element_type=jnp.float32,
    )
    inner_term = jnp.sum(softmax_weights * d_weights, axis=-1)
    d_scores = (softmax_weights * (d_weights - inner_term[..., None])).astype(jnp.bfloat16)
    key_heads = split_heads(keys, heads)
    factor = 1.0 / math.sqrt(key_heads.shape[-1])
    d_queries = (
        jnp.einsum("nhqk,nkhd->nqhd", d_scores, key_heads, preferred_element_type=jnp.float32)
        * factor
    )
    return (
        d_queries.reshape(queries.shape[0], queries.shape[1], -1),
        jnp.transpose(inner_term, (0, 2, 1)),
    )


def key_grads(queries, d_attended, log_total, inner_term, keys, values, heads):
    scores = head_scores(queries, keys, heads)
    softmax_weights = jnp.exp(scores - jnp.transpose(log_total, (0, 2, 1))[..., None])
    d_heads = split_heads(d_attended, heads)
    d_weights = jnp.einsum(
        "nqhd,nkhd->nhqk", d_heads, split_heads(values, heads), preferred_element_type=jnp.float32
    )
    d_scores = (
        softmax_weights * (d_weights - jnp.transpose(inner_term, (0, 2, 1))[..., None])
    ).astype(jnp.bfloat16)
    query_heads = split_heads(queries, heads)
    factor = 1.0 / math.sqrt(query_heads.shape[-1])
    d_keys = (
        jnp.einsum("nhqk,nqhd->nkhd", d_scores, query_heads, preferred_element_type=jnp.float32)
        * factor
    )
    d_values = jnp.einsum(
        "nhqk,nqhd->nkhd",
        softmax_weights.astype(jnp.bfloat16),
        d_heads,
        preferred_element_type=jnp.float32,
    )
    return (
        d_keys.reshape(keys.shape[0], keys.shape[1], -1),
        d_values.reshape(values.shape[0], values.shape[1], -1),
    )


def contract_rows(left, right):
    return lax.dot_general(
        left, right, (((0,), (0,)), ((), ())), preferred_element_type=jnp.float32
    )


def contract_cols(left, right):
    return lax.dot_general(
        left, right, (((1,), (1,)), ((), ())), preferred_element_type=jnp.float32
    )


def per_device(
    base_codes,
    stem_weight,
    conv_weight,
    down_weight,
    norm_gain,
    query_weight,
    key_weight,
    value_weight,
    output_weight,
    up_weight,
    cotangent,
):
    number, row_count = base_codes.shape
    coarse = row_count // 2
    local_heads = HEADS // lax.axis_size("batch")
    reach = (stem_weight.shape[0] - 1) // 2
    padded_bases = with_halo(base_codes + 1, (("seq", 1),), reach)
    embedded, stem_back = jax.vjp(lambda weights: stem_embed(weights, padded_bases), stem_weight)
    padded = with_halo(embedded, (("seq", 1),), DILATION)
    towered, conv_back = jax.vjp(conv_block, conv_weight, padded)
    (lifted, normed), down_back = jax.vjp(down_block, down_weight, norm_gain, towered)
    all_normed = lax.all_gather(normed, "batch", axis=0, tiled=True)
    joined_weight = jnp.concatenate([query_weight, key_weight, value_weight], axis=1)
    projected = jnp.dot(all_normed, joined_weight, preferred_element_type=jnp.float32).astype(
        jnp.bfloat16
    )
    group_count = projected.shape[0] // coarse
    query_cols = query_weight.shape[1]
    queries = projected[:, :query_cols].reshape(group_count, coarse, query_cols)
    keys = projected[:, query_cols : 2 * query_cols].reshape(group_count, coarse, query_cols)
    values = projected[:, 2 * query_cols :].reshape(group_count, coarse, -1)
    all_keys, all_values = (
        lax.all_gather(keys, "seq", axis=1, tiled=True),
        lax.all_gather(values, "seq", axis=1, tiled=True),
    )
    attended, log_total = attend_rows(queries, all_keys, all_values, local_heads)
    flat_attended = attended.reshape(-1, attended.shape[-1])
    block = flat_attended
    mixed = lax.psum_scatter(
        jnp.dot(block, output_weight, preferred_element_type=jnp.float32).astype(jnp.bfloat16),
        "batch",
        scatter_dimension=0,
        tiled=True,
    ).astype(jnp.float32)
    features, tail_back = jax.vjp(tail_block, up_weight, lifted, mixed, towered)
    d_up, d_lifted, d_mixed, d_tail = tail_back(cotangent)
    all_d_mixed = lax.all_gather(d_mixed.astype(jnp.bfloat16), "batch", axis=0, tiled=True)
    d_attended = (
        contract_cols(all_d_mixed, output_weight).astype(jnp.bfloat16).reshape(attended.shape)
    )
    out_term = contract_rows(all_d_mixed, flat_attended)
    d_queries, inner_term = query_grads(
        queries, all_keys, all_values, log_total, d_attended, local_heads
    )
    full_queries, full_d_attended = (
        lax.all_gather(queries, "seq", axis=1, tiled=True),
        lax.all_gather(d_attended, "seq", axis=1, tiled=True),
    )
    full_log_total, full_inner = (
        lax.all_gather(log_total, "seq", axis=1, tiled=True),
        lax.all_gather(inner_term, "seq", axis=1, tiled=True),
    )
    d_keys, d_values = key_grads(
        full_queries, full_d_attended, full_log_total, full_inner, keys, values, local_heads
    )
    d_projected = jnp.concatenate(
        [
            d_queries.astype(jnp.bfloat16).reshape(-1, query_cols),
            d_keys.astype(jnp.bfloat16).reshape(-1, query_cols),
            d_values.astype(jnp.bfloat16).reshape(-1, values.shape[-1]),
        ],
        axis=1,
    )
    weight_term = contract_rows(all_normed, d_projected)
    grad_query, grad_key, grad_value, grad_out = (
        lax.psum_scatter(
            weight_term[:, :query_cols].astype(jnp.bfloat16), "seq", scatter_dimension=0, tiled=True
        ).astype(jnp.float32),
        lax.psum_scatter(
            weight_term[:, query_cols : 2 * query_cols].astype(jnp.bfloat16),
            "seq",
            scatter_dimension=0,
            tiled=True,
        ).astype(jnp.float32),
        lax.psum_scatter(
            weight_term[:, 2 * query_cols :].astype(jnp.bfloat16),
            "seq",
            scatter_dimension=0,
            tiled=True,
        ).astype(jnp.float32),
        lax.psum_scatter(
            out_term.astype(jnp.bfloat16), "seq", scatter_dimension=0, tiled=True
        ).astype(jnp.float32),
    )
    block = d_projected
    d_normed = lax.psum_scatter(
        contract_cols(block, joined_weight).astype(jnp.bfloat16),
        "batch",
        scatter_dimension=0,
        tiled=True,
    )
    d_down, d_gain, d_pooled_path = down_back((d_lifted, d_normed))
    d_towered = (d_tail.astype(jnp.float32) + d_pooled_path.astype(jnp.float32)).astype(
        jnp.bfloat16
    )
    d_conv, d_padded = conv_back(d_towered)
    rim_pair = jnp.concatenate(
        [d_padded[:, :DILATION], d_padded[:, DILATION + row_count :]], axis=1
    )
    nearby = with_halo(rim_pair, (("seq", 1),), DILATION)
    center = d_padded[:, DILATION : DILATION + row_count].astype(jnp.float32)
    center = center.at[:, :DILATION].add(nearby[:, :DILATION].astype(jnp.float32))
    center = center.at[:, row_count - DILATION :].add(nearby[:, 3 * DILATION :].astype(jnp.float32))
    (d_stem,) = stem_back(center.astype(jnp.bfloat16))
    channel_count = conv_weight.shape[2]
    stem_flat = d_stem.astype(jnp.float32).reshape(-1, channel_count)
    conv_flat = d_conv.astype(jnp.float32).reshape(-1, channel_count)
    down_flat = d_down.astype(jnp.float32)
    up_flat = d_up.astype(jnp.float32)
    gain_flat = d_gain.reshape(1, -1)
    reduced = (
        lax.psum_scatter(stem_flat, ("seq", "batch"), scatter_dimension=1, tiled=True),
        lax.psum_scatter(conv_flat, ("seq", "batch"), scatter_dimension=1, tiled=True),
        lax.psum_scatter(down_flat, ("seq", "batch"), scatter_dimension=1, tiled=True),
        lax.psum_scatter(up_flat, ("seq", "batch"), scatter_dimension=1, tiled=True),
        lax.psum_scatter(gain_flat, ("seq", "batch"), scatter_dimension=1, tiled=True),
    )
    grad_stem = reduced[0].reshape(stem_weight.shape[0], 4, -1)
    grad_conv = reduced[1].reshape(3, conv_weight.shape[1], -1)
    grad_gain = reduced[4].reshape(-1)
    return (
        features,
        grad_stem,
        grad_conv,
        reduced[2],
        grad_gain,
        reduced[3],
        grad_query,
        grad_key,
        grad_value,
        grad_out,
    )


def solution(mesh):
    placed = (
        P("batch", "seq"),
        P(),
        P(),
        P(),
        P(),
        P(None, "batch"),
        P(None, "batch"),
        P(None, "batch"),
        P("batch", None),
        P(),
        P("batch", "seq", None),
    )
    return jax.shard_map(
        per_device,
        mesh=mesh,
        in_specs=placed,
        out_specs=(
            P("batch", "seq", None),
            P(None, None, ("seq", "batch")),
            P(None, None, ("seq", "batch")),
            P(None, ("seq", "batch")),
            P(("seq", "batch")),
            P(None, ("seq", "batch")),
            P("seq", "batch"),
            P("seq", "batch"),
            P("seq", "batch"),
            P("seq", "batch"),
        ),
        check_vma=False,
    )
```

profile of v0, /device:TPU:1, one launch (start us, length us, event | category | flops | bytes accessed | tf_op | source)
XLA Modules:
  0.0 1337.9 jit_solution(11303091295988706414)
XLA Ops:
  8.1 6.9 collective-permute-start
  17.0 4.3 collective-permute-done.1
  26.4 5.1 collective-permute-start.2
  49.0 26.6 %all-gather.11.cloned.1.call-done = bf16[512,1536]{1,0:T(8,128)(2,1)} async-done(((bf16[64,1536]{1,0:T(8,128)(2,1)}), bf16[512,1536]{1,0:T(8,128)(2,1)}) %all-gather.11.cloned.1.call-update) | async-done | bytes 1572880 | tf_op jit(solution)/shard_map/all_gather | solution.py:198
  82.3 34.7 %all-gather.17.cloned.1.call-done = bf16[512,1536]{1,0:T(8,128)(2,1)} async-done(((bf16[64,1536]{1,0:T(8,128)(2,1)}), bf16[512,1536]{1,0:T(8,128)(2,1)}) %all-gather.17.cloned.1.call-update) | async-done | bytes 1572880 | tf_op jit(solution)/shard_map/all_gather | solution.py:223
  122.7 51.1 %all-gather.15.cloned.1.call-done = bf16[8,1024,128]{2,1,0:T(8,128)(2,1)} async-done(((bf16[8,64,128]{2,1,0:T(8,128)(2,1)}), bf16[8,1024,128]{2,1,0:T(8,128)(2,1)}) %all-gather.15.cloned.1.call-update) | async-done | bytes 2097168 | tf_op jit(solution)/shard_map/all_gather | solution.py:209
  173.8 3.8 exponential_reduce_fusion
  178.2 21.5 %all-gather.2 = f32[16,64,8]{1,2,0:T(8,128)S(1)} all-gather(f32[1,64,8]{1,2,0:T(8,128)S(1)} %get-tuple-element.84), channel_id=2, replica_groups=mesh['seq'=16,'batch'=8] {'seq'}, dimensions={0}, use_global_device_ids=true | all-gather | bytes 34816 | tf_op jit(solution)/shard_map/all_gather | solution.py:236
  200.4 22.8 %all-gather.19.cloned.1.call-done = bf16[8,1024,128]{2,1,0:T(8,128)(2,1)} async-done(((bf16[8,64,128]{2,1,0:T(8,128)(2,1)}), bf16[8,1024,128]{2,1,0:T(8,128)(2,1)}) %all-gather.19.cloned.1.call-update) | async-done | bytes 2097168 | tf_op jit(solution)/shard_map/all_gather | solution.py:232
  223.3 3.8 fusion.124
  227.1 53.3 %all-gather.21.cloned.1.call-done = bf16[8,1024,192]{2,1,0:T(8,128)(2,1)} async-done(((bf16[8,64,192]{2,1,0:T(8,128)(2,1)}), bf16[8,1024,192]{2,1,0:T(8,128)(2,1)}) %all-gather.21.cloned.1.call-update) | async-done | bytes 3145744 | tf_op jit(solution)/shard_map/all_gather | solution.py:233
  280.4 4.4 convolution_convert_fusion.12
  284.8 52.7 %all-gather.13.cloned.1.call-done = bf16[8,1024,192]{2,1,0:T(8,128)(2,1)} async-done(((bf16[8,64,192]{2,1,0:T(8,128)(2,1)}), bf16[8,1024,192]{2,1,0:T(8,128)(2,1)}) %all-gather.13.cloned.1.call-update) | async-done | bytes 3145744 | tf_op jit(solution)/shard_map/all_gather | solution.py:210
  337.5 5.7 multiply_reduce_fusion
  343.2 21.4 %all-gather.3 = f32[16,64,8]{1,2,0:T(8,128)S(1)} all-gather(f32[1,64,8]{1,2,0:T(8,128)S(1)} %bitcast.212), channel_id=3, replica_groups=mesh['seq'=16,'batch'=8] {'seq'}, dimensions={0}, use_global_device_ids=true | all-gather | bytes 34816 | tf_op jit(solution)/shard_map/all_gather | solution.py:237
  364.7 5.9 fusion.36
  370.6 3.7 fusion.37
  376.9 3.8 convolution_convert_fusion.13
  399.1 10.3 reduce-scatter.22.cloned.1.call-done
  427.3 8.1 copy.65
  435.4 16.1 %reduce-scatter.20.cloned.1.call-done = bf16[64,1536]{1,0:T(8,128)(2,1)} async-done(((bf16[512,1536]{1,0:T(8,128)(2,1)}), bf16[64,1536]{1,0:T(8,128)(2,1)}) %reduce-scatter.20.cloned.1.call-update) | async-done | bytes 196624 | tf_op jit(solution)/shard_map/reduce_scatter | solution.py:215
  451.5 4.0 fusion.3
  455.5 373.6 %fusion.118 = (f32[2304,8]{0,1:T(8,128)}, f32[768,16]{0,1:T(8,128)S(1)}, f32[1536,8]{0,1:T(8,128)}) fusion(f32[2304,768]{0,1:T(8,128)} %copy.65, f32[768,1536]{0,1:T(8,128)} %fusion.4, f32[1536,768]{0,1:T(8,128)} %fusion.3), kind=kCustom, calls=%all-reduce-scatter.3 | all-reduce-scatter fusion | flops 5505026 | bytes 16687104
  837.0 17.3 %collective-permute-start.5 = (bf16[1,8,768]{2,1,0:T(8,128)(2,1)S(1)}, bf16[1,8,768]{2,1,0:T(8,128)(2,1)S(1)}, u32[]{:S(2)}, u32[]{:S(2)}) collective-permute-start(bf16[1,8,768]{2,1,0:T(8,128)(2,1)S(1)} %get-tuple-element.76), channel_id=1, source_target_pairs={{8,0},{16,8},{24,16},{32,24},{40,32},{48,40},{56,48},{64,56},{72,6... | collective-permute-start | bytes 36872 | tf_op jit(solution)/shard_map/ppermute | solution.py:23
  858.2 7.2 collective-permute-start.65
  869.1 6.5 collective-permute-start.64
  880.5 4.3 collective-permute-start.60
  884.8 3.9 collective-permute-start.59
  892.7 4.0 collective-permute-start.56
  902.3 4.6 collective-permute-start.52
  906.9 3.7 collective-permute-start.51
  922.4 11.5 collective-permute-start.45
  933.9 4.0 collective-permute-start.44
  944.7 5.0 collective-permute-start.40
  960.0 3.9 collective-permute-start.96
  969.5 5.7 collective-permute-start.92
  995.5 4.0 collective-permute-start.84
  1032.2 4.5 collective-permute-start.72
  1043.3 64.4 %all-reduce.12 = f32[1,1536]{1,0:T(1,128)S(1)} all-reduce(f32[1,1536]{1,0:T(1,128)S(1)} %reshape.428), channel_id=9, replica_groups=mesh['seq'=16,'batch'=8] {'seq','batch'}, use_global_device_ids=true, to_apply=%region_11.0.clone | all-reduce | flops 1536 | bytes 12288
  1111.2 4.4 collective-permute-start.34
  1117.8 4.7 collective-permute-start.32
  1139.6 3.7 collective-permute-start.24
  1149.7 3.7 collective-permute-start.20
  1165.7 26.3 %concatenate.44 = f32[1536,262]{0,1:T(8,128)S(1)} concatenate(f32[1536,6]{0,1:T(8,128)} %collective-permute-done.101, f32[1536,8]{0,1:T(8,128)S(1)} %copy-done.77, f32[1536,8]{0,1:T(8,128)S(1)} %copy-done.79, f32[1536,8]{0,1:T(8,128)S(1)} %copy-done.81, f32[1536,8]{0,1:T(8,128)S(1)} %copy-done.83, f32[1536,8]{0,1:T(8,128)S(1)} %copy-done.85, f32[1536,8]{0,1:T(8,128)} %copy-done.86, ...), dimensions={1} | concatenate | bytes 3219456
  1199.2 4.9 collective-permute-start.12
  1206.8 48.6 %concatenate.43 = f32[768,524]{0,1:T(8,128)} concatenate(f32[768,12]{0,1:T(8,128)} %copy-done.44, f32[768,16]{0,1:T(8,128)} %copy-done.45, f32[768,16]{0,1:T(8,128)} %copy-done.46, f32[768,16]{0,1:T(8,128)} %copy-done.47, f32[768,16]{0,1:T(8,128)} %copy-done.48, f32[768,16]{0,1:T(8,128)} %copy-done.49, f32[768,16]{0,1:T(8,128)} %copy-done.50, f32[768,16]{0,1:T(8,128)} %copy-done.51, ...), dimensions={1} | concatenate | bytes 3219456
  1260.1 4.7 collective-permute-start.8
  1275.3 52.8 %concatenate.42 = f32[2304,262]{0,1:T(8,128)} concatenate(f32[2304,6]{0,1:T(8,128)S(1)} %collective-permute-done.37, f32[2304,8]{0,1:T(8,128)S(1)} %collective-permute-done.36, f32[2304,8]{0,1:T(8,128)S(1)} %collective-permute-done.35, f32[2304,8]{0,1:T(8,128)S(1)} %collective-permute-done.34, f32[2304,8]{0,1:T(8,128)S(1)} %collective-permute-done.33, ...), dimensions={1} | concatenate | bytes 4829184
  (530 shorter events, 268.8 us)
Async XLA Ops:
  7.2 68.4 %all-gather.11.cloned.1.call-start = ((), (), s32[]{:S(2)}) async-start(), calls=%async_computation.6 | async-start | bytes 1769472 | tf_op jit(solution)/shard_map/all_gather | solution.py:198
  39.3 77.7 %all-gather.17.cloned.1.call-start = ((), (), s32[]{:S(2)}) async-start(), calls=%async_computation.10 | async-start | bytes 1769472 | tf_op jit(solution)/shard_map/all_gather | solution.py:223
  45.1 128.7 %all-gather.15.cloned.1.call-start = ((), (), s32[]{:S(2)}) async-start(), calls=%async_computation.8 | async-start | bytes 2228224 | tf_op jit(solution)/shard_map/all_gather | solution.py:209
  80.5 142.8 %all-gather.19.cloned.1.call-start = ((), (), s32[]{:S(2)}) async-start(), calls=%async_computation.11 | async-start | bytes 2228224 | tf_op jit(solution)/shard_map/all_gather | solution.py:232
  82.3 198.1 %all-gather.21.cloned.1.call-start = ((), (), s32[]{:S(2)}) async-start(), calls=%async_computation.12 | async-start | bytes 4456448 | tf_op jit(solution)/shard_map/all_gather | solution.py:233
  121.7 215.8 %all-gather.13.cloned.1.call-start = ((), (), s32[]{:S(2)}) async-start(), calls=%async_computation.7 | async-start | bytes 4456448 | tf_op jit(solution)/shard_map/all_gather | solution.py:210
  122.6 286.7 %reduce-scatter.22.cloned.1.call-start = ((), (), s32[]{:S(2)}) async-start(), calls=%async_computation.13 | async-start | bytes 1769472 | tf_op jit(solution)/shard_map/reduce_scatter | solution.py:272
  376.6 74.9 %reduce-scatter.20.cloned.1.call-start = ((), (), s32[]{:S(2)}) async-start(), calls=%async_computation.9 | async-start | bytes 1769472 | tf_op jit(solution)/shard_map/reduce_scatter | solution.py:215
  383.2 600.0 %reduce-scatter.26.cloned.1.call-start = ((), (), s32[]{:S(2)}) async-start(), calls=%async_computation.15 | async-start | bytes 417792
  389.7 595.0 %reduce-scatter.28.cloned.1.call-start = ((), (), s32[]{:S(2)}) async-start(), calls=%async_computation.16 | async-start | bytes 417792
  391.7 594.6 %reduce-scatter.30.cloned.1.call-start = ((), (), s32[]{:S(2)}) async-start(), calls=%async_computation.17 | async-start | bytes 835584
  395.9 592.0 %reduce-scatter.24.cloned.1.call-start = ((), (), s32[]{:S(2)}) async-start(), calls=%async_computation.14 | async-start | bytes 835584 | tf_op jit(solution)/shard_map/reduce_scatter | solution.py:267
  399.0 930.6 %all-reduce.20.cloned.1.call-start = ((), (), s32[]{:S(2)}) async-start(), calls=%async_computation.18 | async-start | bytes 786432
  829.1 37.2 %collective-permute-start.69 = (f32[768,12]{0,1:T(8,128)S(1)}, f32[768,12]{0,1:T(8,128)S(1)}, u32[]{:S(2)}, u32[]{:S(2)}) collective-permute-start(f32[768,12]{0,1:T(8,128)S(1)} %slice.243), channel_id=1, source_target_pairs={{0,32},{1,33},{2,34},{3,35},{4,36},{5,37},{6,38},{7,39},{8,40},{9,... | collective-permute-start | bytes 110600
  835.0 21.8 %collective-permute-start.4 = (bf16[1,8,768]{2,1,0:T(8,128)(2,1)S(1)}, bf16[1,8,768]{2,1,0:T(8,128)(2,1)S(1)}, u32[]{:S(2)}, u32[]{:S(2)}) collective-permute-start(bf16[1,8,768]{2,1,0:T(8,128)(2,1)S(1)} %get-tuple-element.77), channel_id=1, source_target_pairs={{0,8},{8,16},{16,24},{24,32},{32,40},{40,48},{48,56},{56,64},{64,7... | collective-permute-start | bytes 36872 | tf_op jit(solution)/shard_map/ppermute | solution.py:20
  837.0 21.2 %collective-permute-start.5 = (bf16[1,8,768]{2,1,0:T(8,128)(2,1)S(1)}, bf16[1,8,768]{2,1,0:T(8,128)(2,1)S(1)}, u32[]{:S(2)}, u32[]{:S(2)}) collective-permute-start(bf16[1,8,768]{2,1,0:T(8,128)(2,1)S(1)} %get-tuple-element.76), channel_id=1, source_target_pairs={{8,0},{16,8},{24,16},{32,24},{40,32},{48,40},{56,48},{64,56},{72,6... | collective-permute-start | bytes 36872 | tf_op jit(solution)/shard_map/ppermute | solution.py:23
  854.3 21.3 %collective-permute-start.68 = (f32[768,16]{0,1:T(8,128)S(1)}, f32[768,16]{0,1:T(8,128)S(1)}, u32[]{:S(2)}, u32[]{:S(2)}) collective-permute-start(f32[768,16]{0,1:T(8,128)S(1)} %copy-done.24), channel_id=1, source_target_pairs={{0,31},{1,32},{2,33},{3,34},{4,35},{5,36},{6,37},{7,38},{8,39},{9,... | collective-permute-start | bytes 147464
  855.6 22.3 %collective-permute-start.67 = (f32[768,16]{0,1:T(8,128)S(1)}, f32[768,16]{0,1:T(8,128)S(1)}, u32[]{:S(2)}, u32[]{:S(2)}) collective-permute-start(f32[768,16]{0,1:T(8,128)S(1)} %copy-done.24), channel_id=1, source_target_pairs={{0,30},{1,31},{2,32},{3,33},{4,34},{5,35},{6,36},{7,37},{8,38},{9,... | collective-permute-start | bytes 147464
  856.9 22.3 %collective-permute-start.66 = (f32[768,16]{0,1:T(8,128)S(1)}, f32[768,16]{0,1:T(8,128)S(1)}, u32[]{:S(2)}, u32[]{:S(2)}) collective-permute-start(f32[768,16]{0,1:T(8,128)S(1)} %copy-done.24), channel_id=1, source_target_pairs={{0,29},{1,30},{2,31},{3,32},{4,33},{5,34},{6,35},{7,36},{8,37},{9,... | collective-permute-start | bytes 147464
  858.2 22.3 %collective-permute-start.65 = (f32[768,16]{0,1:T(8,128)S(1)}, f32[768,16]{0,1:T(8,128)S(1)}, u32[]{:S(2)}, u32[]{:S(2)}) collective-permute-start(f32[768,16]{0,1:T(8,128)S(1)} %copy-done.24), channel_id=1, source_target_pairs={{0,28},{1,29},{2,30},{3,31},{4,32},{5,33},{6,34},{7,35},{8,36},{9,... | collective-permute-start | bytes 147464
  880.5 16.2 %collective-permute-start.60 = (f32[768,16]{0,1:T(8,128)S(1)}, f32[768,16]{0,1:T(8,128)S(1)}, u32[]{:S(2)}, u32[]{:S(2)}) collective-permute-start(f32[768,16]{0,1:T(8,128)S(1)} %copy-done.24), channel_id=1, source_target_pairs={{0,23},{1,24},{2,25},{3,26},{4,27},{5,28},{6,29},{7,30},{8,31},{9,... | collective-permute-start | bytes 147464
  912.7 21.2 %collective-permute-start.49 = (f32[768,16]{0,1:T(8,128)S(1)}, f32[768,16]{0,1:T(8,128)S(1)}, u32[]{:S(2)}, u32[]{:S(2)}) collective-permute-start(f32[768,16]{0,1:T(8,128)S(1)} %copy-done.24), channel_id=1, source_target_pairs={{0,12},{1,13},{2,14},{3,15},{4,16},{5,17},{6,18},{7,19},{8,20},{9,... | collective-permute-start | bytes 147464
  915.2 22.7 %collective-permute-start.48 = (f32[768,16]{0,1:T(8,128)S(1)}, f32[768,16]{0,1:T(8,128)S(1)}, u32[]{:S(2)}, u32[]{:S(2)}) collective-permute-start(f32[768,16]{0,1:T(8,128)S(1)} %copy-done.24), channel_id=1, source_target_pairs={{0,11},{1,12},{2,13},{3,14},{4,15},{5,16},{6,17},{7,18},{8,19},{9,... | collective-permute-start | bytes 147464
  918.2 22.6 %collective-permute-start.47 = (f32[768,16]{0,1:T(8,128)S(1)}, f32[768,16]{0,1:T(8,128)S(1)}, u32[]{:S(2)}, u32[]{:S(2)}) collective-permute-start(f32[768,16]{0,1:T(8,128)S(1)} %copy-done.24), channel_id=1, source_target_pairs={{0,10},{1,11},{2,12},{3,13},{4,14},{5,15},{6,16},{7,17},{8,18},{9,... | collective-permute-start | bytes 147464
  920.3 22.4 %collective-permute-start.46 = (f32[768,16]{0,1:T(8,128)S(1)}, f32[768,16]{0,1:T(8,128)S(1)}, u32[]{:S(2)}, u32[]{:S(2)}) collective-permute-start(f32[768,16]{0,1:T(8,128)S(1)} %copy-done.24), channel_id=1, source_target_pairs={{0,9},{1,10},{2,11},{3,12},{4,13},{5,14},{6,15},{7,16},{8,17},{9,1... | collective-permute-start | bytes 147464
  922.4 22.3 %collective-permute-start.45 = (f32[768,16]{0,1:T(8,128)S(1)}, f32[768,16]{0,1:T(8,128)S(1)}, u32[]{:S(2)}, u32[]{:S(2)}) collective-permute-start(f32[768,16]{0,1:T(8,128)S(1)} %copy-done.24), channel_id=1, source_target_pairs={{0,8},{1,9},{2,10},{3,11},{4,12},{5,13},{6,14},{7,15},{8,16},{9,17... | collective-permute-start | bytes 147464
  969.5 19.9 %collective-permute-start.92 = (f32[1536,8]{0,1:T(8,128)}, f32[1536,8]{0,1:T(8,128)}, u32[]{:S(2)}, u32[]{:S(2)}) collective-permute-start(f32[1536,8]{0,1:T(8,128)} %get-tuple-element.71), channel_id=1, source_target_pairs={{0,23},{1,24},{2,25},{3,26},{4,27},{5,28},{6,29},{7,30},{8,31},{9,... | collective-permute-start | bytes 147464
  975.2 16.4 %collective-permute-start.91 = (f32[1536,8]{0,1:T(8,128)}, f32[1536,8]{0,1:T(8,128)}, u32[]{:S(2)}, u32[]{:S(2)}) collective-permute-start(f32[1536,8]{0,1:T(8,128)} %get-tuple-element.71), channel_id=1, source_target_pairs={{0,22},{1,23},{2,24},{3,25},{4,26},{5,27},{6,28},{7,29},{8,30},{9,... | collective-permute-start | bytes 147464
  977.1 16.4 %collective-permute-start.90 = (f32[1536,8]{0,1:T(8,128)}, f32[1536,8]{0,1:T(8,128)}, u32[]{:S(2)}, u32[]{:S(2)}) collective-permute-start(f32[1536,8]{0,1:T(8,128)} %get-tuple-element.71), channel_id=1, source_target_pairs={{0,21},{1,22},{2,23},{3,24},{4,25},{5,26},{6,27},{7,28},{8,29},{9,... | collective-permute-start | bytes 147464
  979.0 16.4 %collective-permute-start.89 = (f32[1536,8]{0,1:T(8,128)}, f32[1536,8]{0,1:T(8,128)}, u32[]{:S(2)}, u32[]{:S(2)}) collective-permute-start(f32[1536,8]{0,1:T(8,128)} %get-tuple-element.71), channel_id=1, source_target_pairs={{0,20},{1,21},{2,22},{3,23},{4,24},{5,25},{6,26},{7,27},{8,28},{9,... | collective-permute-start | bytes 147464
  981.0 18.5 %collective-permute-start.88 = (f32[1536,8]{0,1:T(8,128)}, f32[1536,8]{0,1:T(8,128)}, u32[]{:S(2)}, u32[]{:S(2)}) collective-permute-start(f32[1536,8]{0,1:T(8,128)} %get-tuple-element.71), channel_id=1, source_target_pairs={{0,19},{1,20},{2,21},{3,22},{4,23},{5,24},{6,25},{7,26},{8,27},{9,... | collective-permute-start | bytes 147464
  1030.9 91.7 %collective-permute-start.36 = (f32[2304,8]{0,1:T(8,128)}, f32[2304,8]{0,1:T(8,128)S(1)}, u32[]{:S(2)}, u32[]{:S(2)}) collective-permute-start(f32[2304,8]{0,1:T(8,128)} %get-tuple-element.69), channel_id=1, source_target_pairs={{0,31},{1,32},{2,33},{3,34},{4,35},{5,36},{6,37},{7,38},{8,39},{9,... | collective-permute-start | bytes 221192
  1032.2 75.5 %collective-permute-start.72 = (f32[1536,8]{0,1:T(8,128)}, f32[1536,8]{0,1:T(8,128)S(1)}, u32[]{:S(2)}, u32[]{:S(2)}) collective-permute-start(f32[1536,8]{0,1:T(8,128)} %get-tuple-element.71), channel_id=1, source_target_pairs={{0,3},{1,4},{2,5},{3,6},{4,7},{5,8},{6,9},{7,10},{8,11},{9,12},{10... | collective-permute-start | bytes 147464
  1036.7 74.5 %collective-permute-start.71 = (f32[1536,8]{0,1:T(8,128)}, f32[1536,8]{0,1:T(8,128)S(1)}, u32[]{:S(2)}, u32[]{:S(2)}) collective-permute-start(f32[1536,8]{0,1:T(8,128)} %get-tuple-element.71), channel_id=1, source_target_pairs={{0,2},{1,3},{2,4},{3,5},{4,6},{5,7},{6,8},{7,9},{8,10},{9,11},{10,... | collective-permute-start | bytes 147464
  1039.9 75.7 %collective-permute-start.70 = (f32[1536,8]{0,1:T(8,128)}, f32[1536,8]{0,1:T(8,128)S(1)}, u32[]{:S(2)}, u32[]{:S(2)}) collective-permute-start(f32[1536,8]{0,1:T(8,128)} %get-tuple-element.71), channel_id=1, source_target_pairs={{0,1},{1,2},{2,3},{3,4},{4,5},{5,6},{6,7},{7,8},{8,9},{9,10},{10,1... | collective-permute-start | bytes 147464
  1041.9 75.9 %collective-permute-start.37 = (f32[2304,6]{0,1:T(8,128)S(1)}, f32[2304,6]{0,1:T(8,128)S(1)}, u32[]{:S(2)}, u32[]{:S(2)}) collective-permute-start(f32[2304,6]{0,1:T(8,128)S(1)} %slice.242), channel_id=1, source_target_pairs={{0,32},{1,33},{2,34},{3,35},{4,36},{5,37},{6,38},{7,39},{8,40},{9,... | collective-permute-start | bytes 165896
  1107.6 17.9 %collective-permute-start.35 = (f32[2304,8]{0,1:T(8,128)}, f32[2304,8]{0,1:T(8,128)S(1)}, u32[]{:S(2)}, u32[]{:S(2)}) collective-permute-start(f32[2304,8]{0,1:T(8,128)} %get-tuple-element.69), channel_id=1, source_target_pairs={{0,30},{1,31},{2,32},{3,33},{4,34},{5,35},{6,36},{7,37},{8,38},{9,... | collective-permute-start | bytes 221192
  1111.2 16.8 %collective-permute-start.34 = (f32[2304,8]{0,1:T(8,128)}, f32[2304,8]{0,1:T(8,128)S(1)}, u32[]{:S(2)}, u32[]{:S(2)}) collective-permute-start(f32[2304,8]{0,1:T(8,128)} %get-tuple-element.69), channel_id=1, source_target_pairs={{0,29},{1,30},{2,31},{3,32},{4,33},{5,34},{6,35},{7,36},{8,37},{9,... | collective-permute-start | bytes 221192
  1149.7 42.3 %collective-permute-start.20 = (f32[2304,8]{0,1:T(8,128)}, f32[2304,8]{0,1:T(8,128)S(1)}, u32[]{:S(2)}, u32[]{:S(2)}) collective-permute-start(f32[2304,8]{0,1:T(8,128)} %get-tuple-element.69), channel_id=1, source_target_pairs={{0,15},{1,16},{2,17},{3,18},{4,19},{5,20},{6,21},{7,22},{8,23},{9,... | collective-permute-start | bytes 221192
  1153.5 42.1 %collective-permute-start.19 = (f32[2304,8]{0,1:T(8,128)}, f32[2304,8]{0,1:T(8,128)S(1)}, u32[]{:S(2)}, u32[]{:S(2)}) collective-permute-start(f32[2304,8]{0,1:T(8,128)} %get-tuple-element.69), channel_id=1, source_target_pairs={{0,14},{1,15},{2,16},{3,17},{4,18},{5,19},{6,20},{7,21},{8,22},{9,... | collective-permute-start | bytes 221192
  1156.8 40.2 %collective-permute-start.18 = (f32[2304,8]{0,1:T(8,128)}, f32[2304,8]{0,1:T(8,128)S(1)}, u32[]{:S(2)}, u32[]{:S(2)}) collective-permute-start(f32[2304,8]{0,1:T(8,128)} %get-tuple-element.69), channel_id=1, source_target_pairs={{0,13},{1,14},{2,15},{3,16},{4,17},{5,18},{6,19},{7,20},{8,21},{9,... | collective-permute-start | bytes 221192
  1159.1 40.1 %collective-permute-start.17 = (f32[2304,8]{0,1:T(8,128)}, f32[2304,8]{0,1:T(8,128)S(1)}, u32[]{:S(2)}, u32[]{:S(2)}) collective-permute-start(f32[2304,8]{0,1:T(8,128)} %get-tuple-element.69), channel_id=1, source_target_pairs={{0,12},{1,13},{2,14},{3,15},{4,16},{5,17},{6,18},{7,19},{8,20},{9,... | collective-permute-start | bytes 221192
  1161.0 43.1 %collective-permute-start.16 = (f32[2304,8]{0,1:T(8,128)}, f32[2304,8]{0,1:T(8,128)S(1)}, u32[]{:S(2)}, u32[]{:S(2)}) collective-permute-start(f32[2304,8]{0,1:T(8,128)} %get-tuple-element.69), channel_id=1, source_target_pairs={{0,11},{1,12},{2,13},{3,14},{4,15},{5,16},{6,17},{7,18},{8,19},{9,... | collective-permute-start | bytes 221192
  1192.1 63.3 %collective-permute-start.15 = (f32[2304,8]{0,1:T(8,128)}, f32[2304,8]{0,1:T(8,128)S(1)}, u32[]{:S(2)}, u32[]{:S(2)}) collective-permute-start(f32[2304,8]{0,1:T(8,128)} %get-tuple-element.69), channel_id=1, source_target_pairs={{0,10},{1,11},{2,12},{3,13},{4,14},{5,15},{6,16},{7,17},{8,18},{9,... | collective-permute-start | bytes 221192
  1195.6 61.8 %collective-permute-start.14 = (f32[2304,8]{0,1:T(8,128)}, f32[2304,8]{0,1:T(8,128)S(1)}, u32[]{:S(2)}, u32[]{:S(2)}) collective-permute-start(f32[2304,8]{0,1:T(8,128)} %get-tuple-element.69), channel_id=1, source_target_pairs={{0,9},{1,10},{2,11},{3,12},{4,13},{5,14},{6,15},{7,16},{8,17},{9,1... | collective-permute-start | bytes 221192
  1197.0 63.1 %collective-permute-start.13 = (f32[2304,8]{0,1:T(8,128)}, f32[2304,8]{0,1:T(8,128)S(1)}, u32[]{:S(2)}, u32[]{:S(2)}) collective-permute-start(f32[2304,8]{0,1:T(8,128)} %get-tuple-element.69), channel_id=1, source_target_pairs={{0,8},{1,9},{2,10},{3,11},{4,12},{5,13},{6,14},{7,15},{8,16},{9,17... | collective-permute-start | bytes 221192
  1199.2 65.6 %collective-permute-start.12 = (f32[2304,8]{0,1:T(8,128)}, f32[2304,8]{0,1:T(8,128)S(1)}, u32[]{:S(2)}, u32[]{:S(2)}) collective-permute-start(f32[2304,8]{0,1:T(8,128)} %get-tuple-element.69), channel_id=1, source_target_pairs={{0,7},{1,8},{2,9},{3,10},{4,11},{5,12},{6,13},{7,14},{8,15},{9,16}... | collective-permute-start | bytes 221192
  1204.1 62.8 %collective-permute-start.11 = (f32[2304,8]{0,1:T(8,128)}, f32[2304,8]{0,1:T(8,128)}, u32[]{:S(2)}, u32[]{:S(2)}) collective-permute-start(f32[2304,8]{0,1:T(8,128)} %get-tuple-element.69), channel_id=1, source_target_pairs={{0,6},{1,7},{2,8},{3,9},{4,10},{5,11},{6,12},{7,13},{8,14},{9,15},... | collective-permute-start | bytes 221192
  (181 other events, 5494.7 us)
Sparse Core Ops, SparseCore 0:
  39.4 36.1 all-gather.10
  77.3 39.7 all-gather.16
  119.5 54.2 all-gather.14
  176.1 47.1 all-gather.18
  225.6 54.7 all-gather.20
  282.7 54.7 all-gather.12
  376.7 32.6 reduce-scatter.21
  411.8 39.6 reduce-scatter.19
  455.2 71.6 reduce-scatter.25
  530.5 69.2 reduce-scatter.27
  603.6 76.6 reduce-scatter.29
  683.9 73.7 reduce-scatter.23
  1165.8 139.6 all-reduce.19
where the time goes:
time: 1350 us; the launch traced here: 1340 us
  blocking collectives  481 us (36%)
  starting transfers between devices  295 us (22%)
  waiting for transfers between devices  278 us (21%)
  local copies, waits for them, and re-layouts  178 us (13%)
  matrix products  74.5 us (6%)
  between operations  17.1 us (1%)
  other arithmetic  15.1 us (1%)
    unnamed x2, blocking collectives  438 us
    unnamed x100, starting transfers between devices  259 us
    unnamed x251, local copies, waits for them, and re-layouts  158 us
    all_gather x1, waiting for transfers between devices, per_device(): lax.all_gather(d_attended, 'seq', axis=1, tiled=True)  53.3 us
    all_gather x1, waiting for transfers between devices, per_device(): lax.all_gather(values, 'seq', axis=1, tiled=True)  52.7 us
    all_gather x1, waiting for transfers between devices, per_device(): lax.all_gather(keys, 'seq', axis=1, tiled=True)  51.1 us
    all_gather x1, waiting for transfers between devices, per_device(): lax.all_gather(d_mixed.astype(jnp.bfloat16), 'batch', axis=0, tiled=True)  34.7 us
  transfers between devices with their start and end apart: 115, of which 12 were waited for; matrix products, arithmetic and copies ran while one was open for 45% of the time, Pallas kernels for 0%

commit v1 on v0

v1 whole, which is shorter than its diff:
```python
import functools
import math

import jax
import jax.numpy as jnp
from jax import lax
from jax.experimental import pallas as pl
from jax.experimental.pallas import tpu as pltpu
from jax.sharding import PartitionSpec as P

EPSILON = 1e-06
MESH = pl.DeviceIdType.MESH
F32 = jnp.float32
BF16 = jnp.bfloat16
SEQ = 16
BATCH = 8


class OverBatch:
    count = BATCH

    def dst(self, i, s, b):
        j = lax.rem(b + i, BATCH)
        return j, s, j, b

    def src(self, i, s, b):
        j = lax.rem(b + BATCH - i, BATCH)
        return j, s, j

    def same(self, i):
        return i == 0


class OverSeq:
    count = SEQ

    def dst(self, i, s, b):
        j = lax.rem(s + i, SEQ)
        return j, j, b, s

    def src(self, i, s, b):
        j = lax.rem(s + SEQ - i, SEQ)
        return j, j, b

    def same(self, i):
        return i == 0


class Columns:
    count = SEQ

    def dst(self, i, s, b):
        j = lax.rem(s + i, SEQ)
        return j, 2 * b + j // BATCH, lax.rem(j, BATCH), s

    def src(self, i, s, b):
        j = lax.rem(SEQ * BATCH + lax.rem(s, 2) * BATCH + b - i, SEQ)
        return j, j, s // 2

    def same(self, i):
        return None


class Codes:
    count = 2 * BATCH

    def dst(self, i, s, b):
        j = lax.rem(b + i // 2, BATCH)
        return 0, 2 * b + i % 2, j, s

    def src(self, i, s, b):
        return i, i, s // 2

    def same(self, i):
        return None


class ToWorkers:
    count = BATCH

    def dst(self, i, s, b):
        return 0, 2 * b + s // BATCH, lax.rem(s + i, BATCH), lax.rem(s, BATCH)

    def src(self, i, s, b):
        j = lax.rem(b + BATCH - i, BATCH)
        return j, BATCH * lax.rem(s, 2) + j, s // 2

    def same(self, i):
        return None


class ToBlock:
    count = 1

    def dst(self, i, s, b):
        return 0, 2 * b + s // BATCH, lax.rem(s, BATCH), 0

    def src(self, i, s, b):
        return 0, BATCH * lax.rem(s, 2) + b, s // 2

    def same(self, i):
        return None


class ToOwner:
    count = 1

    def dst(self, i, s, b):
        return 0, BATCH * lax.rem(s, 2) + b, s // 2, 0

    def src(self, i, s, b):
        return 0, 2 * b + s // BATCH, lax.rem(s, BATCH)

    def same(self, i):
        return None


def exchange_body(patterns, *refs):
    number = len(patterns)
    sources, results = refs[:number], refs[number : 2 * number]
    sends, receives = refs[2 * number : 3 * number], refs[3 * number :]
    s, b = lax.axis_index("seq"), lax.axis_index("batch")
    barrier = pltpu.get_barrier_semaphore()
    expected = 0
    for pattern in patterns:
        for i in range(pattern.count):
            if pattern.same(i):
                continue
            _, other_s, other_b = pattern.src(i, s, b)
            _, target_s, target_b, _ = pattern.dst(i, s, b)
            if pattern.same(i) is None:
                away = jnp.logical_or(other_s != s, other_b != b)

                @pl.when(away)
                def _():
                    pl.semaphore_signal(
                        barrier, inc=1, device_id=(other_s, other_b), device_id_type=MESH
                    )

                there = jnp.logical_or(target_s != s, target_b != b)
                expected = expected + there.astype(jnp.int32)
            else:
                pl.semaphore_signal(
                    barrier, inc=1, device_id=(other_s, other_b), device_id_type=MESH
                )
                expected = expected + 1
    pl.semaphore_wait(barrier, expected)

    def steps(action):
        for k, pattern in enumerate(patterns):
            for i in range(pattern.count):
                piece, target_s, target_b, slot = pattern.dst(i, s, b)
                near = functools.partial(
                    pltpu.make_async_copy,
                    sources[k].at[piece],
                    results[k].at[slot],
                    sends[k].at[i],
                )
                far = functools.partial(
                    pltpu.make_async_remote_copy,
                    src_ref=sources[k].at[piece],
                    dst_ref=results[k].at[slot],
                    send_sem=sends[k].at[i],
                    recv_sem=receives[k].at[slot],
                    device_id=(target_s, target_b),
                    device_id_type=MESH,
                )
                same = pattern.same(i)
                if same is None:
                    home = jnp.logical_and(target_s == s, target_b == b)
                    pl.when(home)(functools.partial(action, near, None))
                    pl.when(jnp.logical_not(home))(functools.partial(action, None, far))
                elif same:
                    action(near, None)
                else:
                    action(None, far)

    def start(near, far):
        (near if far is None else far)().start()

    def finish(near, far):
        if far is None:
            near().wait()
        else:
            far().wait_send()

    steps(start)
    for k, pattern in enumerate(patterns):
        for i in range(pattern.count):
            slot, other_s, other_b = pattern.src(i, s, b)
            same = pattern.same(i)
            if same:
                continue
            arriving = pltpu.make_async_remote_copy(
                src_ref=sources[k].at[0],
                dst_ref=results[k].at[slot],
                send_sem=sends[k].at[i],
                recv_sem=receives[k].at[slot],
                device_id=(other_s, other_b),
                device_id_type=MESH,
            )
            if same is None:
                away = jnp.logical_or(other_s != s, other_b != b)
                pl.when(away)(arriving.wait_recv)
            else:
                arriving.wait_recv()
    steps(finish)


def exchange(arrays, patterns, slots, collective_id):
    return pl.pallas_call(
        functools.partial(exchange_body, patterns),
        out_shape=[
            jax.ShapeDtypeStruct((slot,) + array.shape[1:], array.dtype)
            for array, slot in zip(arrays, slots)
        ],
        in_specs=[pl.BlockSpec(memory_space=pl.ANY)] * len(arrays),
        out_specs=[pl.BlockSpec(memory_space=pl.ANY)] * len(arrays),
        scratch_shapes=[pltpu.SemaphoreType.DMA((pattern.count,)) for pattern in patterns]
        + [pltpu.SemaphoreType.DMA((slot,)) for slot in slots],
        compiler_params=pltpu.CompilerParams(collective_id=collective_id, has_side_effects=True),
        name="exchange_%d" % collective_id,
    )(*arrays)


def mm(left, right, dims):
    return lax.dot_general(left, right, ((dims[0:1], dims[1:2]), ((), ())), preferred_element_type=F32)


def attention_body(
    q_ref, kv_ref, da_ref, att_ref, dq_ref, dkv_ref,
    other, sent, arrived, own_sum, far_sum, send_sem, recv_sem,
):
    s, b = lax.axis_index("seq"), lax.axis_index("batch")
    peer = (s + 1 - 2 * lax.rem(s, 2), b)
    barrier = pltpu.get_barrier_semaphore()
    pl.semaphore_signal(barrier, inc=1, device_id=peer, device_id_type=MESH)
    pl.semaphore_wait(barrier, 1)
    first = pltpu.make_async_remote_copy(
        src_ref=kv_ref, dst_ref=other, send_sem=send_sem.at[0], recv_sem=recv_sem.at[0],
        device_id=peer, device_id_type=MESH,
    )
    first.start()
    own_sum[...] = jnp.zeros_like(own_sum)
    far_sum[...] = jnp.zeros_like(far_sum)
    first.wait()
    factor = 1.0 / math.sqrt(128)
    rows = 128

    def step(t, carry):
        here = pl.ds(pl.multiple_of(t * rows, rows), rows)
        q, da = q_ref[here, :], da_ref[here, :]
        blocks = ((kv_ref, own_sum), (other, far_sum))
        scores = [mm(q, kv[:, :128], (1, 1)) * factor for kv, _ in blocks]
        total = sum(jnp.sum(jnp.exp(x), axis=1, keepdims=True) for x in scores)
        log_total = jnp.log(total)
        probs = [jnp.exp(x - log_total) for x in scores]
        dprobs = [mm(da, kv[:, 128:], (1, 1)) for kv, _ in blocks]
        inner = sum(jnp.sum(p * d, axis=1, keepdims=True) for p, d in zip(probs, dprobs))
        att = jnp.zeros((rows, 256), F32)
        dq = jnp.zeros((rows, 128), F32)
        for (kv, total_ref), p, d in zip(blocks, probs, dprobs):
            ds = (p * (d - inner)).astype(BF16)
            pb = p.astype(BF16)
            att = att + mm(pb, kv[:, 128:], (1, 0))
            dq = dq + mm(ds, kv[:, :128], (1, 0))
            total_ref[:, :128] += mm(ds, q, (0, 0)) * factor
            total_ref[:, 128:] += mm(pb, da, (0, 0))
        att_ref[here, :] = att.astype(BF16)
        dq_ref[here, :] = (dq * factor).astype(BF16)
        return carry

    lax.fori_loop(0, q_ref.shape[0] // rows, step, 0)
    sent[...] = far_sum[...].astype(BF16)
    second = pltpu.make_async_remote_copy(
        src_ref=sent, dst_ref=arrived, send_sem=send_sem.at[1], recv_sem=recv_sem.at[1],
        device_id=peer, device_id_type=MESH,
    )
    second.start()
    second.wait()
    dkv_ref[...] = (own_sum[...] + arrived[...].astype(F32)).astype(BF16)


def attention(q, kv, da):
    rows = q.shape[0]
    vmem = pl.BlockSpec(memory_space=pltpu.VMEM)
    return pl.pallas_call(
        attention_body,
        out_shape=[
            jax.ShapeDtypeStruct((rows, 256), BF16),
            jax.ShapeDtypeStruct((rows, 128), BF16),
            jax.ShapeDtypeStruct((rows, 384), BF16),
        ],
        in_specs=[vmem] * 3,
        out_specs=[vmem] * 3,
        scratch_shapes=[
            pltpu.VMEM((rows, 384), BF16),
            pltpu.VMEM((rows, 384), BF16),
            pltpu.VMEM((rows, 384), BF16),
            pltpu.VMEM((rows, 384), F32),
            pltpu.VMEM((rows, 384), F32),
            pltpu.SemaphoreType.DMA((2,)),
            pltpu.SemaphoreType.DMA((2,)),
        ],
        compiler_params=pltpu.CompilerParams(
            collective_id=1, has_side_effects=True, vmem_limit_bytes=32 * 1024 * 1024
        ),
        name="attention",
    )(q, kv, da)


def dot(left, right):
    return jnp.dot(left, right, preferred_element_type=F32)


def dot_rows(left, right):
    return lax.dot_general(left, right, (((0,), (0,)), ((), ())), preferred_element_type=F32)


def dot_cols(left, right):
    return lax.dot_general(left, right, (((1,), (1,)), ((), ())), preferred_element_type=F32)


def parity_matrix(size, dtype):
    row = lax.broadcasted_iota(jnp.int32, (size, size), 0)
    column = lax.broadcasted_iota(jnp.int32, (size, size), 1)
    half = size // 2
    return (column == jnp.where(row < half, 2 * row, 2 * (row - half) + 1)).astype(dtype)


def one_hots(even, odd, h):
    pad = jnp.zeros((1, 8), jnp.int32)
    streams = []
    for stream in (even, odd):
        stream = jnp.concatenate([pad, stream, pad], axis=1)
        streams.append(lax.dynamic_slice_in_dim(stream, 512 * h, 528, axis=1))
    e, o = streams
    where = lax.broadcasted_iota(jnp.int32, (1, 520), 1) - 4 + 512 * h
    inside = jnp.logical_and(where >= 0, where < 1024)
    taps = []
    for parity in range(2):
        rows = []
        for tap in range(-7, 8):
            offset = parity + tap
            source, shift = (e, offset // 2) if offset % 2 == 0 else (o, (offset - 1) // 2)
            rows.append(lax.slice_in_dim(source, 4 + shift, 4 + shift + 520, axis=1))
        rows.append(jnp.zeros((1, 520), jnp.int32))
        taps.append(jnp.where(inside, jnp.concatenate(rows, axis=0), 0))
    taps = jnp.stack(taps)
    code = lax.broadcasted_iota(jnp.int32, (1, 4, 1, 1), 1) + 1
    hot = (taps[:, None] == code).astype(BF16).reshape(2, 64, 520)
    return jnp.stack([hot[:, :, 4 + d : 4 + d + 512] for d in (-4, 0, 4)], axis=1)


def gelu_grad(x):
    inner = math.sqrt(2.0 / math.pi) * (x + 0.044715 * x * x * x)
    t = jnp.tanh(inner)
    slope = math.sqrt(2.0 / math.pi) * (1.0 + 3 * 0.044715 * x * x)
    return 0.5 * (1.0 + t) + 0.5 * x * (1.0 - t * t) * slope


def per_device(
    base_codes,
    stem_weight,
    conv_weight,
    down_weight,
    norm_gain,
    query_weight,
    key_weight,
    value_weight,
    output_weight,
    up_weight,
    cotangent,
):
    s, b = lax.axis_index("seq"), lax.axis_index("batch")
    h = lax.rem(s, 2)

    order = parity_matrix(128, BF16)
    cot = dot(order, cotangent[0]).astype(BF16)
    d_low = (cot[:64].astype(F32) + cot[64:].astype(F32)).astype(BF16)
    codes = dot_cols((base_codes + 1).astype(BF16), order).astype(jnp.int32)
    codes = jnp.broadcast_to(codes, (1, 8, 128))
    codes_all, low_half, cot_blk = exchange(
        [codes, d_low[None], cot[None]], [Codes(), ToWorkers(), ToBlock()], [16, 8, 1], 2
    )
    d_low_half = low_half.reshape(512, 768)
    cot_blk = cot_blk[0]

    stem = jnp.pad(stem_weight, ((0, 1), (0, 0), (0, 0))).transpose(1, 0, 2).reshape(64, 768)
    even = codes_all[:, 0, :64].reshape(1, 1024)
    odd = codes_all[:, 0, 64:].reshape(1, 1024)
    hot = one_hots(even, odd, h)
    emb = jnp.concatenate(
        [
            jnp.concatenate([dot_rows(hot[p, d], stem).astype(BF16) for d in range(3)], axis=1)
            for p in range(2)
        ],
        axis=0,
    )
    conv_flat = conv_weight.reshape(2304, 768)
    conv = dot(emb, conv_flat)
    tower = (emb[:, 768:1536].astype(F32) + jax.nn.gelu(conv)).astype(BF16)
    pooled = (0.5 * (tower[:512].astype(F32) + tower[512:].astype(F32))).astype(BF16)
    lifted = dot(pooled, down_weight).astype(BF16)
    lifted_f = lifted.astype(F32)
    factor = lax.rsqrt(jnp.mean(lifted_f * lifted_f, axis=-1, keepdims=True) + EPSILON)
    normed = (lifted_f * factor * norm_gain).astype(BF16)
    value_pad = jnp.pad(value_weight, ((0, 0), (0, 64)))
    output_pad = jnp.pad(output_weight, ((0, 64), (0, 0)))
    kv_weight = jnp.concatenate([key_weight, value_pad], axis=1)
    q = dot(normed, query_weight).astype(BF16)
    kv = dot(normed, kv_weight).astype(BF16)
    d_mixed = dot_cols(d_low_half, up_weight).astype(BF16)
    d_att = dot_cols(d_mixed, output_pad).astype(BF16)

    att, dq, dkv = attention(q, kv, d_att)

    d_normed_part = (dot_cols(dq, query_weight) + dot_cols(dkv, kv_weight)).astype(BF16)
    mixed_part = dot(att, output_pad).astype(BF16)
    grads = jnp.concatenate(
        [
            dot_rows(normed, dq).astype(BF16),
            dot_rows(normed, dkv)[:, :320].astype(BF16),
            dot_rows(d_mixed, att)[:, :192].astype(BF16),
        ],
        axis=1,
    ).reshape(16, 96, 640)
    mixed_all, d_normed_all, grads_all = exchange(
        [mixed_part.reshape(8, 64, 1536), d_normed_part.reshape(8, 64, 1536), grads],
        [OverBatch(), OverBatch(), OverSeq()],
        [8, 8, 16],
        3,
    )

    def block(array, rows):
        return lax.dynamic_slice_in_dim(array, rows, 64, axis=0)

    def both(array):
        return jnp.concatenate([block(array, 64 * b), block(array, 512 + 64 * b)], axis=0)

    mixed = jnp.sum(mixed_all.astype(F32), axis=0)
    d_normed = jnp.sum(d_normed_all.astype(F32), axis=0).astype(BF16).astype(F32)
    tower_b, conv_b = both(tower), both(conv)
    lifted_b, d_updated = block(lifted_f, 64 * b), block(d_mixed, 64 * b)
    factor_b = block(factor, 64 * b)
    updated = (lifted_b + mixed).astype(BF16)
    lowered = dot(updated, up_weight)
    features = (
        tower_b.astype(F32) + jnp.concatenate([lowered, lowered], axis=0)
    ).astype(BF16)
    features = dot_rows(order, features).astype(BF16)

    gained = d_normed * norm_gain
    d_gain = jnp.sum(d_normed * (lifted_b * factor_b), axis=0, keepdims=True)
    shared = jnp.mean(gained * lifted_b, axis=-1, keepdims=True) * (factor_b * factor_b * factor_b)
    d_lifted = (
        (gained * factor_b - lifted_b * shared).astype(BF16).astype(F32) + d_updated.astype(F32)
    ).astype(BF16)
    d_pooled = dot_cols(d_lifted, down_weight) * 0.5
    d_tower = cot_blk.astype(F32) + jnp.concatenate([d_pooled, d_pooled], axis=0)
    d_tower = d_tower.astype(BF16)
    d_conv = (d_tower.astype(F32) * gelu_grad(conv_b)).astype(BF16)
    d_emb = dot_cols(d_conv, conv_flat)
    stem_part = jnp.zeros((64, 768), F32)
    hot_b = lax.dynamic_slice_in_dim(hot, 64 * b, 64, axis=3)
    hot_b = hot_b.transpose(1, 2, 0, 3).reshape(3, 64, 128)
    for d in range(3):
        term = d_emb[:, 768 * d : 768 * (d + 1)]
        if d == 1:
            term = term + d_tower.astype(F32)
        stem_part = stem_part + dot(hot_b[d], term.astype(BF16))

    first = jnp.concatenate(
        [
            jnp.concatenate([d_lifted, jnp.broadcast_to(d_gain, (16, 1536)).astype(BF16)], axis=0)
            .reshape(80, 8, 192)
            .transpose(1, 0, 2),
            jnp.pad(updated, ((0, 16), (0, 0))).reshape(80, 8, 192).transpose(1, 0, 2),
        ],
        axis=2,
    )
    second = (
        jnp.concatenate([d_conv, stem_part.astype(BF16)], axis=0)
        .reshape(192, 8, 96)
        .transpose(1, 0, 2)
    )
    second = jnp.pad(second, ((0, 0), (0, 0), (0, 32)))
    first_all, second_all = exchange([first, second], [OverBatch(), OverBatch()], [8, 8], 4)

    d_lifted_c = first_all[:, :64, :192].reshape(512, 192)
    updated_c = first_all[:, :64, 192:].reshape(512, 192)
    gain_c = jnp.sum(first_all[:, 64, :192].astype(F32), axis=0)
    d_conv_c = (
        second_all[:, :128, :96].reshape(8, 2, 64, 96).transpose(1, 0, 2, 3).reshape(1024, 96)
    )
    stem_c = jnp.sum(second_all[:, 128:, :96].astype(F32), axis=0)
    down_t = dot_rows(d_lifted_c, pooled)
    up_t = dot_rows(d_low_half, updated_c)
    conv_t = dot_rows(d_conv_c, emb)
    flat = jnp.concatenate(
        [
            down_t.astype(BF16).reshape(16, 72, 128),
            conv_t.astype(BF16).reshape(16, 108, 128),
            stem_c.T.astype(BF16).reshape(16, 3, 128),
            jnp.pad(gain_c.astype(BF16).reshape(16, 1, 12), ((0, 0), (0, 8), (0, 116))),
        ],
        axis=1,
    )
    up_pieces = jnp.pad(up_t.astype(BF16).reshape(16, 48, 192), ((0, 0), (0, 0), (0, 64)))
    flat_all, up_all, features = exchange(
        [flat, up_pieces, features[None]], [Columns(), OverSeq(), ToOwner()], [16, 16, 1], 5
    )
    up_sum = jnp.sum(up_all.astype(F32), axis=0)
    up_sum = jnp.pad(up_sum.reshape(8, 6, 256), ((0, 0), (0, 2), (0, 0)))
    (up_final,) = exchange([up_sum], [OverBatch()], [8], 6)
    grad_up = up_final[:, :6, :192].transpose(0, 2, 1).reshape(1536, 6)

    flat_sum = jnp.sum(flat_all.astype(F32), axis=0)
    grad_down = flat_sum[:72].reshape(12, 768).T
    grad_conv = flat_sum[72:180].reshape(6, 3, 768).transpose(1, 2, 0)
    grad_stem = flat_sum[180:183].reshape(6, 4, 16)[:, :, :15].transpose(2, 1, 0)
    grad_gain = flat_sum[183, :12]
    grads_sum = jnp.sum(grads_all.astype(F32), axis=0)
    return (
        features,
        grad_stem,
        grad_conv,
        grad_down,
        grad_gain,
        grad_up,
        grads_sum[:, :128],
        grads_sum[:, 128:256],
        grads_sum[:, 256:448],
        grads_sum[:, 448:],
    )


def solution(mesh):
    placed = (
        P("batch", "seq"),
        P(),
        P(),
        P(),
        P(),
        P(None, "batch"),
        P(None, "batch"),
        P(None, "batch"),
        P("batch", None),
        P(),
        P("batch", "seq", None),
    )
    return jax.shard_map(
        per_device,
        mesh=mesh,
        in_specs=placed,
        out_specs=(
            P("batch", "seq", None),
            P(None, None, ("seq", "batch")),
            P(None, None, ("seq", "batch")),
            P(None, ("seq", "batch")),
            P(("seq", "batch")),
            P(None, ("seq", "batch")),
            P("seq", "batch"),
            P("seq", "batch"),
            P("seq", "batch"),
            P("seq", "batch"),
        ),
        check_vma=False,
    )
```

time: 1350 us -> 324 us (0.24)
  blocking collectives: 481 us -> 0 us
  starting transfers between devices: 295 us -> 0 us
  waiting for transfers between devices: 278 us -> 0 us
  Pallas kernels: 0 us -> 167 us
  local copies, waits for them, and re-layouts: 178 us -> 77.5 us
  matrix products: 74.5 us -> 49.9 us
  between operations: 17.1 us -> 1.44 us
    unnamed x2 -> x0, blocking collectives: 438 us -> none
    unnamed x100 -> x0, starting transfers between devices: 259 us -> none
    all_gather x6 -> x0, waiting for transfers between devices: 241 us -> none  [the longest x1 53.3 us: per_device(): lax.all_gather(d_attended, 'seq', axis=1, tiled=True)]
    pallas_call x0 -> x6, Pallas kernels: none -> 167 us  [the longest x5 159 us: exchange(): pl.pallas_call(functools.partial(exchange_body, patterns), out_shape=[jax...]
    unnamed x251 -> x98, local copies, waits for them, and re-layouts: 158 us -> 10.4 us
    all_gather x2 -> x0, blocking collectives: 42.9 us -> none  [the longest x1 21.5 us: per_device(): lax.all_gather(log_total, 'seq', axis=1, tiled=True)]
    ppermute x6 -> x0, starting transfers between devices: 35.1 us -> none  [the longest x3 21.1 us: with_halo(): lax.ppermute(lax.slice_in_dim(block, 0, width, axis=dim), axis, backward)]
    reduce_scatter x3 -> x0, waiting for transfers between devices: 26.4 us -> none  [the longest x1 16.1 us: per_device(): lax.psum_scatter(jnp.dot(block, output_weight, preferred_element_type=jnp...]
  transfers between devices with their start and end apart: 115 -> 0, of which waited for: 12 -> 0; matrix products, arithmetic and copies ran while one was open for 45% -> 0% of each run, Pallas kernels for 0% -> 0%
where the time goes in v1:
time: 324 us; the launch traced here: 321 us
  Pallas kernels  167 us (52%)
  local copies, waits for them, and re-layouts  77.5 us (24%)
  matrix products  49.9 us (15%)
  other arithmetic  25.6 us (8%)
    pallas_call x5, Pallas kernels, exchange(): pl.pallas_call(functools.partial(exchange_body, patterns), out_shape=[jax...  159 us
    dot_general x13, matrix products, dot_rows(): lax.dot_general(left, right, (((0,), (0,)), ((), ())), preferred_element_...  22.6 us
    dot_general x10, matrix products, dot(): return jnp.dot(left, right, preferred_element_type=F32)  17 us
    unnamed x98, local copies, waits for them, and re-layouts  10.4 us
    dot_general x7, matrix products, dot_cols(): lax.dot_general(left, right, (((1,), (1,)), ((), ())), preferred_element_...  10.2 us
    pallas_call x1, Pallas kernels, attention(): pl.pallas_call(attention_body, out_shape=[jax.ShapeDtypeStruct((rows, 256...  7.45 us
    concatenate x5, local copies, waits for them, and re-layouts, one_hots(): taps.append(jnp.where(inside, jnp.concatenate(rows, axis=0), 0))  6.89 us

profile of v1, /device:TPU:1, one launch (start us, length us, event | category | flops | bytes accessed | tf_op | source)
XLA Modules:
  0.0 321.3 jit_solution(9838400199025775488)
XLA Ops:
  0.7 2.0 copy-done
  10.7 1.9 copy.50
  12.6 34.5 %exchange_2.1 = (s32[16,8,128]{2,1,0:T(8,128)}, bf16[8,64,768]{2,1,0:T(8,128)(2,1)}, bf16[1,128,768]{2,1,0:T(8,128)(2,1)}) custom-call(s32[1,8,128]{2,1,0:T(8,128)} %broadcast_in_dim.42.refs_0_, bf16[1,64,768]{2,1,0:T(8,128)(2,1)} %fusion.67.refs_1_, bf16[1,128,768]{2,1,0:T(8,128)(2,1)} %bitcast.193), custom_call_target="tpu_custom_call" | custom-call | tf_op jit(solution)/shard_map/exchange_2/pallas_call | solution.py:211
  53.1 2.7 concatenate.171
  55.9 2.7 concatenate.173
  62.4 1.5 squeeze.44
  65.2 1.5 squeeze.43
  68.1 1.5 squeeze.42
  69.5 1.5 convolution_convert_fusion.5
  71.1 1.8 convolution_convert_fusion.6
  72.8 1.7 convolution_convert_fusion.7
  78.1 5.6 %fusion.8 = (bf16[1024,768]{1,0:T(8,128)(2,1)}, f32[1024,768]{1,0:T(8,128)S(1)}) fusion(bf16[512,768]{1,0:T(8,128)(2,1)S(1)} %convolution_convert_fusion.5, bf16[512,768]{1,0:T(8,128)(2,1)S(1)} %convolution_convert_fusion.8, bf16[512,768]{1,0:T(8,128)(2,1)S(1)} %convolution_convert_fusion.6, bf16[512,768]{1,0:T(8,128)(2,1)S(1)} %convolution_convert_fusion.7, ...), kind=kOutput, calls=%fused_computation.13 | convolution fusion | flops 3669491712 | bytes 12976128 | tf_op jit(solution)/shard_map/dot_general | solution.py:313
  84.5 1.6 constant_dynamic-slice_fusion.15
  86.2 2.9 multiply_reduce_fusion
  92.5 7.4 %attention.1 = (bf16[512,256]{1,0:T(8,128)(2,1)S(1)}, bf16[512,128]{1,0:T(8,128)(2,1)S(1)}, bf16[512,384]{1,0:T(8,128)(2,1)S(1)}) custom-call(bf16[512,128]{1,0:T(8,128)(2,1)S(1)} %convolution_convert_fusion.16.q_ref, bf16[512,384]{1,0:T(8,128)(2,1)S(1)} %convolution_convert_fusion.11.kv_ref, bf16[512,256]{1,0:T(8,128)(2,1)S(1)} %convolution_convert_fusion.13.da_ref), custom_call_target="tpu_custom_call" | custom-call | tf_op jit(solution)/shard_map/attention/pallas_call | solution.py:287
  103.4 4.0 %copy.51 = bf16[1536,640]{1,0:T(8,128)(2,1)} copy(bf16[1536,640]{0,1:T(8,128)(2,1)} %pad_maximum_fusion) | data formatting | bytes 3932160 | tf_op jit(solution)/shard_map/concatenate | solution.py:420
  107.4 3.0 convolution_convert_fusion.1
  111.5 1.8 fusion.9
  113.3 66.2 %exchange_3.1 = (bf16[8,64,1536]{2,1,0:T(8,128)(2,1)}, bf16[8,64,1536]{2,1,0:T(8,128)(2,1)}, bf16[16,96,640]{2,1,0:T(8,128)(2,1)}) custom-call(bf16[8,64,1536]{2,1,0:T(8,128)(2,1)} %bitcast.182, bf16[8,64,1536]{2,1,0:T(8,128)(2,1)} %bitcast.183, bf16[16,96,640]{2,1,0:T(8,128)(2,1)} %bitcast.181), custom_call_target="tpu_custom_call" | custom-call | tf_op jit(solution)/shard_map/exchange_3/pallas_call | solution.py:211
  179.5 2.4 reduce_sum.100
  183.4 1.9 convert_reduce_fusion
  186.9 1.8 add_convert_fusion.1
  188.7 1.5 convolution_multiply_fusion
  191.0 2.0 reshape.860
  192.9 1.8 copy.69
  194.7 2.3 fusion.30
  197.0 2.3 fusion.135
  201.1 2.0 reshape.861
  204.1 1.9 pad_maximum_fusion.1.refs_0_
  206.1 2.5 fusion.132
  210.0 2.2 reshape.862
  214.0 14.2 %exchange_4.1 = (bf16[8,80,384]{2,1,0:T(8,128)(2,1)}, bf16[8,192,128]{2,1,0:T(8,128)(2,1)}) custom-call(bf16[8,80,384]{2,1,0:T(8,128)(2,1)} %pad_maximum_fusion.1.refs_0_, bf16[8,192,128]{2,1,0:T(8,128)(2,1)} %pad.36.refs_1_), custom_call_target="tpu_custom_call" | custom-call | tf_op jit(solution)/shard_map/exchange_4/pallas_call | solution.py:211
  228.3 2.4 fusion.13
  232.4 2.5 convolution_convert_fusion.12
  235.0 1.9 reshape.864
  239.5 8.5 %convolution_convert_fusion = bf16[96,2304]{1,0:T(8,128)(2,1)} fusion(bf16[1024,96]{1,0:T(8,128)(2,1)S(1)} %bitcast.201, bf16[512,768]{1,0:T(8,128)(2,1)} %copy-done.21, bf16[512,768]{1,0:T(8,128)(2,1)} %copy-done.22, bf16[512,768]{1,0:T(8,128)(2,1)} %copy-done.23, bf16[512,768]{1,0:T(8,128)(2,1)} %copy-done.24, bf16[512,768]{1,0:T(8,128)(2,1)} %copy-done.25, ...), kind=kOutput, calls=%fused_computation.3 | convolution fusion | flops 481517568 | bytes 5357568 | tf_op jit(solution)/shard_map/dot_general | solution.py:317
  249.5 2.4 reshape.867
  251.9 2.1 fusion.20.refs_0_
  254.0 1.9 copy.61
  255.9 1.8 pad.38.refs_1_
  257.7 35.9 %exchange_5.1 = (bf16[16,192,128]{2,1,0:T(8,128)(2,1)}, bf16[16,48,256]{2,1,0:T(8,128)(2,1)}, bf16[1,128,768]{2,1,0:T(8,128)(2,1)}) custom-call(bf16[16,192,128]{2,1,0:T(8,128)(2,1)} %fusion.20.refs_0_, bf16[16,48,256]{2,1,0:T(8,128)(2,1)} %pad.38.refs_1_, bf16[1,128,768]{2,1,0:T(8,128)(2,1)} %fusion.15.refs_2_), custom_call_target="tpu_custom_call" | custom-call | tf_op jit(solution)/shard_map/exchange_5/pallas_call | solution.py:211
  293.6 1.7 convert_reduce_fusion.3
  296.7 1.5 pad.39.refs_0_
  298.2 8.6 %exchange_6.1 = f32[8,8,256]{2,1,0:T(8,128)} custom-call(f32[8,8,256]{2,1,0:T(8,128)} %pad.39.refs_0_), custom_call_target="tpu_custom_call" | custom-call | tf_op jit(solution)/shard_map/exchange_6/pallas_call | solution.py:211
  308.3 1.5 reshape.875
  316.7 1.5 reshape.872
  318.1 1.5 copy.63
  319.7 1.6 copy.72
  (176 shorter events, 58.1 us)
Async XLA Ops:
  0.6 2.0 copy-start
  2.7 44.5 %copy-start.39 = (pred[128]{0:T(512)(128)(4,1)}, pred[128]{0:T(512)(128)(4,1)S(1)}, u32[]{:S(2)}) copy-start(pred[128]{0:T(512)(128)(4,1)S(1)} %iota_compare_fusion.2) | copy-start | bytes 388
  3.3 43.9 %copy-start.41 = (s32[128]{0:T(128)}, s32[128]{0:T(128)S(1)}, u32[]{:S(2)}) copy-start(s32[128]{0:T(128)S(1)} %get-tuple-element.114) | copy-start | bytes 1540
  3.3 43.9 %copy-start.43 = (s32[128]{0:T(128)}, s32[128]{0:T(128)S(1)}, u32[]{:S(2)}) copy-start(s32[128]{0:T(128)S(1)} %get-tuple-element.115) | copy-start | bytes 1540
  9.4 0.7 copy-start.14
  69.5 5.0 %copy-start.7 = (bf16[16,4,768]{2,0,1:T(8,128)(2,1)S(1)}, bf16[16,4,768]{2,0,1:T(8,128)(2,1)}, u32[]{:S(2)}) copy-start(bf16[16,4,768]{2,0,1:T(8,128)(2,1)} %pad.32) | copy-start | bytes 294916
  69.5 5.0 %copy-start.20 = (pred[2,64,520]{2,1,0:T(32,128)(4,1)S(1)}, pred[2,64,520]{2,1,0:T(32,128)(4,1)}, u32[]{:S(2)}) copy-start(pred[2,64,520]{2,1,0:T(32,128)(4,1)} %get-tuple-element.73) | copy-start | bytes 199684
  71.0 7.0 %copy-start.21 = (bf16[512,768]{1,0:T(8,128)(2,1)}, bf16[512,768]{1,0:T(8,128)(2,1)S(1)}, u32[]{:S(2)}) copy-start(bf16[512,768]{1,0:T(8,128)(2,1)S(1)} %convolution_convert_fusion.5) | copy-start | bytes 2359300
  71.0 4.9 %copy-start.11 = (bf16[1536,768]{1,0:T(8,128)(2,1)S(1)}, bf16[1536,768]{1,0:T(8,128)(2,1)}, u32[]{:S(2)}) copy-start(bf16[1536,768]{1,0:T(8,128)(2,1)} %param.20) | copy-start | bytes 7077892
  71.0 4.9 %copy-start.27 = (bf16[8,64,768]{2,1,0:T(8,128)(2,1)S(1)}, bf16[8,64,768]{2,1,0:T(8,128)(2,1)}, u32[]{:S(2)}) copy-start(bf16[8,64,768]{2,1,0:T(8,128)(2,1)} %get-tuple-element.25) | copy-start | bytes 2359300
  72.8 5.3 %copy-start.22 = (bf16[512,768]{1,0:T(8,128)(2,1)}, bf16[512,768]{1,0:T(8,128)(2,1)S(1)}, u32[]{:S(2)}) copy-start(bf16[512,768]{1,0:T(8,128)(2,1)S(1)} %convolution_convert_fusion.6) | copy-start | bytes 2359300
  74.5 3.6 %copy-start.23 = (bf16[512,768]{1,0:T(8,128)(2,1)}, bf16[512,768]{1,0:T(8,128)(2,1)S(1)}, u32[]{:S(2)}) copy-start(bf16[512,768]{1,0:T(8,128)(2,1)S(1)} %convolution_convert_fusion.7) | copy-start | bytes 2359300
  75.0 3.1 copy-start.24
  75.5 2.6 copy-start.25
  76.0 2.1 copy-start.26
  76.0 1.4 copy-start.29
  77.5 23.8 %copy-start.12 = (bf16[512,1536]{1,0:T(8,128)(2,1)}, bf16[512,1536]{1,0:T(8,128)(2,1)S(1)}, u32[]{:S(2)}) copy-start(bf16[512,1536]{1,0:T(8,128)(2,1)S(1)} %convolution_convert_fusion.2) | copy-start | bytes 4718596
  78.1 8.0 %copy-start.9 = (bf16[768,1536]{1,0:T(8,128)(2,1)S(1)}, bf16[768,1536]{1,0:T(8,128)(2,1)}, u32[]{:S(2)}) copy-start(bf16[768,1536]{1,0:T(8,128)(2,1)} %param.14) | copy-start | bytes 7077892
  86.2 3.0 copy-start.35
  89.1 1.6 copy-start.6
  89.2 1.5 copy-start.17
  89.2 2.1 copy-start.30
  89.2 2.3 copy-start.45
  99.9 1.3 copy-start.2
  100.0 1.3 copy-start.4
  100.0 1.4 copy-start.1
  107.4 3.0 copy-start.5
  107.4 3.0 copy-start.31
  107.4 3.0 copy-start.46
  110.4 1.0 copy-start.3
  110.4 1.1 copy-start.18
  181.8 4.8 %copy-start.19 = (bf16[8,64,1536]{2,1,0:T(8,128)(2,1)S(1)}, bf16[8,64,1536]{2,1,0:T(8,128)(2,1)}, u32[]{:S(2)}) copy-start(bf16[8,64,1536]{2,1,0:T(8,128)(2,1)} %get-tuple-element.30) | copy-start | bytes 4718596
  183.4 3.5 %copy-start.15 = (bf16[64,1536]{1,0:T(8,128)(2,1)S(1)}, bf16[64,1536]{1,0:T(8,128)(2,1)}, u32[]{:S(2)}) copy-start(bf16[64,1536]{1,0:T(8,128)(2,1)} %reduce_sum.100) | copy-start | bytes 589828
  185.3 3.4 %copy-start.10 = (bf16[768,1536]{1,0:T(8,128)(2,1)S(1)}, bf16[768,1536]{1,0:T(8,128)(2,1)}, u32[]{:S(2)}) copy-start(bf16[768,1536]{1,0:T(8,128)(2,1)} %param.14) | copy-start | bytes 7077892
  190.9 8.4 %copy-start.40 = (pred[128]{0:T(512)(128)(4,1)S(1)}, pred[128]{0:T(512)(128)(4,1)}, u32[]{:S(2)}) copy-start(pred[128]{0:T(512)(128)(4,1)} %copy-done.39) | copy-start | bytes 388
  191.0 8.4 %copy-start.42 = (s32[128]{0:T(128)S(1)}, s32[128]{0:T(128)}, u32[]{:S(2)}) copy-start(s32[128]{0:T(128)} %copy-done.41) | copy-start | bytes 1540
  191.0 8.4 %copy-start.44 = (s32[128]{0:T(128)S(1)}, s32[128]{0:T(128)}, u32[]{:S(2)}) copy-start(s32[128]{0:T(128)} %copy-done.43) | copy-start | bytes 1540
  192.9 6.4 %copy-start.33 = (bf16[64,768]{1,0:T(8,128)(2,1)S(1)}, bf16[64,768]{1,0:T(8,128)(2,1)}, u32[]{:S(2)}) copy-start(bf16[64,768]{1,0:T(8,128)(2,1)} %get-tuple-element.78) | copy-start | bytes 294916
  192.9 6.4 %copy-start.34 = (bf16[64,768]{1,0:T(8,128)(2,1)S(1)}, bf16[64,768]{1,0:T(8,128)(2,1)}, u32[]{:S(2)}) copy-start(bf16[64,768]{1,0:T(8,128)(2,1)} %get-tuple-element.79) | copy-start | bytes 294916
  194.7 5.7 %copy-start.16 = (bf16[64,1536]{1,0:T(8,128)(2,1)S(1)}, bf16[64,1536]{1,0:T(8,128)(2,1)}, u32[]{:S(2)}) copy-start(bf16[64,1536]{1,0:T(8,128)(2,1)} %get-tuple-element.77) | copy-start | bytes 589828
  206.1 2.6 copy-start.38
  206.1 2.7 copy-start.8
  206.1 2.8 copy-start.13
  206.1 2.8 copy-start.36
  206.1 3.0 copy-start.37
  206.1 3.1 copy-start.28
  311.1 0.6 copy-start.32

commit v2 on v0

v2 whole, which is shorter than its diff:
```python
import functools
import math

import jax
import jax.numpy as jnp
from jax import lax
from jax.experimental import pallas as pl
from jax.experimental.pallas import tpu as pltpu
from jax.sharding import PartitionSpec as P

EPSILON = 1e-06
MESH = pl.DeviceIdType.MESH
F32 = jnp.float32
BF16 = jnp.bfloat16
SEQ = 16
BATCH = 8


class OverBatch:
    count = BATCH

    def dst(self, i, s, b):
        j = lax.rem(b + i, BATCH)
        return j, s, j, b

    def src(self, i, s, b):
        j = lax.rem(b + BATCH - i, BATCH)
        return j, s, j


class OverSeq:
    count = SEQ

    def dst(self, i, s, b):
        j = lax.rem(s + i, SEQ)
        return j, j, b, s

    def src(self, i, s, b):
        j = lax.rem(s + SEQ - i, SEQ)
        return j, j, b


class Columns:
    count = SEQ

    def dst(self, i, s, b):
        j = lax.rem(s + i, SEQ)
        return j, 2 * b + j // BATCH, lax.rem(j, BATCH), s

    def src(self, i, s, b):
        j = lax.rem(SEQ * BATCH + lax.rem(s, 2) * BATCH + b - i, SEQ)
        return j, j, s // 2


class Codes:
    count = 2 * BATCH

    def dst(self, i, s, b):
        j = lax.rem(b + i // 2, BATCH)
        return 0, 2 * b + i % 2, j, s

    def src(self, i, s, b):
        return i, i, s // 2


class ToWorkers:
    count = BATCH

    def dst(self, i, s, b):
        return 0, 2 * b + s // BATCH, lax.rem(s + i, BATCH), lax.rem(s, BATCH)

    def src(self, i, s, b):
        j = lax.rem(b + BATCH - i, BATCH)
        return j, BATCH * lax.rem(s, 2) + j, s // 2


class ToBlock:
    count = 1

    def dst(self, i, s, b):
        return 0, 2 * b + s // BATCH, lax.rem(s, BATCH), 0

    def src(self, i, s, b):
        return 0, BATCH * lax.rem(s, 2) + b, s // 2


class ToOwner:
    count = 1

    def dst(self, i, s, b):
        return 0, BATCH * lax.rem(s, 2) + b, s // 2, 0

    def src(self, i, s, b):
        return 0, 2 * b + s // BATCH, lax.rem(s, BATCH)


class Link:
    def __init__(self, pattern, source, result, sends, receives, s, b):
        self.pattern, self.source, self.result = pattern, source, result
        self.sends, self.receives, self.s, self.b = sends, receives, s, b

    def copy(self, i):
        piece, target_s, target_b, slot = self.pattern.dst(i, self.s, self.b)
        away = jnp.logical_or(target_s != self.s, target_b != self.b)
        return away, pltpu.make_async_remote_copy(
            src_ref=self.source(piece),
            dst_ref=self.result.at[slot],
            send_sem=self.sends.at[i],
            recv_sem=self.receives.at[slot],
            device_id=(target_s, target_b),
            device_id_type=MESH,
        )

    def keep(self, i):
        piece, target_s, target_b, slot = self.pattern.dst(i, self.s, self.b)
        home = jnp.logical_and(target_s == self.s, target_b == self.b)

        @pl.when(home)
        def _():
            self.result[slot] = self.source(piece)[...]

    def each(self, action):
        def step(i, carry):
            action(i)
            return carry

        lax.fori_loop(0, self.pattern.count, step, 0)

    def start_one(self, i):
        away, copy = self.copy(i)
        pl.when(away)(copy.start)

    def start(self):
        self.each(self.start_one)
        self.each(self.keep)

    def receive(self):
        def wait(i):
            slot, other_s, other_b = self.pattern.src(i, self.s, self.b)
            away = jnp.logical_or(other_s != self.s, other_b != self.b)
            copy = pltpu.make_async_remote_copy(
                src_ref=self.result.at[slot],
                dst_ref=self.result.at[slot],
                send_sem=self.sends.at[i],
                recv_sem=self.receives.at[slot],
                device_id=(other_s, other_b),
                device_id_type=MESH,
            )
            pl.when(away)(copy.wait_recv)

        self.each(wait)

    def drain(self):
        def wait(i):
            away, copy = self.copy(i)
            pl.when(away)(copy.wait_send)

        self.each(wait)


def dot(left, right):
    return jnp.dot(left, right, preferred_element_type=F32)


def dot_rows(left, right):
    return lax.dot_general(left, right, (((0,), (0,)), ((), ())), preferred_element_type=F32)


def dot_cols(left, right):
    return lax.dot_general(left, right, (((1,), (1,)), ((), ())), preferred_element_type=F32)


def iota(shape, dim):
    return lax.broadcasted_iota(jnp.int32, shape, dim)


def zero_one(mask):
    return jnp.where(mask, 1.0, 0.0).astype(BF16)


def gelu_grad(x):
    inner = math.sqrt(2.0 / math.pi) * (x + 0.044715 * x * x * x)
    t = jnp.tanh(inner)
    slope = math.sqrt(2.0 / math.pi) * (1.0 + 3 * 0.044715 * x * x)
    return 0.5 * (1.0 + t) + 0.5 * x * (1.0 - t * t) * slope


INPUTS = ["codes", "cot", "gain", "stem", "conv_h", "down_h", "q_h", "k_h", "v_h", "o_h", "up_h"]
OUTPUTS = [
    ("features", (128, 768), BF16),
    ("g_stem", (64, 6), F32),
    ("g_conv", (2304, 6), F32),
    ("g_down", (768, 12), F32),
    ("g_gain", (16, 128), F32),
    ("g_up", (1536, 6), F32),
    ("g_q", (96, 128), F32),
    ("g_k", (96, 128), F32),
    ("g_v", (96, 192), F32),
    ("g_o", (96, 192), F32),
]
SCRATCH = [
    ("conv_w", (2304, 768), BF16),
    ("down_w", (768, 1536), BF16),
    ("q_w", (1536, 128), BF16),
    ("k_w", (1536, 128), BF16),
    ("v_raw", (1536, 192), BF16),
    ("v_w", (1536, 256), BF16),
    ("o_w", (256, 1536), BF16),
    ("up_w", (1536, 768), BF16),
    ("select", (768, 1024), BF16),
    ("codes_s", (1, 8, 128), F32),
    ("codes_r", (16, 8, 128), F32),
    ("low_s", (1, 64, 768), BF16),
    ("low_r", (8, 64, 768), BF16),
    ("blk_s", (1, 128, 768), BF16),
    ("blk_r", (1, 128, 768), BF16),
    ("code", (2, 640, 128), F32),
    ("picked", (2, 528, 128), F32),
    ("emb", (8, 128, 2304), BF16),
    ("conv", (8, 128, 768), F32),
    ("tower", (8, 128, 768), BF16),
    ("pooled", (8, 80, 896), BF16),
    ("lifted", (512, 1536), BF16),
    ("factor", (512, 128), F32),
    ("normed", (512, 1536), BF16),
    ("q", (512, 128), BF16),
    ("kv", (512, 384), BF16),
    ("kv_far", (512, 384), BF16),
    ("d_mixed", (512, 1536), BF16),
    ("d_att", (512, 256), BF16),
    ("att", (512, 256), BF16),
    ("dqkv", (512, 512), BF16),
    ("dkv_own", (512, 384), F32),
    ("dkv_far", (512, 384), F32),
    ("dkv_s", (512, 384), BF16),
    ("dkv_r", (512, 384), BF16),
    ("low_sel", (512, 1024), BF16),
    ("mixed_s", (8, 64, 1536), BF16),
    ("mixed_r", (8, 64, 1536), BF16),
    ("dn_s", (8, 64, 1536), BF16),
    ("dn_r", (8, 64, 1536), BF16),
    ("proj_s", (1536, 640), BF16),
    ("proj_r", (16, 96, 640), BF16),
    ("feat_s", (1, 128, 768), BF16),
    ("feat_r", (1, 128, 768), BF16),
    ("upd_s", (8, 64, 256), BF16),
    ("upd_r", (8, 64, 256), BF16),
    ("dl_s", (8, 80, 256), BF16),
    ("dl_r", (8, 80, 256), BF16),
    ("dc_s", (8, 192, 128), BF16),
    ("dc_r", (8, 192, 128), BF16),
    ("up_s", (16, 64, 256), BF16),
    ("up_r", (16, 64, 256), BF16),
    ("down_s", (16, 16, 896), BF16),
    ("down_r", (16, 16, 896), BF16),
    ("conv_acc", (128, 2304), F32),
    ("conv_s", (16, 16, 1280), BF16),
    ("conv_r", (16, 16, 1280), BF16),
    ("last_s", (8, 8, 256), F32),
    ("last_r", (8, 8, 256), F32),
]
LINKS = [
    ("codes", Codes()),
    ("low", ToWorkers()),
    ("blk", ToBlock()),
    ("mixed", OverBatch()),
    ("dn", OverBatch()),
    ("proj", OverSeq()),
    ("feat", ToOwner()),
    ("upd", OverBatch()),
    ("dl", OverBatch()),
    ("dc", OverBatch()),
    ("up", OverSeq()),
    ("down", Columns()),
    ("conv", Columns()),
    ("last", OverBatch()),
]
WEIGHTS = [
    ("conv_h", "conv_w"),
    ("down_h", "down_w"),
    ("q_h", "q_w"),
    ("k_h", "k_w"),
    ("v_h", "v_raw"),
    ("o_h", "o_w"),
    ("up_h", "up_w"),
]


class Namespace:
    pass


def loop(count, step):
    def body(i, carry):
        step(i)
        return carry

    lax.fori_loop(0, count, body, 0)


def rows_of(i, size):
    return pl.ds(pl.multiple_of(i * size, size), size)


def kernel_body(*refs):
    names = INPUTS + [x[0] for x in OUTPUTS] + [x[0] + "_" for x in SCRATCH]
    n = Namespace()
    for name, ref in zip(names, refs):
        setattr(n, name, ref)
    semaphores = refs[len(names) :]
    weight_sems, swap_send, swap_recv = semaphores[:3]
    s, b = lax.axis_index("seq"), lax.axis_index("batch")
    h = lax.rem(s, 2)
    peer = (s + 1 - 2 * h, b)
    links = {}
    for k, (name, pattern) in enumerate(LINKS):
        sent = getattr(n, name + "_s_")
        if name == "proj":
            source = lambda piece, sent=sent: sent.at[rows_of(piece, 96)]
        else:
            source = lambda piece, sent=sent: sent.at[piece]
        links[name] = Link(
            pattern, source, getattr(n, name + "_r_"), semaphores[3 + 2 * k], semaphores[4 + 2 * k], s, b
        )

    barrier = pltpu.get_barrier_semaphore()
    for name in ("codes", "mixed", "proj", "down", "feat"):
        pattern = links[name].pattern

        def greet(i, pattern=pattern):
            _, other_s, other_b = pattern.src(i, s, b)

            @pl.when(jnp.logical_or(other_s != s, other_b != b))
            def _():
                pl.semaphore_signal(
                    barrier, inc=1, device_id=(other_s, other_b), device_id_type=MESH
                )

        loop(pattern.count, greet)
    own_window = (b == s // 2).astype(jnp.int32)
    own_block = own_window * (s == BATCH * h + b).astype(jnp.int32)
    expected = 16 + 7 + 15 + 16 + 1 - 2 * own_window - own_block

    weights = [
        pltpu.make_async_copy(getattr(n, source), getattr(n, target + "_"), weight_sems.at[k])
        if target != "o_w"
        else pltpu.make_async_copy(n.o_h, n.o_w_.at[pl.ds(0, 192)], weight_sems.at[k])
        for k, (source, target) in enumerate(WEIGHTS)
    ]
    for copy in weights:
        copy.start()

    row, column = iota((128, 128), 0), iota((128, 128), 1)
    order = zero_one(column == jnp.where(row < 64, 2 * row, 2 * row - 127))
    cot = dot(order, n.cot[...])
    n.blk_s_[0] = cot.astype(BF16)
    n.low_s_[0] = (cot[:64] + cot[64:]).astype(BF16)
    codes = jnp.broadcast_to((n.codes[...] + 1).astype(F32), (8, 128)).astype(BF16)
    n.codes_s_[0] = dot_cols(codes, order)

    pl.semaphore_wait(barrier, expected)
    links["codes"].start()
    links["low"].start()
    links["blk"].start()

    def fill(c):
        lane = iota((768, 128), 1) + 128 * c
        wanted = 6 * (lane // 8) + lane % 8
        hit = jnp.logical_and(iota((768, 128), 0) == wanted, lane % 8 < 6)
        n.select_[:, rows_of(c, 128)] = zero_one(hit)

    loop(8, fill)
    n.o_w_[192:, :] = jnp.zeros((64, 1536), BF16)
    gain_row = zero_one(jnp.logical_and(iota((16, 128), 0) == 0, iota((16, 128), 1) == 0))
    for j in range(8):
        n.pooled_[j, :, 768:] = jnp.zeros((80, 128), BF16)
        n.pooled_[j, 64:, :768] = jnp.zeros((16, 768), BF16)
        n.pooled_[j, 64:, 768:] = gain_row

    links["codes"].receive()
    ones = jnp.ones((128, 128), BF16)
    for i in range(10):
        place = BATCH * h + (i - 1)
        inside = jnp.logical_and(place >= 0, place < 16)
        line = n.codes_r_[jnp.clip(place, 0, 15)][0:1]
        line = jnp.where(inside, line, 0.0)
        spread = dot(jnp.where(row == column, line, 0.0).astype(BF16), ones)
        n.code_[0, 64 * i : 64 * i + 64] = spread[:64]
        n.code_[1, 64 * i : 64 * i + 64] = spread[64:]
    lane_tap = iota((1, 128), 1) // 4
    lane_code = (iota((1, 128), 1) % 4 + 1).astype(F32)
    for parity in range(2):
        picked = jnp.zeros((528, 128), F32)
        for tap in range(15):
            offset = parity + tap - 7
            stream, shift = offset % 2, (offset - offset % 2) // 2
            begin = 56 + shift
            picked = jnp.where(lane_tap == tap, n.code_[stream, begin : begin + 528, :], picked)
        where = iota((528, 128), 0) - 8 + 512 * h
        inside = jnp.logical_and(where >= 0, where < 1024)
        n.picked_[parity] = jnp.where(inside, picked, 0.0)

    def one_hots(j):
        found = []
        for parity in range(2):
            near = n.picked_[parity, pl.ds(pl.multiple_of(64 * j, 64), 80), :]
            for step in (-4, 0, 4):
                found.append(zero_one(near[8 + step : 72 + step] == lane_code))
        return found

    def embed(j):
        value = dot(jnp.concatenate(one_hots(j), axis=0), n.stem[...]).astype(BF16)
        for parity in range(2):
            for step in range(3):
                begin = 64 * (3 * parity + step)
                n.emb_[j, 64 * parity : 64 * parity + 64, 768 * step : 768 * step + 768] = value[
                    begin : begin + 64
                ]

    loop(8, embed)
    for copy in weights:
        copy.wait()
    n.v_w_[:, 128:] = jnp.zeros((1536, 128), BF16)
    n.v_w_[:, :192] = n.v_raw_[...]

    def forward(t):
        pair = pl.ds(2 * t, 2)
        here = rows_of(t, 128)
        conv = dot(n.emb_[pair].reshape(256, 2304), n.conv_w_[...])
        n.conv_[pair] = conv.reshape(2, 128, 768)
        center = n.emb_[pair, :, 768:1536].reshape(256, 768).astype(F32)
        tower = (center + jax.nn.gelu(conv)).astype(BF16)
        n.tower_[pair] = tower.reshape(2, 128, 768)
        halves = tower.astype(F32).reshape(2, 2, 64, 768)
        pooled = (0.5 * (halves[:, 0] + halves[:, 1])).astype(BF16)
        n.pooled_[pair, 0:64, 0:768] = pooled
        lifted = dot(pooled.reshape(128, 768), n.down_w_[...]).astype(BF16)
        n.lifted_[here, :] = lifted
        lifted = lifted.astype(F32)
        factor = lax.rsqrt(jnp.mean(lifted * lifted, axis=-1, keepdims=True) + EPSILON)
        n.factor_[here, :] = jnp.broadcast_to(factor, (128, 128))
        normed = (lifted * factor * n.gain[...]).astype(BF16)
        n.normed_[here, :] = normed
        n.q_[here, :] = dot(normed, n.q_w_[...]).astype(BF16)
        n.kv_[here, :128] = dot(normed, n.k_w_[...]).astype(BF16)
        n.kv_[here, 128:] = dot(normed, n.v_w_[...]).astype(BF16)

    loop(4, forward)
    swap = pltpu.make_async_remote_copy(
        src_ref=n.kv_, dst_ref=n.kv_far_, send_sem=swap_send.at[0], recv_sem=swap_recv.at[0],
        device_id=peer, device_id_type=MESH,
    )
    swap.start()
    links["low"].receive()

    def cotangents(t):
        pair, here = pl.ds(2 * t, 2), rows_of(t, 128)
        low = n.low_r_[pair].reshape(128, 768)
        d_mixed = dot_cols(low, n.up_w_[...]).astype(BF16)
        n.d_mixed_[here, :] = d_mixed
        n.d_att_[here, :] = dot_cols(d_mixed, n.o_w_[...]).astype(BF16)
        n.low_sel_[here, :] = dot(low, n.select_[...]).astype(BF16)

    loop(4, cotangents)
    n.dkv_own_[...] = jnp.zeros((512, 384), F32)
    n.dkv_far_[...] = jnp.zeros((512, 384), F32)
    swap.wait()

    scale = 1.0 / math.sqrt(128)

    def send_pair(link, t):
        for j in (2 * t, 2 * t + 1):
            i = lax.rem(j - b + BATCH, BATCH)
            link.start_one(i)

    def attend(t):
        here = rows_of(t, 128)
        q, da = n.q_[here, :], n.d_att_[here, :]
        blocks = ((n.kv_, n.dkv_own_), (n.kv_far_, n.dkv_far_))
        scores = [dot_cols(q, kv[:, :128]) * scale for kv, _ in blocks]
        total = sum(jnp.sum(jnp.exp(x), axis=1, keepdims=True) for x in scores)
        log_total = jnp.log(total)
        probs = [jnp.exp(x - log_total) for x in scores]
        dprobs = [dot_cols(da, kv[:, 128:]) for kv, _ in blocks]
        inner = sum(jnp.sum(p * d, axis=1, keepdims=True) for p, d in zip(probs, dprobs))
        att = jnp.zeros((128, 256), F32)
        dq = jnp.zeros((128, 128), F32)
        for (kv, total_ref), p, d in zip(blocks, probs, dprobs):
            ds = (p * (d - inner)).astype(BF16)
            pb = p.astype(BF16)
            att = att + dot(pb, kv[:, 128:])
            dq = dq + dot(ds, kv[:, :128])
            total_ref[:, :128] += dot_rows(ds, q) * scale
            total_ref[:, 128:] += dot_rows(pb, da)
        att = att.astype(BF16)
        n.att_[here, :] = att
        n.dqkv_[here, :128] = (dq * scale).astype(BF16)
        n.mixed_s_[pl.ds(2 * t, 2)] = dot(att, n.o_w_[...]).astype(BF16).reshape(2, 64, 1536)
        send_pair(links["mixed"], t)

    loop(4, attend)
    n.dkv_s_[...] = n.dkv_far_[...].astype(BF16)
    swap_back = pltpu.make_async_remote_copy(
        src_ref=n.dkv_s_, dst_ref=n.dkv_r_, send_sem=swap_send.at[1], recv_sem=swap_recv.at[1],
        device_id=peer, device_id_type=MESH,
    )
    swap_back.start()
    swap_back.wait()
    n.dqkv_[:, 128:] = (n.dkv_own_[...] + n.dkv_r_[...].astype(F32)).astype(BF16)

    def back_through_projections(t):
        here = rows_of(t, 128)
        d_normed = (
            dot_cols(n.dqkv_[here, :128], n.q_w_[...])
            + dot_cols(n.dqkv_[here, 128:256], n.k_w_[...])
            + dot_cols(n.dqkv_[here, 256:], n.v_w_[...])
        )
        n.dn_s_[pl.ds(2 * t, 2)] = d_normed.astype(BF16).reshape(2, 64, 1536)
        send_pair(links["dn"], t)

    loop(4, back_through_projections)

    def projection_grads(c):
        chunk = rows_of(c, 128)
        first = dot_rows(n.normed_[:, chunk], n.dqkv_[...]).astype(BF16)
        second = dot_rows(n.d_mixed_[:, chunk], n.att_[...]).astype(BF16)
        n.proj_s_[chunk, :] = jnp.concatenate([first[:, :448], second[:, :192]], axis=1)

    loop(12, projection_grads)
    links["proj"].start()

    here = rows_of(b, 64)
    links["mixed"].each(links["mixed"].keep)
    links["dn"].each(links["dn"].keep)
    hots = one_hots(b)
    lifted = n.lifted_[here, :].astype(F32)
    factor = n.factor_[here, 0:1]
    d_updated = n.d_mixed_[here, :].astype(F32)
    links["mixed"].receive()
    mixed = n.mixed_r_[0].astype(F32)
    for j in range(1, 8):
        mixed = mixed + n.mixed_r_[j].astype(F32)
    updated = (lifted + mixed).astype(BF16)

    def select_into(target, value):
        for half in range(2):
            moved = dot(value[:, 768 * half : 768 * half + 768], n.select_[...]).astype(BF16)
            for j in range(4):
                target[4 * half + j] = moved[:, 256 * j : 256 * j + 256]

    select_into(n.upd_s_, updated)
    links["upd"].start()
    lowered = dot(updated, n.up_w_[...])
    features = n.tower_[b].astype(F32) + jnp.concatenate([lowered, lowered], axis=0)
    n.feat_s_[0] = dot_rows(order, features.astype(BF16)).astype(BF16)
    links["feat"].start()

    links["dn"].receive()
    d_normed = n.dn_r_[0].astype(F32)
    for j in range(1, 8):
        d_normed = d_normed + n.dn_r_[j].astype(F32)
    d_normed = d_normed.astype(BF16).astype(F32)
    gained = d_normed * n.gain[...]
    d_gain = jnp.sum(d_normed * (lifted * factor), axis=0, keepdims=True)
    shared = jnp.mean(gained * lifted, axis=-1, keepdims=True) * (factor * factor * factor)
    d_lifted = (gained * factor - lifted * shared).astype(BF16).astype(F32) + d_updated
    d_lifted = d_lifted.astype(BF16)
    select_into(
        n.dl_s_,
        jnp.concatenate([d_lifted, jnp.broadcast_to(d_gain, (16, 1536)).astype(BF16)], axis=0),
    )
    links["dl"].start()
    d_pooled = dot_cols(d_lifted, n.down_w_[...]) * 0.5
    links["blk"].receive()
    d_tower = n.blk_r_[0].astype(F32) + jnp.concatenate([d_pooled, d_pooled], axis=0)
    d_tower = d_tower.astype(BF16)
    d_conv = (d_tower.astype(F32) * gelu_grad(n.conv_[b])).astype(BF16)
    d_stem = jnp.zeros((128, 768), F32)
    for step in range(3):
        d_emb = dot_cols(d_conv, n.conv_w_[768 * step : 768 * step + 768, :])
        if step == 1:
            d_emb = d_emb + d_tower.astype(F32)
        hot = jnp.concatenate([hots[step], hots[3 + step]], axis=0)
        d_stem = d_stem + dot_rows(hot, d_emb.astype(BF16))
    both = jnp.concatenate([d_conv, d_stem[:64].astype(BF16)], axis=0)
    both = dot(both, n.select_[...]).astype(BF16)
    for j in range(8):
        n.dc_s_[j] = both[:, 128 * j : 128 * j + 128]
    links["dc"].start()

    links["upd"].receive()
    updated = n.upd_r_[...].reshape(512, 256)
    n.up_s_[...] = dot_rows(n.low_sel_[...], updated).astype(BF16).reshape(16, 64, 256)
    links["up"].start()
    links["dl"].receive()
    down = dot_rows(n.dl_r_[...].reshape(640, 256), n.pooled_[...].reshape(640, 896))
    n.down_s_[...] = down.astype(BF16).reshape(16, 16, 896)
    links["down"].start()
    n.conv_acc_[...] = jnp.zeros((128, 2304), F32)
    links["dc"].receive()

    def conv_grads(t):
        pair = pl.ds(2 * t, 2)
        left = n.dc_r_[pair, 0:128, :].reshape(256, 128)
        n.conv_acc_[...] += dot_rows(left, n.emb_[pair].reshape(256, 2304))

    loop(4, conv_grads)
    same = zero_one(iota((512, 128), 0) % 64 == iota((512, 128), 1))
    stem = dot_rows(n.dc_r_[:, 128:, :].reshape(512, 128), same)
    n.conv_s_[:, 0:8, :] = n.conv_acc_[:, :1280].reshape(16, 8, 1280).astype(BF16)
    rest = jnp.concatenate([n.conv_acc_[:, 1280:], stem, jnp.zeros((128, 128), F32)], axis=1)
    n.conv_s_[:, 8:16, :] = rest.reshape(16, 8, 1280).astype(BF16)
    links["conv"].start()

    def total(ref, count):
        value = ref[0].astype(F32)
        for j in range(1, count):
            value = value + ref[j].astype(F32)
        return value

    links["up"].receive()
    n.last_s_[...] = total(n.up_r_, 16).reshape(8, 8, 256)
    links["last"].start()
    links["proj"].receive()
    proj = total(n.proj_r_, 16)
    n.g_q[...] = proj[:, :128]
    n.g_k[...] = proj[:, 128:256]
    n.g_v[...] = proj[:, 256:448]
    n.g_o[...] = proj[:, 448:]
    links["feat"].receive()
    n.features[...] = n.feat_r_[0]
    links["down"].receive()
    down = total(n.down_r_, 16)
    n.g_gain[...] = down[:, 768:]
    lane = iota((16, 12), 1)
    twelve = zero_one(iota((16, 12), 0) == 8 * (lane // 6) + lane % 6)
    n.g_down[...] = dot_rows(down[:, :768].astype(BF16), twelve)
    links["last"].receive()
    lane = iota((192, 256), 1)
    tight = jnp.logical_and(iota((192, 256), 0) == 6 * (lane // 8) + lane % 8, lane % 8 < 6)
    tight = zero_one(tight)
    for j in range(8):
        piece = dot_cols(tight, n.last_r_[j].astype(BF16))
        n.g_up[192 * j : 192 * j + 192, :] = piece[:, :6]
    links["conv"].receive()
    conv = total(n.conv_r_, 16).astype(BF16)
    six = zero_one(iota((8, 6), 0) == iota((8, 6), 1))
    n.g_conv[:1280, :] = dot_rows(conv[:8], six)
    n.g_conv[1280:, :] = dot_rows(conv[8:, :1024], six)
    n.g_stem[...] = dot_rows(conv[8:, 1024:1088], six)
    for link in links.values():
        link.drain()


def per_device(
    base_codes,
    stem_weight,
    conv_weight,
    down_weight,
    norm_gain,
    query_weight,
    key_weight,
    value_weight,
    output_weight,
    up_weight,
    cotangent,
):
    vmem, anywhere = pl.BlockSpec(memory_space=pltpu.VMEM), pl.BlockSpec(memory_space=pl.ANY)
    stem = jnp.pad(stem_weight.reshape(60, 768), ((0, 68), (0, 0)))
    semaphores = [pltpu.SemaphoreType.DMA((len(WEIGHTS),))] + [pltpu.SemaphoreType.DMA((2,))] * 2
    for name, pattern in LINKS:
        slots = {x[0]: x[1] for x in SCRATCH}[name + "_r"][0]
        semaphores += [pltpu.SemaphoreType.DMA((pattern.count,)), pltpu.SemaphoreType.DMA((slots,))]
    features, g_stem, g_conv, g_down, g_gain, g_up, g_q, g_k, g_v, g_o = pl.pallas_call(
        kernel_body,
        out_shape=[jax.ShapeDtypeStruct(shape, dtype) for _, shape, dtype in OUTPUTS],
        in_specs=[vmem] * 4 + [anywhere] * 7,
        out_specs=[vmem] * len(OUTPUTS),
        scratch_shapes=[pltpu.VMEM(shape, dtype) for _, shape, dtype in SCRATCH] + semaphores,
        compiler_params=pltpu.CompilerParams(
            collective_id=0, has_side_effects=True, vmem_limit_bytes=60 * 1024 * 1024
        ),
        name="step",
    )(
        base_codes,
        cotangent[0],
        norm_gain.reshape(1, 1536),
        stem,
        conv_weight.reshape(2304, 768),
        down_weight,
        query_weight,
        key_weight,
        value_weight,
        output_weight,
        up_weight,
    )
    return (
        features[None],
        g_stem[:60].reshape(15, 4, 6),
        g_conv.reshape(3, 768, 6),
        g_down,
        jnp.concatenate([g_gain[:6, 0], g_gain[8:14, 0]]),
        g_up,
        g_q,
        g_k,
        g_v,
        g_o,
    )


def solution(mesh):
    placed = (
        P("batch", "seq"),
        P(),
        P(),
        P(),
        P(),
        P(None, "batch"),
        P(None, "batch"),
        P(None, "batch"),
        P("batch", None),
        P(),
        P("batch", "seq", None),
    )
    return jax.shard_map(
        per_device,
        mesh=mesh,
        in_specs=placed,
        out_specs=(
            P("batch", "seq", None),
            P(None, None, ("seq", "batch")),
            P(None, None, ("seq", "batch")),
            P(None, ("seq", "batch")),
            P(("seq", "batch")),
            P(None, ("seq", "batch")),
            P("seq", "batch"),
            P("seq", "batch"),
            P("seq", "batch"),
            P("seq", "batch"),
        ),
        check_vma=False,
    )
```

time: 1350 us -> 186 us (0.14)
  blocking collectives: 481 us -> 0 us
  starting transfers between devices: 295 us -> 0 us
  waiting for transfers between devices: 278 us -> 0 us
  Pallas kernels: 0 us -> 167 us
  local copies, waits for them, and re-layouts: 178 us -> 16.8 us
  matrix products: 74.5 us -> 0 us
  between operations: 17.1 us -> 0.7 us
  other arithmetic: 15.1 us -> 0.6 us
    unnamed x2 -> x0, blocking collectives: 438 us -> none
    unnamed x100 -> x0, starting transfers between devices: 259 us -> none
    all_gather x6 -> x0, waiting for transfers between devices: 241 us -> none  [the longest x1 53.3 us: per_device(): lax.all_gather(d_attended, 'seq', axis=1, tiled=True)]
    pallas_call x0 -> x1, Pallas kernels: none -> 167 us  [per_device(): pl.pallas_call(kernel_body, out_shape=[jax.ShapeDtypeStruct(shape, dtype)...]
    unnamed x251 -> x20, local copies, waits for them, and re-layouts: 158 us -> 12.2 us
    dot_general x30 -> x0, matrix products: 74.5 us -> none  [the longest x9 13.3 us: conv_block(): jnp.dot(shifted, weights[tap_index], preferred_element_type=jnp.float32)]
    all_gather x2 -> x0, blocking collectives: 42.9 us -> none  [the longest x1 21.5 us: per_device(): lax.all_gather(log_total, 'seq', axis=1, tiled=True)]
    ppermute x6 -> x0, starting transfers between devices: 35.1 us -> none  [the longest x3 21.1 us: with_halo(): lax.ppermute(lax.slice_in_dim(block, 0, width, axis=dim), axis, backward)]
  transfers between devices with their start and end apart: 115 -> 0, of which waited for: 12 -> 0; matrix products, arithmetic and copies ran while one was open for 45% -> 0% of each run, Pallas kernels for 0% -> 0%
where the time goes in v2:
time: 186 us; the launch traced here: 185 us
  Pallas kernels  167 us (90%)
  local copies, waits for them, and re-layouts  16.8 us (9%)
    pallas_call x1, Pallas kernels, per_device(): pl.pallas_call(kernel_body, out_shape=[jax.ShapeDtypeStruct(shape, dtype)...  167 us
    unnamed x20, local copies, waits for them, and re-layouts  12.2 us

profile of v2, /device:TPU:1, one launch (start us, length us, event | category | flops | bytes accessed | tf_op | source)
XLA Modules:
  0.0 185.4 jit_solution(18428298550072129116)
XLA Ops:
  0.6 1.3 reshape.35.refs_2_
  1.9 0.9 reshape.36
  2.9 0.7 pad.4.refs_3_
  3.5 2.3 %copy.26.refs_8_ = bf16[1536,192]{1,0:T(8,128)(2,1)} copy(bf16[1536,192]{0,1:T(8,128)(2,1)} %param.18) | data formatting | bytes 1179648 | tf_op args[7]
  5.8 167.2 %step.1 = (bf16[128,768]{1,0:T(8,128)(2,1)}, f32[64,6]{1,0:T(8,128)}, f32[2304,6]{1,0:T(8,128)}, f32[768,12]{1,0:T(8,128)}, f32[16,128]{1,0:T(8,128)}, /*index=5...) custom-call(s32[1,128]{1,0:T(1,128)} %refs_0_.1, ...), custom_call_target="tpu_custom_call" | custom-call | tf_op jit(solution)/shard_map/step/pallas_call | solution.py:674
  173.1 0.0 copy-start
  173.1 0.0 copy-start.4
  173.1 0.0 copy-start.3
  173.1 0.0 copy-start.2
  173.1 0.0 copy-start.1
  173.1 0.8 reshape.40
  174.0 0.7 copy.28
  174.7 0.8 slice_reduce_fusion.1
  175.5 0.6 pad_maximum_fusion
  176.1 1.8 copy.30
  177.9 2.0 %copy.31 = f32[1536,6]{0,1:T(8,128)} copy(f32[1536,6]{1,0:T(8,128)} %get-tuple-element.45) | data formatting | bytes 73728
  179.9 2.3 %copy.29 = f32[3,768,6]{1,2,0:T(8,128)} copy(f32[3,768,6]{2,1,0:T(8,128)} %bitcast.6) | data formatting | bytes 110592
  182.1 0.0 copy-done
  182.1 0.7 copy.39
  182.8 0.0 copy-done.4
  182.8 0.6 copy.40
  183.4 0.0 copy-done.3
  183.4 0.6 copy.41
  184.1 0.0 copy-done.2
  184.1 0.6 copy.42
  184.7 0.0 copy-done.1
  184.7 0.6 copy.43
Async XLA Ops:
  173.1 9.1 %copy-start = (bf16[128,768]{1,0:T(8,128)(2,1)S(1)}, bf16[128,768]{1,0:T(8,128)(2,1)}, u32[]{:S(2)}) copy-start(bf16[128,768]{1,0:T(8,128)(2,1)} %get-tuple-element.20) | copy-start | bytes 589828
  173.1 9.7 %copy-start.4 = (f32[96,128]{1,0:T(8,128)S(1)}, f32[96,128]{1,0:T(8,128)}, u32[]{:S(2)}) copy-start(f32[96,128]{1,0:T(8,128)} %get-tuple-element.68) | copy-start | bytes 147460
  173.1 10.4 %copy-start.3 = (f32[96,128]{1,0:T(8,128)S(1)}, f32[96,128]{1,0:T(8,128)}, u32[]{:S(2)}) copy-start(f32[96,128]{1,0:T(8,128)} %get-tuple-element.69) | copy-start | bytes 147460
  173.1 11.0 %copy-start.2 = (f32[96,192]{1,0:T(8,128)S(1)}, f32[96,192]{1,0:T(8,128)}, u32[]{:S(2)}) copy-start(f32[96,192]{1,0:T(8,128)} %get-tuple-element.70) | copy-start | bytes 221188
  173.1 11.6 %copy-start.1 = (f32[96,192]{1,0:T(8,128)S(1)}, f32[96,192]{1,0:T(8,128)}, u32[]{:S(2)}) copy-start(f32[96,192]{1,0:T(8,128)} %get-tuple-element.71) | copy-start | bytes 221188

commit v3 on v2

v3 whole, which is shorter than its diff:
```python
import functools
import math

import jax
import jax.numpy as jnp
from jax import lax
from jax.experimental import pallas as pl
from jax.experimental.pallas import tpu as pltpu
from jax.sharding import PartitionSpec as P

EPSILON = 1e-06
MESH = pl.DeviceIdType.MESH
F32 = jnp.float32
BF16 = jnp.bfloat16
SEQ = 16
BATCH = 8


class OverBatch:
    count = BATCH

    def dst(self, i, s, b):
        j = lax.rem(b + i, BATCH)
        return j, s, j, b

    def src(self, i, s, b):
        j = lax.rem(b + BATCH - i, BATCH)
        return j, s, j


class Share:
    count = BATCH

    def dst(self, i, s, b):
        return 0, s, lax.rem(b + i, BATCH), b

    def src(self, i, s, b):
        j = lax.rem(b + BATCH - i, BATCH)
        return j, s, j


class OverQuads:
    count = SEQ // 2

    def dst(self, i, s, b):
        j = lax.rem(s // 2 + i, SEQ // 2)
        return j, 2 * j + lax.rem(s, 2), b, s // 2

    def src(self, i, s, b):
        j = lax.rem(s // 2 + SEQ // 2 - i, SEQ // 2)
        return j, 2 * j + lax.rem(s, 2), b


class Core:
    count = 1

    def dst(self, i, s, b):
        other = 1 - lax.rem(s, 2)
        return other, s - lax.rem(s, 2) + other, b, 0

    def src(self, i, s, b):
        return 0, s + 1 - 2 * lax.rem(s, 2), b


class XBlocks:
    count = 8

    def dst(self, i, s, b):
        z, x = b // 4, lax.rem(b, 4)
        to, side = lax.rem(x + i // 2, 4), lax.rem(i, 2)
        return 4 * side + to, s, 4 * z + to, 2 * x + side

    def src(self, i, s, b):
        z, x = b // 4, lax.rem(b, 4)
        at, side = lax.rem(x + 4 - i // 2, 4), lax.rem(i, 2)
        return 2 * at + side, s, 4 * z + at


class ZBlocks:
    count = 4

    def dst(self, i, s, b):
        other = 1 - b // 4
        return 4 * other + i, s, 4 * other + lax.rem(b, 4), i

    def src(self, i, s, b):
        return i, s, 4 * (1 - b // 4) + lax.rem(b, 4)


class ZOne:
    count = 1

    def dst(self, i, s, b):
        return 0, s, 4 * (1 - b // 4) + lax.rem(b, 4), 0

    def src(self, i, s, b):
        return 0, s, 4 * (1 - b // 4) + lax.rem(b, 4)


class XOne:
    count = 4

    def dst(self, i, s, b):
        z, x = b // 4, lax.rem(b, 4)
        to = lax.rem(x + i, 4)
        return to, s, 4 * z + to, x

    def src(self, i, s, b):
        z, x = b // 4, lax.rem(b, 4)
        at = lax.rem(x + 4 - i, 4)
        return at, s, 4 * z + at


class Codes:
    count = 2 * BATCH

    def dst(self, i, s, b):
        return 0, 2 * b + lax.rem(i, 2), lax.rem(b + i // 2, BATCH), s

    def src(self, i, s, b):
        return i, i, s // 2


class ToBlock:
    count = 1

    def dst(self, i, s, b):
        return 0, 2 * b + s // BATCH, lax.rem(s, BATCH), 0

    def src(self, i, s, b):
        return 0, BATCH * lax.rem(s, 2) + b, s // 2


class ToOwner:
    count = 1

    def dst(self, i, s, b):
        return 0, BATCH * lax.rem(s, 2) + b, s // 2, 0

    def src(self, i, s, b):
        return 0, 2 * b + s // BATCH, lax.rem(s, BATCH)


class Link:
    def __init__(self, pattern, source, result, sends, receives, s, b):
        self.pattern, self.source, self.result = pattern, source, result
        self.sends, self.receives, self.s, self.b = sends, receives, s, b

    def copy(self, i):
        piece, target_s, target_b, slot = self.pattern.dst(i, self.s, self.b)
        away = jnp.logical_or(target_s != self.s, target_b != self.b)
        return away, pltpu.make_async_remote_copy(
            src_ref=self.source(piece),
            dst_ref=self.result.at[slot],
            send_sem=self.sends.at[i],
            recv_sem=self.receives.at[slot],
            device_id=(target_s, target_b),
            device_id_type=MESH,
        )

    def keep_one(self, i):
        piece, target_s, target_b, slot = self.pattern.dst(i, self.s, self.b)
        home = jnp.logical_and(target_s == self.s, target_b == self.b)

        @pl.when(home)
        def _():
            self.result[slot] = self.source(piece)[...]

    def each(self, action):
        loop(self.pattern.count, action)

    def start_one(self, i):
        away, copy = self.copy(i)
        pl.when(away)(copy.start)

    def keep(self):
        self.each(self.keep_one)

    def start(self):
        self.each(self.start_one)
        self.keep()

    def receive(self):
        def wait(i):
            slot, other_s, other_b = self.pattern.src(i, self.s, self.b)
            away = jnp.logical_or(other_s != self.s, other_b != self.b)
            copy = pltpu.make_async_remote_copy(
                src_ref=self.result.at[slot],
                dst_ref=self.result.at[slot],
                send_sem=self.sends.at[i],
                recv_sem=self.receives.at[slot],
                device_id=(other_s, other_b),
                device_id_type=MESH,
            )
            pl.when(away)(copy.wait_recv)

        self.each(wait)

    def drain(self):
        def wait(i):
            away, copy = self.copy(i)
            pl.when(away)(copy.wait_send)

        self.each(wait)


def dot(left, right):
    return jnp.dot(left, right, preferred_element_type=F32)


def dot_rows(left, right):
    return lax.dot_general(left, right, (((0,), (0,)), ((), ())), preferred_element_type=F32)


def dot_cols(left, right):
    return lax.dot_general(left, right, (((1,), (1,)), ((), ())), preferred_element_type=F32)


def iota(shape, dim):
    return lax.broadcasted_iota(jnp.int32, shape, dim)


def zero_one(mask):
    return jnp.where(mask, 1.0, 0.0).astype(BF16)


def gelu_grad(x):
    inner = math.sqrt(2.0 / math.pi) * (x + 0.044715 * x * x * x)
    t = jnp.tanh(inner)
    slope = math.sqrt(2.0 / math.pi) * (1.0 + 3 * 0.044715 * x * x)
    return 0.5 * (1.0 + t) + 0.5 * x * (1.0 - t * t) * slope


def total(ref, count):
    value = ref[0].astype(F32)
    for j in range(1, count):
        value = value + ref[j].astype(F32)
    return value


def loop(count, step):
    def body(i, carry):
        step(i)
        return carry

    lax.fori_loop(0, count, body, 0)


def rows_of(i, size):
    return pl.ds(pl.multiple_of(i * size, size), size)


INPUTS = dict(codes=0, cot=0, gain=0, stem=0, conv_h=0, down_h=0, q_h=0, k_h=0, v_h=0, o_h=0, up_h=0)
OUTPUTS = dict(
    features=((128, 768), BF16),
    g_stem=((6, 4, 15), F32),
    g_conv=((3, 6, 768), F32),
    g_down=((12, 768), F32),
    g_gain=((1, 128), F32),
    g_up=((6, 1536), F32),
    g_q=((96, 128), F32),
    g_k=((96, 128), F32),
    g_v=((96, 192), F32),
    g_o=((96, 192), F32),
)
SCRATCH = dict(
    conv_w=((2304, 768), BF16),
    down_w=((768, 1536), BF16),
    in_w=((1536, 512), BF16),
    in_t=((512, 1536), BF16),
    o_w=((256, 1536), BF16),
    o_t=((1536, 256), BF16),
    up_w=((1536, 768), BF16),
    stem_f=((64, 768), F32),
    stem_w=((128, 768), BF16),
    select=((768, 1024), BF16),
    select_conv=((768, 1024), BF16),
    select_down=((768, 1024), BF16),
    codes_s=((1, 8, 128), F32),
    codes_r=((16, 8, 128), F32),
    blk_s=((1, 128, 768), BF16),
    blk_r=((1, 128, 768), BF16),
    low_s=((1, 64, 768), BF16),
    low_r=((8, 64, 768), BF16),
    code=((2, 640, 128), F32),
    picked=((2, 528, 128), F32),
    emb=((8, 128, 2304), BF16),
    conv=((128, 768), F32),
    tower=((128, 768), BF16),
    pooled=((512, 768), BF16),
    lifted=((512, 1536), BF16),
    factor=((512, 128), F32),
    normed=((512, 1536), BF16),
    qkv=((512, 512), BF16),
    kv_far=((512, 384), BF16),
    d_mixed=((512, 1536), BF16),
    d_att=((512, 256), BF16),
    att=((512, 256), BF16),
    dqkv=((512, 512), BF16),
    dkv_own=((512, 384), F32),
    dkv_far=((512, 384), F32),
    dkv_s=((512, 384), BF16),
    dkv_r=((512, 384), BF16),
    low_sel=((512, 1024), BF16),
    conv_acc=((128, 2304), F32),
    mixedA_s=((8, 64, 768), BF16),
    mixedA_r=((8, 64, 768), BF16),
    mixedB_s=((8, 64, 768), BF16),
    mixedB_r=((4, 64, 768), BF16),
    mixedC_s=((1, 64, 768), BF16),
    mixedC_r=((1, 64, 768), BF16),
    mixedD_s=((4, 64, 768), BF16),
    mixedD_r=((4, 64, 768), BF16),
    dnA_s=((8, 64, 768), BF16),
    dnA_r=((8, 64, 768), BF16),
    dnB_s=((8, 64, 768), BF16),
    dnB_r=((4, 64, 768), BF16),
    dnC_s=((1, 64, 768), BF16),
    dnC_r=((1, 64, 768), BF16),
    dnD_s=((4, 64, 768), BF16),
    dnD_r=((4, 64, 768), BF16),
    feat_s=((1, 128, 768), BF16),
    feat_r=((1, 128, 768), BF16),
    upd_s=((8, 64, 256), BF16),
    upd_r=((8, 64, 256), BF16),
    dl_s=((8, 64, 256), BF16),
    dl_r=((8, 64, 256), BF16),
    gain_s=((8, 8, 256), F32),
    gain_r=((8, 8, 256), F32),
    dc_s=((8, 128, 128), BF16),
    dc_r=((8, 128, 128), BF16),
    ds_s=((8, 64, 128), BF16),
    ds_r=((8, 64, 128), BF16),
    proj_c_s=((8, 2, 96, 640), BF16),
    proj_c_r=((1, 8, 96, 640), BF16),
    proj_s=((8, 96, 640), BF16),
    proj_r=((8, 96, 640), BF16),
    up_c_s=((8, 2, 64, 256), BF16),
    up_c_r=((1, 8, 64, 256), BF16),
    up_s=((8, 64, 256), BF16),
    up_r=((8, 64, 256), BF16),
    down_c_s=((8, 2, 16, 896), BF16),
    down_c_r=((1, 8, 16, 896), BF16),
    down_s=((8, 16, 896), BF16),
    down_r=((8, 16, 896), BF16),
    conv_c_s=((8, 2, 16, 1280), BF16),
    conv_c_r=((1, 8, 16, 1280), BF16),
    conv_s=((8, 16, 1280), BF16),
    conv_r=((8, 16, 1280), BF16),
    last_s=((8, 8, 256), F32),
    last_r=((8, 8, 256), F32),
)
LINKS = dict(
    codes=Codes(),
    blk=ToBlock(),
    low=Share(),
    mixedA=XBlocks(),
    mixedB=ZBlocks(),
    mixedC=ZOne(),
    mixedD=XOne(),
    dnA=XBlocks(),
    dnB=ZBlocks(),
    dnC=ZOne(),
    dnD=XOne(),
    feat=ToOwner(),
    upd=OverBatch(),
    dl=OverBatch(),
    gain=OverBatch(),
    dc=OverBatch(),
    ds=OverBatch(),
    proj_c=Core(),
    proj=OverQuads(),
    up_c=Core(),
    up=OverQuads(),
    down_c=Core(),
    down=OverQuads(),
    conv_c=Core(),
    conv=OverQuads(),
    last=OverBatch(),
)


class Namespace:
    pass


def kernel_body(*refs):
    names = list(INPUTS) + list(OUTPUTS) + [x + "_" for x in SCRATCH]
    n = Namespace()
    for name, ref in zip(names, refs):
        setattr(n, name, ref)
    semaphores = refs[len(names) :]
    weight_sems, swap_send, swap_recv = semaphores[:3]
    s, b = lax.axis_index("seq"), lax.axis_index("batch")
    h = lax.rem(s, 2)
    z = b // 4
    peer = (s + 1 - 2 * h, b)
    links = Namespace()
    for k, (name, pattern) in enumerate(LINKS.items()):
        sent = getattr(n, name + "_s_")
        if name.endswith("_c"):
            source = lambda piece, sent=sent: sent.at[:, piece]
        else:
            source = lambda piece, sent=sent: sent.at[piece]
        result = getattr(n, name + "_r_")
        link = Link(pattern, source, result, semaphores[3 + 2 * k], semaphores[4 + 2 * k], s, b)
        setattr(links, name, link)

    barrier = pltpu.get_barrier_semaphore()
    for link in (links.codes, links.low, links.proj, links.up_c, links.feat):
        pattern = link.pattern

        def greet(i, pattern=pattern):
            _, other_s, other_b = pattern.src(i, s, b)

            @pl.when(jnp.logical_or(other_s != s, other_b != b))
            def _():
                pl.semaphore_signal(
                    barrier, inc=1, device_id=(other_s, other_b), device_id_type=MESH
                )

        loop(pattern.count, greet)
    own_window = (b == s // 2).astype(jnp.int32)
    own_block = own_window * (s == BATCH * h + b).astype(jnp.int32)
    expected = 16 + 7 + 7 + 1 + 1 - own_window - own_block

    weights = [
        pltpu.make_async_copy(source, target, weight_sems.at[k])
        for k, (source, target) in enumerate(
            [
                (n.q_h, n.in_w_.at[:, pl.ds(0, 128)]),
                (n.k_h, n.in_w_.at[:, pl.ds(128, 128)]),
                (n.v_h, n.in_t_.at[pl.ds(256, 192)]),
                (n.o_h, n.o_w_.at[pl.ds(0, 192)]),
                (n.conv_h, n.conv_w_),
                (n.down_h, n.down_w_),
                (n.up_h, n.up_w_),
            ]
        )
    ]
    for copy in weights:
        copy.start()

    row, column = iota((128, 128), 0), iota((128, 128), 1)
    order = zero_one(column == jnp.where(row < 64, 2 * row, 2 * row - 127))
    codes = jnp.broadcast_to((n.codes[...] + 1).astype(F32), (8, 128)).astype(BF16)
    n.codes_s_[0] = dot_cols(codes, order)
    n.blk_s_[0] = dot(order, n.cot[...]).astype(BF16)

    pl.semaphore_wait(barrier, expected)
    links.codes.start()
    links.blk.start()

    def fill(c):
        within = iota((1, 128), 1)
        i, m = lax.rem(within, 8), within // 8
        good = i < 6
        rows = iota((768, 128), 0)
        place = rows_of(c, 128)
        n.select_[:, place] = zero_one(rows == jnp.where(good, 6 * (m + 16 * c) + i, -1))
        n.select_conv_[:, place] = zero_one(rows == jnp.where(good, 6 * (8 * m + c) + i, -1))
        wanted = 12 * (8 * (m // 2) + c) + 6 * lax.rem(m, 2) + i
        n.select_down_[:, place] = zero_one(rows == jnp.where(good, wanted, -1))

    loop(8, fill)
    for t in range(15):
        n.stem_f_[4 * t : 4 * t + 4, :] = n.stem[t].astype(F32)
    n.stem_f_[60:, :] = jnp.zeros((4, 768), F32)
    n.stem_w_[:64, :] = n.stem_f_[...].astype(BF16)
    n.stem_w_[64:, :] = jnp.zeros((64, 768), BF16)
    for copy in weights[:4]:
        copy.wait()
    n.o_w_[192:, :] = jnp.zeros((64, 1536), BF16)
    n.in_t_[448:, :] = jnp.zeros((64, 1536), BF16)
    eye, eye2 = zero_one(row == column), zero_one(iota((256, 256), 0) == iota((256, 256), 1))
    n.in_t_[:128, :] = dot_cols(eye, n.in_w_[:, :128]).astype(BF16)
    n.in_t_[128:256, :] = dot_cols(eye, n.in_w_[:, 128:256]).astype(BF16)
    n.in_w_[:, 256:] = dot_rows(n.in_t_[256:, :], eye2).astype(BF16)
    n.o_t_[...] = dot_rows(n.o_w_[...], eye2).astype(BF16)

    links.codes.receive()
    ones = jnp.ones((128, 128), BF16)
    for i in range(10):
        place = BATCH * h + (i - 1)
        inside = jnp.logical_and(place >= 0, place < 16)
        line = n.codes_r_[jnp.clip(place, 0, 15)][0:1]
        line = jnp.where(inside, line, 0.0)
        spread = dot(jnp.where(row == column, line, 0.0).astype(BF16), ones)
        n.code_[0, 64 * i : 64 * i + 64] = spread[:64]
        n.code_[1, 64 * i : 64 * i + 64] = spread[64:]
    lane_tap = iota((1, 128), 1) // 4
    lane_code = (iota((1, 128), 1) % 4 + 1).astype(F32)
    for parity in range(2):
        picked = jnp.zeros((528, 128), F32)
        for tap in range(15):
            offset = parity + tap - 7
            stream, shift = offset % 2, (offset - offset % 2) // 2
            begin = 56 + shift
            picked = jnp.where(lane_tap == tap, n.code_[stream, begin : begin + 528, :], picked)
        where = iota((528, 128), 0) - 8 + 512 * h
        inside = jnp.logical_and(where >= 0, where < 1024)
        n.picked_[parity] = jnp.where(inside, picked, 0.0)

    links.blk.receive()
    pairs = n.blk_r_[0].astype(F32)
    n.low_s_[0] = (pairs[:64] + pairs[64:]).astype(BF16)
    links.low.start()

    def one_hots(j):
        found = []
        for parity in range(2):
            near = n.picked_[parity, pl.ds(pl.multiple_of(64 * j, 64), 80), :]
            for step in (-4, 0, 4):
                found.append(zero_one(near[8 + step : 72 + step] == lane_code))
        return found

    def embed(j):
        value = dot(jnp.concatenate(one_hots(j), axis=0), n.stem_w_[...]).astype(BF16)
        for parity in range(2):
            for step in range(3):
                begin = 64 * (3 * parity + step)
                n.emb_[j, 64 * parity : 64 * parity + 64, 768 * step : 768 * step + 768] = value[
                    begin : begin + 64
                ]

    loop(8, embed)
    for copy in weights[4:]:
        copy.wait()
    gain = n.gain[...].reshape(1, 1536)

    def forward(t):
        pair = pl.ds(2 * t, 2)
        here = rows_of(t, 128)
        conv = dot(n.emb_[pair].reshape(256, 2304), n.conv_w_[...])
        center = n.emb_[pair, :, 768:1536].reshape(256, 768).astype(F32)
        tower = (center + jax.nn.gelu(conv)).astype(BF16)
        halves = tower.astype(F32).reshape(2, 2, 64, 768)
        pooled = (0.5 * (halves[:, 0] + halves[:, 1])).astype(BF16).reshape(128, 768)
        n.pooled_[here, :] = pooled
        lifted = dot(pooled, n.down_w_[...]).astype(BF16)
        n.lifted_[here, :] = lifted
        lifted = lifted.astype(F32)
        factor = lax.rsqrt(jnp.mean(lifted * lifted, axis=-1, keepdims=True) + EPSILON)
        n.factor_[here, :] = jnp.broadcast_to(factor, (128, 128))
        normed = (lifted * factor * gain).astype(BF16)
        n.normed_[here, :] = normed
        n.qkv_[here, :] = dot(normed, n.in_w_[...]).astype(BF16)

    loop(4, forward)
    swap = pltpu.make_async_remote_copy(
        src_ref=n.qkv_.at[:, pl.ds(128, 384)], dst_ref=n.kv_far_,
        send_sem=swap_send.at[0], recv_sem=swap_recv.at[0], device_id=peer, device_id_type=MESH,
    )
    swap.start()
    links.low.receive()

    def cotangent_of_mixed(c):
        low = n.low_r_[...].reshape(512, 768)
        chunk = rows_of(c, 256)
        n.d_mixed_[:, chunk] = dot_cols(low, n.up_w_[chunk, :]).astype(BF16)

    loop(6, cotangent_of_mixed)
    n.d_att_[...] = dot(n.d_mixed_[...], n.o_t_[...]).astype(BF16)
    n.dkv_own_[...] = jnp.zeros((512, 384), F32)
    n.dkv_far_[...] = jnp.zeros((512, 384), F32)
    swap.wait()

    scale = 1.0 / math.sqrt(128)

    def send_pair(name, t, value):
        half = value.astype(BF16)
        getattr(n, name + "A_s_")[pl.ds(2 * t, 2)] = half[:, :768].reshape(2, 64, 768)
        getattr(n, name + "B_s_")[pl.ds(2 * t, 2)] = half[:, 768:].reshape(2, 64, 768)
        for j in (2 * t, 2 * t + 1):
            to, side = lax.rem(j, 4), j // 4
            getattr(links, name + "A").start_one(2 * lax.rem(to - lax.rem(b, 4) + 4, 4) + side)

            @pl.when(side != z)
            def _():
                getattr(links, name + "B").start_one(to)

    def attend(t):
        here = rows_of(t, 128)
        q, da = n.qkv_[here, :128], n.d_att_[here, :]
        blocks = (
            (n.qkv_[:, 128:256], n.qkv_[:, 256:], n.dkv_own_),
            (n.kv_far_[:, :128], n.kv_far_[:, 128:], n.dkv_far_),
        )
        scores = [dot_cols(q, k) * scale for k, _, _ in blocks]
        sums = sum(jnp.sum(jnp.exp(x), axis=1, keepdims=True) for x in scores)
        log_total = jnp.log(sums)
        probs = [jnp.exp(x - log_total) for x in scores]
        dprobs = [dot_cols(da, v) for _, v, _ in blocks]
        inner = sum(jnp.sum(p * d, axis=1, keepdims=True) for p, d in zip(probs, dprobs))
        att = jnp.zeros((128, 256), F32)
        dq = jnp.zeros((128, 128), F32)
        for (k, v, total_ref), p, d in zip(blocks, probs, dprobs):
            ds = (p * (d - inner)).astype(BF16)
            pb = p.astype(BF16)
            att = att + dot(pb, v)
            dq = dq + dot(ds, k)
            total_ref[:, :128] += dot_rows(ds, q) * scale
            total_ref[:, 128:] += dot_rows(pb, da)
        att = att.astype(BF16)
        n.att_[here, :] = att
        n.dqkv_[here, :128] = (dq * scale).astype(BF16)
        send_pair("mixed", t, dot(att, n.o_w_[...]))

    loop(4, attend)
    n.dkv_s_[...] = n.dkv_far_[...].astype(BF16)
    swap_back = pltpu.make_async_remote_copy(
        src_ref=n.dkv_s_, dst_ref=n.dkv_r_, send_sem=swap_send.at[1], recv_sem=swap_recv.at[1],
        device_id=peer, device_id_type=MESH,
    )
    swap_back.start()
    swap_back.wait()
    n.dqkv_[:, 128:] = (n.dkv_own_[...] + n.dkv_r_[...].astype(F32)).astype(BF16)

    def back_through_projections(t):
        send_pair("dn", t, dot(n.dqkv_[rows_of(t, 128), :], n.in_t_[...]))

    loop(4, back_through_projections)

    def first_hop(name):
        over_x, over_z = getattr(links, name + "A"), getattr(links, name + "B")
        over_x.keep()
        over_x.receive()
        there = 1 - z
        value = over_x.result[there].astype(F32)
        for j in range(1, 4):
            value = value + over_x.result[2 * j + there].astype(F32)
        getattr(n, name + "C_s_")[0] = value.astype(BF16)
        getattr(links, name + "C").start()
        over_z.receive()
        value = getattr(n, name + "B_s_")[pl.ds(4 * z, 4)].astype(F32)
        value = value + over_z.result[...].astype(F32)
        getattr(n, name + "D_s_")[...] = value.astype(BF16)
        getattr(links, name + "D").start()

    def second_hop(name):
        getattr(links, name + "C").receive()
        left = getattr(links, name + "C").result[0].astype(F32)
        for j in range(4):
            left = left + getattr(links, name + "A").result[2 * j + z].astype(F32)
        getattr(links, name + "D").receive()
        return jnp.concatenate([left, total(getattr(links, name + "D").result, 4)], axis=1)

    first_hop("mixed")

    def projection_grads(c):
        chunk = rows_of(c, 384)
        first = dot_rows(n.normed_[:, chunk], n.dqkv_[...]).astype(BF16)
        second = dot_rows(n.d_mixed_[:, chunk], n.att_[...]).astype(BF16)
        both = jnp.concatenate([first[:, :448], second[:, :192]], axis=1)
        n.proj_c_s_[pl.ds(2 * c, 2)] = both.reshape(2, 2, 96, 640)

    loop(4, projection_grads)
    links.proj_c.start()

    here = rows_of(b, 64)
    n.conv_[...] = dot(n.emb_[b], n.conv_w_[...])
    center = n.emb_[b, :, 768:1536].astype(F32)
    n.tower_[...] = (center + jax.nn.gelu(n.conv_[...])).astype(BF16)
    lifted = n.lifted_[here, :].astype(F32)
    factor = n.factor_[here, 0:1]
    first_hop("dn")
    updated = (lifted + second_hop("mixed")).astype(BF16)

    def select_into(target, value, matrix):
        for half in range(2):
            moved = dot(value[:, 768 * half : 768 * half + 768], matrix[...]).astype(BF16)
            for j in range(4):
                target[4 * half + j] = moved[:, 256 * j : 256 * j + 256]

    select_into(n.upd_s_, updated, n.select_)
    lowered = dot(updated, n.up_w_[...])
    features = n.tower_[...].astype(F32) + jnp.concatenate([lowered, lowered], axis=0)
    n.feat_s_[0] = dot_rows(order, features.astype(BF16)).astype(BF16)
    links.feat.start()

    def core_sum(name):
        getattr(links, name + "_c").receive()
        mine = getattr(n, name + "_c_s_")
        far = getattr(n, name + "_c_r_")
        target = getattr(n, name + "_s_")

        def add(j):
            target[j] = (mine[j, h].astype(F32) + far[0, j].astype(F32)).astype(BF16)

        loop(8, add)
        getattr(links, name).start()

    d_normed = second_hop("dn").astype(BF16).astype(F32)
    d_updated = n.d_mixed_[here, :].astype(F32)
    gained = d_normed * gain
    shared = jnp.mean(gained * lifted, axis=-1, keepdims=True) * (factor * factor * factor)
    d_lifted = (gained * factor - lifted * shared).astype(BF16).astype(F32) + d_updated
    d_lifted = d_lifted.astype(BF16)
    for half in range(2):
        moved = dot(d_lifted[:, 768 * half : 768 * half + 768], n.select_down_[...]).astype(BF16)
        for j in range(8):
            n.dl_s_[j, :, 128 * half : 128 * half + 128] = moved[:, 128 * j : 128 * j + 128]
    links.dl.start()
    d_pooled = dot_cols(d_lifted, n.down_w_[...]) * 0.5
    d_tower = n.blk_r_[0].astype(F32) + jnp.concatenate([d_pooled, d_pooled], axis=0)
    d_tower = d_tower.astype(BF16)
    d_conv = (d_tower.astype(F32) * gelu_grad(n.conv_[...])).astype(BF16)
    moved = dot(d_conv, n.select_conv_[...]).astype(BF16)
    for j in range(8):
        n.dc_s_[j] = moved[:, 128 * j : 128 * j + 128]
    links.dc.start()
    links.upd.start()
    hots = one_hots(b)
    d_stem = jnp.zeros((128, 768), F32)
    for step in range(3):
        d_emb = dot_cols(d_conv, n.conv_w_[768 * step : 768 * step + 768, :])
        if step == 1:
            d_emb = d_emb + d_tower.astype(F32)
        hot = jnp.concatenate([hots[step], hots[3 + step]], axis=0)
        d_stem = d_stem + dot_rows(hot, d_emb.astype(BF16))
    moved = dot(d_stem[:64].astype(BF16), n.select_conv_[...]).astype(BF16)
    for j in range(8):
        n.ds_s_[j] = moved[:, 128 * j : 128 * j + 128]
    links.ds.start()
    d_gain = jnp.sum(d_normed * (lifted * factor), axis=0, keepdims=True).astype(BF16)
    d_gain = jnp.broadcast_to(d_gain, (16, 1536))
    for half in range(2):
        moved = dot(d_gain[:, 768 * half : 768 * half + 768], n.select_down_[...])
        for j in range(8):
            n.gain_s_[j, :, 128 * half : 128 * half + 128] = moved[:8, 128 * j : 128 * j + 128]
    links.gain.start()
    core_sum("proj")

    def select_low(t):
        rows = rows_of(t, 128)
        low = n.low_r_[pl.ds(2 * t, 2)].reshape(128, 768)
        n.low_sel_[rows, :] = dot(low, n.select_[...]).astype(BF16)

    loop(4, select_low)

    links.dl.receive()
    down = dot_rows(n.dl_r_[...].reshape(512, 256), n.pooled_[...]).astype(BF16)
    n.down_c_s_[:, :, :, :768] = down.reshape(8, 2, 16, 768)
    links.gain.receive()
    first_row = jnp.logical_and(iota((64, 128), 0) % 8 == 0, iota((64, 128), 1) == 0)
    gains = dot_rows(n.gain_r_[...].reshape(64, 256).astype(BF16), zero_one(first_row)).astype(BF16)
    n.down_c_s_[:, :, :, 768:] = gains.reshape(8, 2, 16, 128)
    links.down_c.start()
    n.conv_acc_[...] = jnp.zeros((128, 2304), F32)
    links.dc.receive()

    def conv_grads(t):
        pair = pl.ds(2 * t, 2)
        left = n.dc_r_[pair].reshape(256, 128)
        n.conv_acc_[...] += dot_rows(left, n.emb_[pair].reshape(256, 2304))

    loop(4, conv_grads)
    core_sum("down")
    links.ds.receive()
    same = zero_one(iota((512, 128), 0) % 64 == iota((512, 128), 1))
    stem = dot_rows(n.ds_r_[...].reshape(512, 128), same)
    n.conv_c_s_[:, :, 0:8, :] = n.conv_acc_[:, :1280].reshape(8, 2, 8, 1280).astype(BF16)
    rest = jnp.concatenate([n.conv_acc_[:, 1280:], stem, jnp.zeros((128, 128), F32)], axis=1)
    n.conv_c_s_[:, :, 8:16, :] = rest.reshape(8, 2, 8, 1280).astype(BF16)
    links.conv_c.start()
    links.upd.receive()
    up = dot_rows(n.low_sel_[...], n.upd_r_[...].reshape(512, 256)).astype(BF16)
    n.up_c_s_[...] = up.reshape(8, 2, 64, 256)
    links.up_c.start()
    core_sum("conv")
    core_sum("up")

    links.proj.receive()
    proj = total(n.proj_r_, 8)
    n.g_q[...] = proj[:, :128]
    n.g_k[...] = proj[:, 128:256]
    n.g_v[...] = proj[:, 256:448]
    n.g_o[...] = proj[:, 448:]
    links.feat.receive()
    n.features[...] = n.feat_r_[0]
    links.down.receive()
    down = total(n.down_r_, 8)
    n.g_down[0:6, :] = down[0:6, :768]
    n.g_down[6:12, :] = down[8:14, :768]
    lane = iota((16, 128), 1)
    wanted = jnp.where(lane < 6, lane, lane + 2)
    hit = jnp.logical_and(iota((16, 128), 0) == wanted, lane < 12)
    n.g_gain[...] = jnp.sum(jnp.where(hit, down[:, 768:769], 0.0), axis=0, keepdims=True)
    links.up.receive()
    n.last_s_[...] = total(n.up_r_, 8).reshape(8, 8, 256)
    links.last.start()
    links.conv.receive()
    conv = total(n.conv_r_, 8)
    n.g_conv[0] = conv[0:6, :768]
    n.g_conv[1] = jnp.concatenate([conv[0:6, 768:], conv[8:14, :256]], axis=1)
    n.g_conv[2] = conv[8:14, 256:1024]
    stem = conv[8:16, 1024:1152].astype(BF16)
    for code in range(4):
        taps = iota((128, 15), 0) == 4 * iota((128, 15), 1) + code
        n.g_stem[:, code, :] = dot(stem, zero_one(taps))[:6]
    lane = iota((192, 256), 1)
    tight = jnp.logical_and(iota((192, 256), 0) == 6 * (lane // 8) + lane % 8, lane % 8 < 6)
    tight = zero_one(tight)
    links.last.receive()
    for j in range(4):
        pieces = [dot_cols(n.last_r_[2 * j + k].astype(BF16), tight) for k in range(2)]
        n.g_up[:, 384 * j : 384 * j + 384] = jnp.concatenate(pieces, axis=1)[:6]
    for link in vars(links).values():
        link.drain()


def finish_body(*refs):
    number = len(OUTPUTS)
    copies = [
        pltpu.make_async_copy(source, target, refs[-1].at[k])
        for k, (source, target) in enumerate(zip(refs[:number], refs[number : 2 * number]))
    ]
    for copy in copies:
        copy.start()
    for copy in copies:
        copy.wait()


def per_device(
    base_codes,
    stem_weight,
    conv_weight,
    down_weight,
    norm_gain,
    query_weight,
    key_weight,
    value_weight,
    output_weight,
    up_weight,
    cotangent,
):
    vmem, anywhere = pl.BlockSpec(memory_space=pltpu.VMEM), pl.BlockSpec(memory_space=pl.ANY)
    semaphores = [pltpu.SemaphoreType.DMA((7,))] + [pltpu.SemaphoreType.DMA((2,))] * 2
    shapes = {name: x[0] for name, x in SCRATCH.items()}
    for name, pattern in LINKS.items():
        semaphores += [
            pltpu.SemaphoreType.DMA((pattern.count,)),
            pltpu.SemaphoreType.DMA((shapes[name + "_r"][0],)),
        ]
    out_shape = [jax.ShapeDtypeStruct(shape, dtype) for shape, dtype in OUTPUTS.values()]
    results = pl.pallas_call(
        kernel_body,
        out_shape=out_shape,
        in_specs=[vmem] * 4 + [anywhere] * 7,
        out_specs=[vmem] * len(OUTPUTS),
        scratch_shapes=[pltpu.VMEM(shape, dtype) for shape, dtype in SCRATCH.values()] + semaphores,
        compiler_params=pltpu.CompilerParams(
            collective_id=0, has_side_effects=True, vmem_limit_bytes=60 * 1024 * 1024
        ),
        name="step",
    )(
        base_codes,
        cotangent[0],
        norm_gain,
        stem_weight,
        conv_weight.reshape(2304, 768),
        down_weight,
        query_weight,
        key_weight,
        value_weight.T,
        output_weight,
        up_weight,
    )
    features, g_stem, g_conv, g_down, g_gain, g_up, g_q, g_k, g_v, g_o = pl.pallas_call(
        finish_body,
        out_shape=out_shape,
        in_specs=[anywhere] * len(OUTPUTS),
        out_specs=[anywhere] * len(OUTPUTS),
        scratch_shapes=[pltpu.SemaphoreType.DMA((len(OUTPUTS),))],
        name="finish",
    )(*results)
    return (
        features[None],
        g_stem.transpose(2, 1, 0),
        g_conv.transpose(0, 2, 1),
        g_down.T,
        g_gain[0, :12],
        g_up.T,
        g_q,
        g_k,
        g_v,
        g_o,
    )


def solution(mesh):
    placed = (
        P("batch", "seq"),
        P(),
        P(),
        P(),
        P(),
        P(None, "batch"),
        P(None, "batch"),
        P(None, "batch"),
        P("batch", None),
        P(),
        P("batch", "seq", None),
    )
    return jax.shard_map(
        per_device,
        mesh=mesh,
        in_specs=placed,
        out_specs=(
            P("batch", "seq", None),
            P(None, None, ("seq", "batch")),
            P(None, None, ("seq", "batch")),
            P(None, ("seq", "batch")),
            P(("seq", "batch")),
            P(None, ("seq", "batch")),
            P("seq", "batch"),
            P("seq", "batch"),
            P("seq", "batch"),
            P("seq", "batch"),
        ),
        check_vma=False,
    )
```

time: 186 us -> 149 us (0.80); the launches traced: 185 us -> 146 us
  Pallas kernels: 167 us -> 144 us
  local copies, waits for them, and re-layouts: 16.8 us -> 1.12 us
    pallas_call x1 -> x2, Pallas kernels: 167 us -> 144 us  [the longest x1 123 us: per_device(): pl.pallas_call(kernel_body, out_shape=out_shape, in_specs=[vmem] * 4 + [a...]
    unnamed x20 -> x0, local copies, waits for them, and re-layouts: 12.2 us -> none
    reshape x3 -> x0, local copies, waits for them, and re-layouts: 3.05 us -> none  [the longest x1 1.3 us: per_device(): norm_gain.reshape(1, 1536)]
where the time goes in v3:
time: 149 us; the launch traced here: 146 us
  Pallas kernels  144 us (97%)
    pallas_call x1, Pallas kernels, per_device(): pl.pallas_call(kernel_body, out_shape=out_shape, in_specs=[vmem] * 4 + [a...  123 us
    pallas_call x1, Pallas kernels, per_device(): pl.pallas_call(finish_body, out_shape=out_shape, in_specs=[anywhere] * le...  21.7 us

profile of v3, /device:TPU:1, one launch (start us, length us, event | category | flops | bytes accessed | tf_op | source)
XLA Modules:
  0.0 146.1 jit_solution(16667287926895201862)
XLA Ops:
  0.6 122.6 %step.1 = (bf16[128,768]{1,0:T(8,128)(2,1)}, f32[6,4,15]{2,1,0:T(4,128)}, f32[3,6,768]{2,1,0:T(8,128)}, f32[12,768]{1,0:T(8,128)}, f32[1,128]{1,0:T(1,128)}, /*i...) custom-call(s32[1,128]{1,0:T(1,128)} %refs_0_.1, ...), custom_call_target="tpu_custom_call" | custom-call | tf_op jit(solution)/shard_map/step/pallas_call | solution.py:846
  123.3 21.7 %finish.1 = (bf16[128,768]{1,0:T(8,128)(2,1)}, f32[6,4,15]{2,1,0:T(4,128)}, f32[3,6,768]{2,1,0:T(8,128)}, f32[12,768]{1,0:T(8,128)}, f32[1,128]{1,0:T(1,128)}, /...) custom-call(bf16[128,768]{1,0:T(8,128)(2,1)} %get-tuple-element.30.refs_, ...), custom_call_target="tpu_custom_call" | custom-call | tf_op jit(solution)/shard_map/finish/pallas_call | solution.py:869
  145.0 1.1 slice_bitcast_fusion

commit v4 on v3

--- a/solution.py
+++ b/solution.py
@@ -45,6 +45,18 @@
     def dst(self, i, s, b):
         j = lax.rem(s // 2 + i, SEQ // 2)
         return j, 2 * j + lax.rem(s, 2), b, s // 2
+
+    def src(self, i, s, b):
+        j = lax.rem(s // 2 + SEQ // 2 - i, SEQ // 2)
+        return j, 2 * j + lax.rem(s, 2), b
+
+
+class QuadShare:
+    count = SEQ // 2
+
+    def dst(self, i, s, b):
+        j = lax.rem(s // 2 + i, SEQ // 2)
+        return 0, 2 * j + lax.rem(s, 2), b, s // 2
 
     def src(self, i, s, b):
         j = lax.rem(s // 2 + SEQ // 2 - i, SEQ // 2)
@@ -273,7 +285,6 @@
     up_w=((1536, 768), BF16),
     stem_f=((64, 768), F32),
     stem_w=((128, 768), BF16),
-    select=((768, 1024), BF16),
     select_conv=((768, 1024), BF16),
     select_down=((768, 1024), BF16),
     codes_s=((1, 8, 128), F32),
@@ -301,82 +312,87 @@
     dkv_far=((512, 384), F32),
     dkv_s=((512, 384), BF16),
     dkv_r=((512, 384), BF16),
-    low_sel=((512, 1024), BF16),
     conv_acc=((128, 2304), F32),
-    mixedA_s=((8, 64, 768), BF16),
-    mixedA_r=((8, 64, 768), BF16),
-    mixedB_s=((8, 64, 768), BF16),
-    mixedB_r=((4, 64, 768), BF16),
-    mixedC_s=((1, 64, 768), BF16),
-    mixedC_r=((1, 64, 768), BF16),
-    mixedD_s=((4, 64, 768), BF16),
-    mixedD_r=((4, 64, 768), BF16),
-    dnA_s=((8, 64, 768), BF16),
-    dnA_r=((8, 64, 768), BF16),
-    dnB_s=((8, 64, 768), BF16),
-    dnB_r=((4, 64, 768), BF16),
-    dnC_s=((1, 64, 768), BF16),
-    dnC_r=((1, 64, 768), BF16),
-    dnD_s=((4, 64, 768), BF16),
-    dnD_r=((4, 64, 768), BF16),
+    w_up=((256, 768), BF16),
+    w_down=((512, 768), BF16),
+    pick_in=((128, 512), BF16),
+    pick_down=((128, 768), BF16),
+    lpA_s=((8, 64, 384), BF16),
+    lpA_r=((8, 64, 384), BF16),
+    lpB_s=((8, 64, 384), BF16),
+    lpB_r=((4, 64, 384), BF16),
+    lpC_s=((1, 64, 384), BF16),
+    lpC_r=((1, 64, 384), BF16),
+    lpD_s=((4, 64, 384), BF16),
+    lpD_r=((4, 64, 384), BF16),
+    pdA_s=((8, 64, 384), BF16),
+    pdA_r=((8, 64, 384), BF16),
+    pdB_s=((8, 64, 384), BF16),
+    pdB_r=((4, 64, 384), BF16),
+    pdC_s=((1, 64, 384), BF16),
+    pdC_r=((1, 64, 384), BF16),
+    pdD_s=((4, 64, 384), BF16),
+    pdD_r=((4, 64, 384), BF16),
     feat_s=((1, 128, 768), BF16),
     feat_r=((1, 128, 768), BF16),
-    upd_s=((8, 64, 256), BF16),
-    upd_r=((8, 64, 256), BF16),
-    dl_s=((8, 64, 256), BF16),
-    dl_r=((8, 64, 256), BF16),
-    gain_s=((8, 8, 256), F32),
-    gain_r=((8, 8, 256), F32),
+    mean_s=((1, 8, 128), F32),
+    mean_r=((8, 8, 128), F32),
+    gain_s=((1, 8, 128), F32),
+    gain_r=((8, 8, 128), F32),
     dc_s=((8, 128, 128), BF16),
     dc_r=((8, 128, 128), BF16),
     ds_s=((8, 64, 128), BF16),
     ds_r=((8, 64, 128), BF16),
-    proj_c_s=((8, 2, 96, 640), BF16),
-    proj_c_r=((1, 8, 96, 640), BF16),
-    proj_s=((8, 96, 640), BF16),
-    proj_r=((8, 96, 640), BF16),
-    up_c_s=((8, 2, 64, 256), BF16),
-    up_c_r=((1, 8, 64, 256), BF16),
-    up_s=((8, 64, 256), BF16),
-    up_r=((8, 64, 256), BF16),
-    down_c_s=((8, 2, 16, 896), BF16),
-    down_c_r=((1, 8, 16, 896), BF16),
-    down_s=((8, 16, 896), BF16),
-    down_r=((8, 16, 896), BF16),
+    up_s=((8, 16, 768), BF16),
+    up_r=((8, 16, 768), BF16),
+    first_s=((8, 16, 768), BF16),
+    first_r=((8, 16, 768), BF16),
+    mnl_c_s=((8, 2, 48, 1024), BF16),
+    mnl_c_r=((1, 8, 48, 1024), BF16),
+    mnl_s=((8, 48, 1024), BF16),
+    mnl_r=((8, 48, 1024), BF16),
+    mn_s=((1, 48, 768), BF16),
+    mn_r=((8, 48, 768), BF16),
+    full_r=((1, 8, 48, 768), BF16),
+    summed=((768, 768), BF16),
+    slices=((512, 512), BF16),
+    rest=((512, 256), BF16),
+    down_c_s=((8, 2, 16, 768), BF16),
+    down_c_r=((1, 8, 16, 768), BF16),
+    down_s=((8, 16, 768), BF16),
+    down_r=((8, 16, 768), BF16),
     conv_c_s=((8, 2, 16, 1280), BF16),
     conv_c_r=((1, 8, 16, 1280), BF16),
     conv_s=((8, 16, 1280), BF16),
     conv_r=((8, 16, 1280), BF16),
-    last_s=((8, 8, 256), F32),
-    last_r=((8, 8, 256), F32),
 )
 LINKS = dict(
     codes=Codes(),
     blk=ToBlock(),
     low=Share(),
-    mixedA=XBlocks(),
-    mixedB=ZBlocks(),
-    mixedC=ZOne(),
-    mixedD=XOne(),
-    dnA=XBlocks(),
-    dnB=ZBlocks(),
-    dnC=ZOne(),
-    dnD=XOne(),
+    lpA=XBlocks(),
+    lpB=ZBlocks(),
+    lpC=ZOne(),
+    lpD=XOne(),
+    pdA=XBlocks(),
+    pdB=ZBlocks(),
+    pdC=ZOne(),
+    pdD=XOne(),
     feat=ToOwner(),
-    upd=OverBatch(),
-    dl=OverBatch(),
-    gain=OverBatch(),
+    mean=Share(),
+    gain=Share(),
     dc=OverBatch(),
     ds=OverBatch(),
-    proj_c=Core(),
-    proj=OverQuads(),
-    up_c=Core(),
-    up=OverQuads(),
+    up=OverBatch(),
+    first=OverBatch(),
+    mnl_c=Core(),
+    mnl=OverQuads(),
+    mn=QuadShare(),
+    full=Core(),
     down_c=Core(),
     down=OverQuads(),
     conv_c=Core(),
     conv=OverQuads(),
-    last=OverBatch(),
 )
 
 
@@ -397,8 +413,10 @@
     peer = (s + 1 - 2 * h, b)
     links = Namespace()
     for k, (name, pattern) in enumerate(LINKS.items()):
-        sent = getattr(n, name + "_s_")
-        if name.endswith("_c"):
+        sent = n.mn_r_ if name == "full" else getattr(n, name + "_s_")
+        if name == "full":
+            source = lambda piece, sent=sent: sent
+        elif name.endswith("_c"):
             source = lambda piece, sent=sent: sent.at[:, piece]
         else:
             source = lambda piece, sent=sent: sent.at[piece]
@@ -407,7 +425,7 @@
         setattr(links, name, link)
 
     barrier = pltpu.get_barrier_semaphore()
-    for link in (links.codes, links.low, links.proj, links.up_c, links.feat):
+    for link in (links.codes, links.low, links.mnl, links.mnl_c, links.feat):
         pattern = link.pattern
 
         def greet(i, pattern=pattern):
@@ -457,7 +475,6 @@
         good = i < 6
         rows = iota((768, 128), 0)
         place = rows_of(c, 128)
-        n.select_[:, place] = zero_one(rows == jnp.where(good, 6 * (m + 16 * c) + i, -1))
         n.select_conv_[:, place] = zero_one(rows == jnp.where(good, 6 * (8 * m + c) + i, -1))
         wanted = 12 * (8 * (m // 2) + c) + 6 * lax.rem(m, 2) + i
         n.select_down_[:, place] = zero_one(rows == jnp.where(good, wanted, -1))
@@ -552,6 +569,9 @@
         send_sem=swap_send.at[0], recv_sem=swap_recv.at[0], device_id=peer, device_id_type=MESH,
     )
     swap.start()
+    n.w_up_[...] = dot(n.o_w_[...], n.up_w_[...]).astype(BF16)
+    gained = (n.in_t_[...].astype(F32) * gain).astype(BF16)
+    n.w_down_[...] = dot_cols(gained, n.down_w_[...]).astype(BF16)
     links.low.receive()
 
     def cotangent_of_mixed(c):
@@ -569,8 +589,8 @@
 
     def send_pair(name, t, value):
         half = value.astype(BF16)
-        getattr(n, name + "A_s_")[pl.ds(2 * t, 2)] = half[:, :768].reshape(2, 64, 768)
-        getattr(n, name + "B_s_")[pl.ds(2 * t, 2)] = half[:, 768:].reshape(2, 64, 768)
+        getattr(n, name + "A_s_")[pl.ds(2 * t, 2)] = half[:, :384].reshape(2, 64, 384)
+        getattr(n, name + "B_s_")[pl.ds(2 * t, 2)] = half[:, 384:].reshape(2, 64, 384)
         for j in (2 * t, 2 * t + 1):
             to, side = lax.rem(j, 4), j // 4
             getattr(links, name + "A").start_one(2 * lax.rem(to - lax.rem(b, 4) + 4, 4) + side)
@@ -604,7 +624,7 @@
         att = att.astype(BF16)
         n.att_[here, :] = att
         n.dqkv_[here, :128] = (dq * scale).astype(BF16)
-        send_pair("mixed", t, dot(att, n.o_w_[...]))
+        send_pair("lp", t, dot(att, n.w_up_[...]))
 
     loop(4, attend)
     n.dkv_s_[...] = n.dkv_far_[...].astype(BF16)
@@ -613,13 +633,26 @@
         device_id=peer, device_id_type=MESH,
     )
     swap_back.start()
+    low = n.low_r_[...].reshape(512, 768)
+    pick = n.select_down_[:, rows_of(b, 128)]
+    for half in range(2):
+        wide = slice(768 * half, 768 * half + 768)
+        n.slices_[:, 128 * half : 128 * half + 128] = dot(n.lifted_[:, wide], pick).astype(BF16)
     swap_back.wait()
     n.dqkv_[:, 128:] = (n.dkv_own_[...] + n.dkv_r_[...].astype(F32)).astype(BF16)
 
     def back_through_projections(t):
-        send_pair("dn", t, dot(n.dqkv_[rows_of(t, 128), :], n.in_t_[...]))
+        send_pair("pd", t, dot(n.dqkv_[rows_of(t, 128), :], n.w_down_[...]))
 
     loop(4, back_through_projections)
+
+    scaled = (n.pooled_[...].astype(F32) * n.factor_[:, 0:1]).astype(BF16)
+    n.mnl_c_s_[:, :, :, :512] = dot_rows(scaled, n.dqkv_[...]).astype(BF16).reshape(8, 2, 48, 512)
+    n.mnl_c_s_[:, :, :, 512:768] = dot_rows(low, n.att_[...]).astype(BF16).reshape(8, 2, 48, 256)
+    n.mnl_c_s_[:, :, :, 768:] = (
+        dot_rows(low, n.slices_[:, :256]).astype(BF16).reshape(8, 2, 48, 256)
+    )
+    links.mnl_c.start()
 
     def first_hop(name):
         over_x, over_z = getattr(links, name + "A"), getattr(links, name + "B")
@@ -645,39 +678,6 @@
         getattr(links, name + "D").receive()
         return jnp.concatenate([left, total(getattr(links, name + "D").result, 4)], axis=1)
 
-    first_hop("mixed")
-
-    def projection_grads(c):
-        chunk = rows_of(c, 384)
-        first = dot_rows(n.normed_[:, chunk], n.dqkv_[...]).astype(BF16)
-        second = dot_rows(n.d_mixed_[:, chunk], n.att_[...]).astype(BF16)
-        both = jnp.concatenate([first[:, :448], second[:, :192]], axis=1)
-        n.proj_c_s_[pl.ds(2 * c, 2)] = both.reshape(2, 2, 96, 640)
-
-    loop(4, projection_grads)
-    links.proj_c.start()
-
-    here = rows_of(b, 64)
-    n.conv_[...] = dot(n.emb_[b], n.conv_w_[...])
-    center = n.emb_[b, :, 768:1536].astype(F32)
-    n.tower_[...] = (center + jax.nn.gelu(n.conv_[...])).astype(BF16)
-    lifted = n.lifted_[here, :].astype(F32)
-    factor = n.factor_[here, 0:1]
-    first_hop("dn")
-    updated = (lifted + second_hop("mixed")).astype(BF16)
-
-    def select_into(target, value, matrix):
-        for half in range(2):
-            moved = dot(value[:, 768 * half : 768 * half + 768], matrix[...]).astype(BF16)
-            for j in range(4):
-                target[4 * half + j] = moved[:, 256 * j : 256 * j + 256]
-
-    select_into(n.upd_s_, updated, n.select_)
-    lowered = dot(updated, n.up_w_[...])
-    features = n.tower_[...].astype(F32) + jnp.concatenate([lowered, lowered], axis=0)
-    n.feat_s_[0] = dot_rows(order, features.astype(BF16)).astype(BF16)
-    links.feat.start()
-
     def core_sum(name):
         getattr(links, name + "_c").receive()
         mine = getattr(n, name + "_c_s_")
@@ -690,26 +690,34 @@
         loop(8, add)
         getattr(links, name).start()
 
-    d_normed = second_hop("dn").astype(BF16).astype(F32)
-    d_updated = n.d_mixed_[here, :].astype(F32)
-    gained = d_normed * gain
-    shared = jnp.mean(gained * lifted, axis=-1, keepdims=True) * (factor * factor * factor)
-    d_lifted = (gained * factor - lifted * shared).astype(BF16).astype(F32) + d_updated
-    d_lifted = d_lifted.astype(BF16)
-    for half in range(2):
-        moved = dot(d_lifted[:, 768 * half : 768 * half + 768], n.select_down_[...]).astype(BF16)
-        for j in range(8):
-            n.dl_s_[j, :, 128 * half : 128 * half + 128] = moved[:, 128 * j : 128 * j + 128]
-    links.dl.start()
-    d_pooled = dot_cols(d_lifted, n.down_w_[...]) * 0.5
+    first_hop("lp")
+    core_sum("mnl")
+
+    here = rows_of(b, 64)
+    n.conv_[...] = dot(n.emb_[b], n.conv_w_[...])
+    center = n.emb_[b, :, 768:1536].astype(F32)
+    n.tower_[...] = (center + jax.nn.gelu(n.conv_[...])).astype(BF16)
+    lifted = n.lifted_[here, :]
+    factor = n.factor_[here, 0:1]
+    cube = factor * factor * factor
+    first_hop("pd")
+    behind = dot_cols(jnp.concatenate([lifted, n.d_mixed_[here, :]], axis=0), n.down_w_[...])
+    lowered = dot(lifted, n.up_w_[...])
+    slope = gelu_grad(n.conv_[...])
+    straight = second_hop("pd")
+    mean = jnp.sum(straight * n.pooled_[here, :].astype(F32), axis=-1, keepdims=True) / 1536.0
+    d_pooled = 0.5 * (factor * straight - cube * mean * behind[:64] + behind[64:])
     d_tower = n.blk_r_[0].astype(F32) + jnp.concatenate([d_pooled, d_pooled], axis=0)
     d_tower = d_tower.astype(BF16)
-    d_conv = (d_tower.astype(F32) * gelu_grad(n.conv_[...])).astype(BF16)
+    d_conv = (d_tower.astype(F32) * slope).astype(BF16)
     moved = dot(d_conv, n.select_conv_[...]).astype(BF16)
     for j in range(8):
         n.dc_s_[j] = moved[:, 128 * j : 128 * j + 128]
     links.dc.start()
-    links.upd.start()
+    diagonal = iota((64, 128), 0) == iota((64, 128), 1)
+    line = jnp.sum(jnp.where(diagonal, mean, 0.0), axis=0, keepdims=True)
+    n.mean_s_[0] = jnp.broadcast_to(line, (8, 128))
+    links.mean.start()
     hots = one_hots(b)
     d_stem = jnp.zeros((128, 768), F32)
     for step in range(3):
@@ -722,30 +730,45 @@
     for j in range(8):
         n.ds_s_[j] = moved[:, 128 * j : 128 * j + 128]
     links.ds.start()
-    d_gain = jnp.sum(d_normed * (lifted * factor), axis=0, keepdims=True).astype(BF16)
-    d_gain = jnp.broadcast_to(d_gain, (16, 1536))
+
+    lowered = lowered + second_hop("lp")
+    features = n.tower_[...].astype(F32) + jnp.concatenate([lowered, lowered], axis=0)
+    n.feat_s_[0] = dot_rows(order, features.astype(BF16)).astype(BF16)
+    links.feat.start()
+
+    links.mnl.receive()
+    summed = total(n.mnl_r_, 8)
+    n.mn_s_[0] = summed[:, :768].astype(BF16)
+    links.mn.start()
+    wide = dot(summed[:, 512:768].astype(BF16), n.o_w_[...])
+    sides = [
+        dot_cols(summed[:, 768 + 128 * half : 896 + 128 * half].astype(BF16), pick)
+        for half in range(2)
+    ]
+    wide = (wide + jnp.concatenate(sides, axis=1)).astype(BF16)
+    groups = iota((64, 48), 0)
+    groups = jnp.where(groups % 8 < 6, 6 * (groups // 8) + groups % 8, -1)
+    wide = dot(zero_one(iota((64, 48), 1) == groups), wide)
+    n.up_s_[:, 0:8, :] = wide[:, :768].reshape(8, 8, 768).astype(BF16)
+    n.up_s_[:, 8:16, :] = wide[:, 768:].reshape(8, 8, 768).astype(BF16)
+    links.up.start()
+
     for half in range(2):
-        moved = dot(d_gain[:, 768 * half : 768 * half + 768], n.select_down_[...])
-        for j in range(8):
-            n.gain_s_[j, :, 128 * half : 128 * half + 128] = moved[:8, 128 * j : 128 * j + 128]
-    links.gain.start()
-    core_sum("proj")
-
-    def select_low(t):
-        rows = rows_of(t, 128)
-        low = n.low_r_[pl.ds(2 * t, 2)].reshape(128, 768)
-        n.low_sel_[rows, :] = dot(low, n.select_[...]).astype(BF16)
-
-    loop(4, select_low)
-
-    links.dl.receive()
-    down = dot_rows(n.dl_r_[...].reshape(512, 256), n.pooled_[...]).astype(BF16)
-    n.down_c_s_[:, :, :, :768] = down.reshape(8, 2, 16, 768)
-    links.gain.receive()
-    first_row = jnp.logical_and(iota((64, 128), 0) % 8 == 0, iota((64, 128), 1) == 0)
-    gains = dot_rows(n.gain_r_[...].reshape(64, 256).astype(BF16), zero_one(first_row)).astype(BF16)
-    n.down_c_s_[:, :, :, 768:] = gains.reshape(8, 2, 16, 128)
+        wide = slice(768 * half, 768 * half + 768)
+        n.slices_[:, 256 + 128 * half : 384 + 128 * half] = dot(n.d_mixed_[:, wide], pick).astype(BF16)
+    links.mean.receive()
+
+    def remainder(j):
+        rows = rows_of(j, 64)
+        mean = jnp.sum(jnp.where(diagonal, n.mean_r_[j][0:1], 0.0), axis=1, keepdims=True)
+        factor = n.factor_[rows, 0:1]
+        part = factor * factor * factor * mean * n.slices_[rows, :256].astype(F32)
+        n.rest_[rows, :] = (n.slices_[rows, 256:].astype(F32) - part).astype(BF16)
+
+    loop(8, remainder)
+    n.down_c_s_[...] = dot_rows(n.rest_[...], n.pooled_[...]).astype(BF16).reshape(8, 2, 16, 768)
     links.down_c.start()
+
     n.conv_acc_[...] = jnp.zeros((128, 2304), F32)
     links.dc.receive()
 
@@ -755,7 +778,6 @@
         n.conv_acc_[...] += dot_rows(left, n.emb_[pair].reshape(256, 2304))
 
     loop(4, conv_grads)
-    core_sum("down")
     links.ds.receive()
     same = zero_one(iota((512, 128), 0) % 64 == iota((512, 128), 1))
     stem = dot_rows(n.ds_r_[...].reshape(512, 128), same)
@@ -763,32 +785,51 @@
     rest = jnp.concatenate([n.conv_acc_[:, 1280:], stem, jnp.zeros((128, 128), F32)], axis=1)
     n.conv_c_s_[:, :, 8:16, :] = rest.reshape(8, 2, 8, 1280).astype(BF16)
     links.conv_c.start()
-    links.upd.receive()
-    up = dot_rows(n.low_sel_[...], n.upd_r_[...].reshape(512, 256)).astype(BF16)
-    n.up_c_s_[...] = up.reshape(8, 2, 64, 256)
-    links.up_c.start()
+    links.mn.receive()
+    links.full.start()
     core_sum("conv")
-    core_sum("up")
-
-    links.proj.receive()
-    proj = total(n.proj_r_, 8)
-    n.g_q[...] = proj[:, :128]
-    n.g_k[...] = proj[:, 128:256]
-    n.g_v[...] = proj[:, 256:448]
-    n.g_o[...] = proj[:, 448:]
+    core_sum("down")
+
+    lane, channel = iota((128, 1536), 0), iota((128, 1536), 1)
+    wanted = jnp.where(lane < 96, 96 * s + lane, -1)
+    hit = channel == wanted
+    gain_here = jnp.sum(jnp.where(hit, gain, 0.0), axis=1, keepdims=True)[:96]
+    n.pick_down_[...] = dot_cols(zero_one(hit), n.down_w_[...]).astype(BF16)
+    wanted = 96 * s + 12 * (lane // 16) + 6 * (lane % 16 // 8) + lane % 8
+    hit = jnp.logical_and(channel == wanted, lane % 8 < 6)
+    gained = (n.in_t_[...].astype(F32) * gain).astype(BF16)
+    n.pick_in_[...] = dot_cols(zero_one(hit), gained).astype(BF16)
+    links.full.receive()
+
+    def assemble(q):
+        near = pl.ds(pl.multiple_of(96 * q + 48 * h, 16), 48)
+        far = pl.ds(pl.multiple_of(96 * q + 48 * (1 - h), 16), 48)
+        n.summed_[near, :] = n.mn_r_[q]
+        n.summed_[far, :] = n.full_r_[0, q]
+
+    loop(8, assemble)
+    first = dot_cols(n.pick_in_[...], n.summed_[:, :512])
+    n.first_s_[...] = first.astype(BF16).reshape(8, 16, 768)
+    links.first.start()
+    inner = dot(n.pick_down_[...], n.summed_[:, :512])[:96]
+    rows = pl.ds(pl.multiple_of(96 * s, 16), 96)
+    part = jnp.sum(inner * n.in_w_[rows, :].astype(F32), axis=1, keepdims=True)
+    diagonal = iota((96, 128), 0) == iota((96, 128), 1)
+    line = jnp.sum(jnp.where(diagonal, part, 0.0), axis=0, keepdims=True)
+    n.gain_s_[0] = jnp.broadcast_to(line, (8, 128))
+    links.gain.start()
+    inner = inner * gain_here
+    n.g_q[...] = inner[:, :128]
+    n.g_k[...] = inner[:, 128:256]
+    n.g_v[...] = inner[:, 256:448]
+    n.g_o[...] = dot(n.up_w_[rows, :], n.summed_[:, 512:])[:, :192]
+
     links.feat.receive()
     n.features[...] = n.feat_r_[0]
-    links.down.receive()
-    down = total(n.down_r_, 8)
-    n.g_down[0:6, :] = down[0:6, :768]
-    n.g_down[6:12, :] = down[8:14, :768]
-    lane = iota((16, 128), 1)
-    wanted = jnp.where(lane < 6, lane, lane + 2)
-    hit = jnp.logical_and(iota((16, 128), 0) == wanted, lane < 12)
-    n.g_gain[...] = jnp.sum(jnp.where(hit, down[:, 768:769], 0.0), axis=0, keepdims=True)
     links.up.receive()
-    n.last_s_[...] = total(n.up_r_, 8).reshape(8, 8, 256)
-    links.last.start()
+    up = total(n.up_r_, 8)
+    n.g_up[:, :768] = up[0:6]
+    n.g_up[:, 768:] = up[8:14]
     links.conv.receive()
     conv = total(n.conv_r_, 8)
     n.g_conv[0] = conv[0:6, :768]
@@ -798,27 +839,25 @@
     for code in range(4):
         taps = iota((128, 15), 0) == 4 * iota((128, 15), 1) + code
         n.g_stem[:, code, :] = dot(stem, zero_one(taps))[:6]
-    lane = iota((192, 256), 1)
-    tight = jnp.logical_and(iota((192, 256), 0) == 6 * (lane // 8) + lane % 8, lane % 8 < 6)
-    tight = zero_one(tight)
-    links.last.receive()
-    for j in range(4):
-        pieces = [dot_cols(n.last_r_[2 * j + k].astype(BF16), tight) for k in range(2)]
-        n.g_up[:, 384 * j : 384 * j + 384] = jnp.concatenate(pieces, axis=1)[:6]
+    links.down.receive()
+    links.first.receive()
+    down = total(n.down_r_, 8) + total(n.first_r_, 8)
+    n.g_down[0:6, :] = down[0:6]
+    n.g_down[6:12, :] = down[8:14]
+    links.gain.receive()
+    gains = total(n.gain_r_, 8)
+    high = gains.astype(BF16)
+    low = (gains - high.astype(F32)).astype(BF16)
+    shift = zero_one(jnp.logical_and(row == column + 12 * b, column < 12))
+    n.g_gain[...] = (dot(high, shift) + dot(low, shift))[0:1]
     for link in vars(links).values():
         link.drain()
 
 
 def finish_body(*refs):
     number = len(OUTPUTS)
-    copies = [
-        pltpu.make_async_copy(source, target, refs[-1].at[k])
-        for k, (source, target) in enumerate(zip(refs[:number], refs[number : 2 * number]))
-    ]
-    for copy in copies:
-        copy.start()
-    for copy in copies:
-        copy.wait()
+    for source, target in zip(refs[:number], refs[number:]):
+        target[...] = source[...]
 
 
 def per_device(
@@ -869,9 +908,8 @@
     features, g_stem, g_conv, g_down, g_gain, g_up, g_q, g_k, g_v, g_o = pl.pallas_call(
         finish_body,
         out_shape=out_shape,
-        in_specs=[anywhere] * len(OUTPUTS),
-        out_specs=[anywhere] * len(OUTPUTS),
-        scratch_shapes=[pltpu.SemaphoreType.DMA((len(OUTPUTS),))],
+        in_specs=[vmem] * len(OUTPUTS),
+        out_specs=[vmem] * len(OUTPUTS),
         name="finish",
     )(*results)
     return (

time: 149 us -> 109 us (0.73)
  Pallas kernels: 144 us -> 105 us
    pallas_call x1, Pallas kernels: 21.7 us -> 2.06 us  [per_device(): pl.pallas_call(finish_body, out_shape=out_shape, in_specs=[vmem] * len(OU...]
    pallas_call x1, Pallas kernels: 123 us -> 103 us  [per_device(): pl.pallas_call(kernel_body, out_shape=out_shape, in_specs=[vmem] * 4 + [a...]
where the time goes in v4:
time: 109 us; the launch traced here: 107 us
  Pallas kernels  105 us (96%)
  local copies, waits for them, and re-layouts  1.12 us (1%)
    pallas_call x1, Pallas kernels, per_device(): pl.pallas_call(kernel_body, out_shape=out_shape, in_specs=[vmem] * 4 + [a...  103 us

profile of v4, /device:TPU:1, one launch (start us, length us, event | category | flops | bytes accessed | tf_op | source)
XLA Modules:
  0.0 107.1 jit_solution(3204326892412027453)
XLA Ops:
  0.6 103.3 %step.1 = (bf16[128,768]{1,0:T(8,128)(2,1)}, f32[6,4,15]{2,1,0:T(4,128)}, f32[3,6,768]{2,1,0:T(8,128)}, f32[12,768]{1,0:T(8,128)}, f32[1,128]{1,0:T(1,128)}, /*i...) custom-call(s32[1,128]{1,0:T(1,128)} %refs_0_.1, ...), custom_call_target="tpu_custom_call" | custom-call | tf_op jit(solution)/shard_map/step/pallas_call | solution.py:885
  103.9 2.1 %finish.1 = (bf16[128,768]{1,0:T(8,128)(2,1)}, f32[6,4,15]{2,1,0:T(4,128)}, f32[3,6,768]{2,1,0:T(8,128)}, f32[12,768]{1,0:T(8,128)}, f32[1,128]{1,0:T(1,128)}, /...) custom-call(bf16[128,768]{1,0:T(8,128)(2,1)} %get-tuple-element.30.refs_, ...), custom_call_target="tpu_custom_call" | custom-call | tf_op jit(solution)/shard_map/finish/pallas_call | solution.py:908
  106.0 1.1 %slice_bitcast_fusion = f32[12]{0:T(128)} fusion(f32[1,128]{1,0:T(1,128)} %get-tuple-element.44), kind=kLoop, calls=%fused_computation | loop fusion | bytes 96 | tf_op jit(solution)/shard_map/squeeze | solution.py:920

commit v5 on v4

--- a/solution.py
+++ b/solution.py
@@ -281,7 +281,6 @@
     in_w=((1536, 512), BF16),
     in_t=((512, 1536), BF16),
     o_w=((256, 1536), BF16),
-    o_t=((1536, 256), BF16),
     up_w=((1536, 768), BF16),
     stem_f=((64, 768), F32),
     stem_w=((128, 768), BF16),
@@ -291,7 +290,8 @@
     codes_r=((16, 8, 128), F32),
     blk_s=((1, 128, 768), BF16),
     blk_r=((1, 128, 768), BF16),
-    low_s=((1, 64, 768), BF16),
+    own_s=((1, 64, 768), BF16),
+    own_r=((1, 64, 768), BF16),
     low_r=((8, 64, 768), BF16),
     code=((2, 640, 128), F32),
     picked=((2, 528, 128), F32),
@@ -304,7 +304,6 @@
     normed=((512, 1536), BF16),
     qkv=((512, 512), BF16),
     kv_far=((512, 384), BF16),
-    d_mixed=((512, 1536), BF16),
     d_att=((512, 256), BF16),
     att=((512, 256), BF16),
     dqkv=((512, 512), BF16),
@@ -368,6 +367,7 @@
 )
 LINKS = dict(
     codes=Codes(),
+    own=ToBlock(),
     blk=ToBlock(),
     low=Share(),
     lpA=XBlocks(),
@@ -396,6 +396,9 @@
 )
 
 
+FORWARDED = dict(low="own_r", full="mn_r")
+
+
 class Namespace:
     pass
 
@@ -413,7 +416,7 @@
     peer = (s + 1 - 2 * h, b)
     links = Namespace()
     for k, (name, pattern) in enumerate(LINKS.items()):
-        sent = n.mn_r_ if name == "full" else getattr(n, name + "_s_")
+        sent = getattr(n, FORWARDED.get(name, name + "_s") + "_")
         if name == "full":
             source = lambda piece, sent=sent: sent
         elif name.endswith("_c"):
@@ -463,11 +466,13 @@
     order = zero_one(column == jnp.where(row < 64, 2 * row, 2 * row - 127))
     codes = jnp.broadcast_to((n.codes[...] + 1).astype(F32), (8, 128)).astype(BF16)
     n.codes_s_[0] = dot_cols(codes, order)
-    n.blk_s_[0] = dot(order, n.cot[...]).astype(BF16)
+    cot = dot(order, n.cot[...])
+    n.own_s_[0] = (cot[:64] + cot[64:]).astype(BF16)
+    n.blk_s_[0] = cot.astype(BF16)
 
     pl.semaphore_wait(barrier, expected)
     links.codes.start()
-    links.blk.start()
+    links.own.start()
 
     def fill(c):
         within = iota((1, 128), 1)
@@ -493,7 +498,6 @@
     n.in_t_[:128, :] = dot_cols(eye, n.in_w_[:, :128]).astype(BF16)
     n.in_t_[128:256, :] = dot_cols(eye, n.in_w_[:, 128:256]).astype(BF16)
     n.in_w_[:, 256:] = dot_rows(n.in_t_[256:, :], eye2).astype(BF16)
-    n.o_t_[...] = dot_rows(n.o_w_[...], eye2).astype(BF16)
 
     links.codes.receive()
     ones = jnp.ones((128, 128), BF16)
@@ -518,10 +522,9 @@
         inside = jnp.logical_and(where >= 0, where < 1024)
         n.picked_[parity] = jnp.where(inside, picked, 0.0)
 
-    links.blk.receive()
-    pairs = n.blk_r_[0].astype(F32)
-    n.low_s_[0] = (pairs[:64] + pairs[64:]).astype(BF16)
+    links.own.receive()
     links.low.start()
+    links.blk.start()
 
     def one_hots(j):
         found = []
@@ -570,17 +573,12 @@
     )
     swap.start()
     n.w_up_[...] = dot(n.o_w_[...], n.up_w_[...]).astype(BF16)
-    gained = (n.in_t_[...].astype(F32) * gain).astype(BF16)
-    n.w_down_[...] = dot_cols(gained, n.down_w_[...]).astype(BF16)
     links.low.receive()
 
-    def cotangent_of_mixed(c):
-        low = n.low_r_[...].reshape(512, 768)
-        chunk = rows_of(c, 256)
-        n.d_mixed_[:, chunk] = dot_cols(low, n.up_w_[chunk, :]).astype(BF16)
-
-    loop(6, cotangent_of_mixed)
-    n.d_att_[...] = dot(n.d_mixed_[...], n.o_t_[...]).astype(BF16)
+    def low():
+        return n.low_r_[...].reshape(512, 768)
+
+    n.d_att_[...] = dot_cols(low(), n.w_up_[...]).astype(BF16)
     n.dkv_own_[...] = jnp.zeros((512, 384), F32)
     n.dkv_far_[...] = jnp.zeros((512, 384), F32)
     swap.wait()
@@ -633,24 +631,26 @@
         device_id=peer, device_id_type=MESH,
     )
     swap_back.start()
-    low = n.low_r_[...].reshape(512, 768)
+    gained = (n.in_t_[...].astype(F32) * gain).astype(BF16)
+    n.w_down_[...] = dot_cols(gained, n.down_w_[...]).astype(BF16)
+    swap_back.wait()
+    n.dqkv_[:, 128:] = (n.dkv_own_[...] + n.dkv_r_[...].astype(F32)).astype(BF16)
+
+    def back_through_projections(t):
+        send_pair("pd", t, dot(n.dqkv_[rows_of(t, 128), :], n.w_down_[...]))
+
+    loop(4, back_through_projections)
+
     pick = n.select_down_[:, rows_of(b, 128)]
     for half in range(2):
         wide = slice(768 * half, 768 * half + 768)
         n.slices_[:, 128 * half : 128 * half + 128] = dot(n.lifted_[:, wide], pick).astype(BF16)
-    swap_back.wait()
-    n.dqkv_[:, 128:] = (n.dkv_own_[...] + n.dkv_r_[...].astype(F32)).astype(BF16)
-
-    def back_through_projections(t):
-        send_pair("pd", t, dot(n.dqkv_[rows_of(t, 128), :], n.w_down_[...]))
-
-    loop(4, back_through_projections)
 
     scaled = (n.pooled_[...].astype(F32) * n.factor_[:, 0:1]).astype(BF16)
     n.mnl_c_s_[:, :, :, :512] = dot_rows(scaled, n.dqkv_[...]).astype(BF16).reshape(8, 2, 48, 512)
-    n.mnl_c_s_[:, :, :, 512:768] = dot_rows(low, n.att_[...]).astype(BF16).reshape(8, 2, 48, 256)
+    n.mnl_c_s_[:, :, :, 512:768] = dot_rows(low(), n.att_[...]).astype(BF16).reshape(8, 2, 48, 256)
     n.mnl_c_s_[:, :, :, 768:] = (
-        dot_rows(low, n.slices_[:, :256]).astype(BF16).reshape(8, 2, 48, 256)
+        dot_rows(low(), n.slices_[:, :256]).astype(BF16).reshape(8, 2, 48, 256)
     )
     links.mnl_c.start()
 
@@ -700,13 +700,29 @@
     lifted = n.lifted_[here, :]
     factor = n.factor_[here, 0:1]
     cube = factor * factor * factor
-    first_hop("pd")
-    behind = dot_cols(jnp.concatenate([lifted, n.d_mixed_[here, :]], axis=0), n.down_w_[...])
+    d_updated = dot_cols(n.own_r_[0], n.up_w_[...]).astype(BF16)
+    behind = dot_cols(jnp.concatenate([lifted, d_updated], axis=0), n.down_w_[...])
     lowered = dot(lifted, n.up_w_[...])
     slope = gelu_grad(n.conv_[...])
+    first_hop("pd")
+    lowered = lowered + second_hop("lp")
+    features = n.tower_[...].astype(F32) + jnp.concatenate([lowered, lowered], axis=0)
+    n.feat_s_[0] = dot_rows(order, features.astype(BF16)).astype(BF16)
+    links.feat.start()
+
+    lane, channel = iota((128, 1536), 0), iota((128, 1536), 1)
+    wanted = jnp.where(lane < 96, 96 * s + lane, -1)
+    hit = channel == wanted
+    gain_here = jnp.sum(jnp.where(hit, gain, 0.0), axis=1, keepdims=True)[:96]
+    n.pick_down_[...] = dot_cols(zero_one(hit), n.down_w_[...]).astype(BF16)
+    wanted = 96 * s + 12 * (lane // 16) + 6 * (lane % 16 // 8) + lane % 8
+    hit = jnp.logical_and(channel == wanted, lane % 8 < 6)
+    gained = (n.in_t_[...].astype(F32) * gain).astype(BF16)
+    n.pick_in_[...] = dot_cols(zero_one(hit), gained).astype(BF16)
     straight = second_hop("pd")
     mean = jnp.sum(straight * n.pooled_[here, :].astype(F32), axis=-1, keepdims=True) / 1536.0
     d_pooled = 0.5 * (factor * straight - cube * mean * behind[:64] + behind[64:])
+    links.blk.receive()
     d_tower = n.blk_r_[0].astype(F32) + jnp.concatenate([d_pooled, d_pooled], axis=0)
     d_tower = d_tower.astype(BF16)
     d_conv = (d_tower.astype(F32) * slope).astype(BF16)
@@ -718,6 +734,12 @@
     line = jnp.sum(jnp.where(diagonal, mean, 0.0), axis=0, keepdims=True)
     n.mean_s_[0] = jnp.broadcast_to(line, (8, 128))
     links.mean.start()
+
+    links.mnl.receive()
+    summed = total(n.mnl_r_, 8)
+    n.mn_s_[0] = summed[:, :768].astype(BF16)
+    links.mn.start()
+
     hots = one_hots(b)
     d_stem = jnp.zeros((128, 768), F32)
     for step in range(3):
@@ -731,15 +753,6 @@
         n.ds_s_[j] = moved[:, 128 * j : 128 * j + 128]
     links.ds.start()
 
-    lowered = lowered + second_hop("lp")
-    features = n.tower_[...].astype(F32) + jnp.concatenate([lowered, lowered], axis=0)
-    n.feat_s_[0] = dot_rows(order, features.astype(BF16)).astype(BF16)
-    links.feat.start()
-
-    links.mnl.receive()
-    summed = total(n.mnl_r_, 8)
-    n.mn_s_[0] = summed[:, :768].astype(BF16)
-    links.mn.start()
     wide = dot(summed[:, 512:768].astype(BF16), n.o_w_[...])
     sides = [
         dot_cols(summed[:, 768 + 128 * half : 896 + 128 * half].astype(BF16), pick)
@@ -755,20 +768,8 @@
 
     for half in range(2):
         wide = slice(768 * half, 768 * half + 768)
-        n.slices_[:, 256 + 128 * half : 384 + 128 * half] = dot(n.d_mixed_[:, wide], pick).astype(BF16)
-    links.mean.receive()
-
-    def remainder(j):
-        rows = rows_of(j, 64)
-        mean = jnp.sum(jnp.where(diagonal, n.mean_r_[j][0:1], 0.0), axis=1, keepdims=True)
-        factor = n.factor_[rows, 0:1]
-        part = factor * factor * factor * mean * n.slices_[rows, :256].astype(F32)
-        n.rest_[rows, :] = (n.slices_[rows, 256:].astype(F32) - part).astype(BF16)
-
-    loop(8, remainder)
-    n.down_c_s_[...] = dot_rows(n.rest_[...], n.pooled_[...]).astype(BF16).reshape(8, 2, 16, 768)
-    links.down_c.start()
-
+        part = dot_rows(pick, n.up_w_[wide, :]).astype(BF16)
+        n.slices_[:, 256 + 128 * half : 384 + 128 * half] = dot_cols(low(), part).astype(BF16)
     n.conv_acc_[...] = jnp.zeros((128, 2304), F32)
     links.dc.receive()
 
@@ -785,20 +786,25 @@
     rest = jnp.concatenate([n.conv_acc_[:, 1280:], stem, jnp.zeros((128, 128), F32)], axis=1)
     n.conv_c_s_[:, :, 8:16, :] = rest.reshape(8, 2, 8, 1280).astype(BF16)
     links.conv_c.start()
+
+    links.mean.receive()
+
+    def remainder(j):
+        rows = rows_of(j, 64)
+        mean = jnp.sum(jnp.where(diagonal, n.mean_r_[j][0:1], 0.0), axis=1, keepdims=True)
+        factor = n.factor_[rows, 0:1]
+        part = factor * factor * factor * mean * n.slices_[rows, :256].astype(F32)
+        n.rest_[rows, :] = (n.slices_[rows, 256:].astype(F32) - part).astype(BF16)
+
+    loop(8, remainder)
+    n.down_c_s_[...] = dot_rows(n.rest_[...], n.pooled_[...]).astype(BF16).reshape(8, 2, 16, 768)
+    links.down_c.start()
+
+    core_sum("conv")
     links.mn.receive()
     links.full.start()
-    core_sum("conv")
     core_sum("down")
 
-    lane, channel = iota((128, 1536), 0), iota((128, 1536), 1)
-    wanted = jnp.where(lane < 96, 96 * s + lane, -1)
-    hit = channel == wanted
-    gain_here = jnp.sum(jnp.where(hit, gain, 0.0), axis=1, keepdims=True)[:96]
-    n.pick_down_[...] = dot_cols(zero_one(hit), n.down_w_[...]).astype(BF16)
-    wanted = 96 * s + 12 * (lane // 16) + 6 * (lane % 16 // 8) + lane % 8
-    hit = jnp.logical_and(channel == wanted, lane % 8 < 6)
-    gained = (n.in_t_[...].astype(F32) * gain).astype(BF16)
-    n.pick_in_[...] = dot_cols(zero_one(hit), gained).astype(BF16)
     links.full.receive()
 
     def assemble(q):
@@ -847,9 +853,9 @@
     links.gain.receive()
     gains = total(n.gain_r_, 8)
     high = gains.astype(BF16)
-    low = (gains - high.astype(F32)).astype(BF16)
+    fine = (gains - high.astype(F32)).astype(BF16)
     shift = zero_one(jnp.logical_and(row == column + 12 * b, column < 12))
-    n.g_gain[...] = (dot(high, shift) + dot(low, shift))[0:1]
+    n.g_gain[...] = (dot(high, shift) + dot(fine, shift))[0:1]
     for link in vars(links).values():
         link.drain()
 

time: 109 us -> 108 us (level); the launches traced: 107 us -> 108 us
  no operation moved by 1% of the time
where the time goes in v5:
time: 108 us
  Pallas kernels  106 us (98%)
  local copies, waits for them, and re-layouts  1.12 us (1%)
    pallas_call x1, Pallas kernels, per_device(): pl.pallas_call(kernel_body, out_shape=out_shape, in_specs=[vmem] * 4 + [a...  104 us

profile of v5, /device:TPU:1, one launch (start us, length us, event | category | flops | bytes accessed | tf_op | source)
XLA Modules:
  0.0 107.6 jit_solution(13284316709944054037)
XLA Ops:
  0.6 103.8 %step.1 = (bf16[128,768]{1,0:T(8,128)(2,1)}, f32[6,4,15]{2,1,0:T(4,128)}, f32[3,6,768]{2,1,0:T(8,128)}, f32[12,768]{1,0:T(8,128)}, f32[1,128]{1,0:T(1,128)}, /*i...) custom-call(s32[1,128]{1,0:T(1,128)} %refs_0_.1, ...), custom_call_target="tpu_custom_call" | custom-call | tf_op jit(solution)/shard_map/step/pallas_call | solution.py:891
  104.4 2.1 %finish.1 = (bf16[128,768]{1,0:T(8,128)(2,1)}, f32[6,4,15]{2,1,0:T(4,128)}, f32[3,6,768]{2,1,0:T(8,128)}, f32[12,768]{1,0:T(8,128)}, f32[1,128]{1,0:T(1,128)}, /...) custom-call(bf16[128,768]{1,0:T(8,128)(2,1)} %get-tuple-element.30.refs_, ...), custom_call_target="tpu_custom_call" | custom-call | tf_op jit(solution)/shard_map/finish/pallas_call | solution.py:914
  106.5 1.1 %slice_bitcast_fusion = f32[12]{0:T(128)} fusion(f32[1,128]{1,0:T(1,128)} %get-tuple-element.44), kind=kLoop, calls=%fused_computation | loop fusion | bytes 96 | tf_op jit(solution)/shard_map/squeeze | solution.py:926

commit v6 on v5

--- a/solution.py
+++ b/solution.py
@@ -301,7 +301,6 @@
     pooled=((512, 768), BF16),
     lifted=((512, 1536), BF16),
     factor=((512, 128), F32),
-    normed=((512, 1536), BF16),
     qkv=((512, 512), BF16),
     kv_far=((512, 384), BF16),
     d_att=((512, 256), BF16),
@@ -346,14 +345,18 @@
     up_r=((8, 16, 768), BF16),
     first_s=((8, 16, 768), BF16),
     first_r=((8, 16, 768), BF16),
-    mnl_c_s=((8, 2, 48, 1024), BF16),
-    mnl_c_r=((1, 8, 48, 1024), BF16),
-    mnl_s=((8, 48, 1024), BF16),
-    mnl_r=((8, 48, 1024), BF16),
-    mn_s=((1, 48, 768), BF16),
-    mn_r=((8, 48, 768), BF16),
-    full_r=((1, 8, 48, 768), BF16),
-    summed=((768, 768), BF16),
+    rows_c_s=((8, 2, 48, 640), BF16),
+    rows_c_r=((1, 8, 48, 640), BF16),
+    rows_s=((8, 48, 640), BF16),
+    rows_r=((8, 48, 640), BF16),
+    side_c_s=((8, 2, 48, 256), BF16),
+    side_c_r=((1, 8, 48, 256), BF16),
+    side_s=((8, 48, 256), BF16),
+    side_r=((8, 48, 256), BF16),
+    mn_s=((1, 48, 640), BF16),
+    mn_r=((8, 48, 640), BF16),
+    full_r=((1, 8, 48, 640), BF16),
+    summed=((768, 640), BF16),
     slices=((512, 512), BF16),
     rest=((512, 256), BF16),
     down_c_s=((8, 2, 16, 768), BF16),
@@ -385,8 +388,10 @@
     ds=OverBatch(),
     up=OverBatch(),
     first=OverBatch(),
-    mnl_c=Core(),
-    mnl=OverQuads(),
+    rows_c=Core(),
+    rows=OverQuads(),
+    side_c=Core(),
+    side=OverQuads(),
     mn=QuadShare(),
     full=Core(),
     down_c=Core(),
@@ -428,7 +433,7 @@
         setattr(links, name, link)
 
     barrier = pltpu.get_barrier_semaphore()
-    for link in (links.codes, links.low, links.mnl, links.mnl_c, links.feat):
+    for link in (links.codes, links.low, links.rows, links.rows_c, links.feat):
         pattern = link.pattern
 
         def greet(i, pattern=pattern):
@@ -549,24 +554,23 @@
     gain = n.gain[...].reshape(1, 1536)
 
     def forward(t):
-        pair = pl.ds(2 * t, 2)
-        here = rows_of(t, 128)
-        conv = dot(n.emb_[pair].reshape(256, 2304), n.conv_w_[...])
-        center = n.emb_[pair, :, 768:1536].reshape(256, 768).astype(F32)
+        four = pl.ds(4 * t, 4)
+        here = rows_of(t, 256)
+        conv = dot(n.emb_[four].reshape(512, 2304), n.conv_w_[...])
+        center = n.emb_[four, :, 768:1536].reshape(512, 768).astype(F32)
         tower = (center + jax.nn.gelu(conv)).astype(BF16)
-        halves = tower.astype(F32).reshape(2, 2, 64, 768)
-        pooled = (0.5 * (halves[:, 0] + halves[:, 1])).astype(BF16).reshape(128, 768)
+        halves = tower.astype(F32).reshape(4, 2, 64, 768)
+        pooled = (0.5 * (halves[:, 0] + halves[:, 1])).astype(BF16).reshape(256, 768)
         n.pooled_[here, :] = pooled
         lifted = dot(pooled, n.down_w_[...]).astype(BF16)
         n.lifted_[here, :] = lifted
         lifted = lifted.astype(F32)
         factor = lax.rsqrt(jnp.mean(lifted * lifted, axis=-1, keepdims=True) + EPSILON)
-        n.factor_[here, :] = jnp.broadcast_to(factor, (128, 128))
+        n.factor_[here, :] = jnp.broadcast_to(factor, (256, 128))
         normed = (lifted * factor * gain).astype(BF16)
-        n.normed_[here, :] = normed
         n.qkv_[here, :] = dot(normed, n.in_w_[...]).astype(BF16)
 
-    loop(4, forward)
+    loop(2, forward)
     swap = pltpu.make_async_remote_copy(
         src_ref=n.qkv_.at[:, pl.ds(128, 384)], dst_ref=n.kv_far_,
         send_sem=swap_send.at[0], recv_sem=swap_recv.at[0], device_id=peer, device_id_type=MESH,
@@ -633,26 +637,32 @@
     swap_back.start()
     gained = (n.in_t_[...].astype(F32) * gain).astype(BF16)
     n.w_down_[...] = dot_cols(gained, n.down_w_[...]).astype(BF16)
+    pieces = dot_rows(low(), n.att_[...])[:, :192].astype(BF16)
+    n.rows_c_s_[:, :, :, 448:] = pieces.reshape(8, 2, 48, 192)
+    scaled = (n.pooled_[...].astype(F32) * n.factor_[:, 0:1]).astype(BF16)
     swap_back.wait()
     n.dqkv_[:, 128:] = (n.dkv_own_[...] + n.dkv_r_[...].astype(F32)).astype(BF16)
 
+    pieces = dot_rows(scaled, n.dqkv_[...])[:, :448].astype(BF16)
+    n.rows_c_s_[:, :, :, :448] = pieces.reshape(8, 2, 48, 448)
+    links.rows_c.start()
+
     def back_through_projections(t):
         send_pair("pd", t, dot(n.dqkv_[rows_of(t, 128), :], n.w_down_[...]))
 
     loop(4, back_through_projections)
 
-    pick = n.select_down_[:, rows_of(b, 128)]
-    for half in range(2):
-        wide = slice(768 * half, 768 * half + 768)
-        n.slices_[:, 128 * half : 128 * half + 128] = dot(n.lifted_[:, wide], pick).astype(BF16)
-
-    scaled = (n.pooled_[...].astype(F32) * n.factor_[:, 0:1]).astype(BF16)
-    n.mnl_c_s_[:, :, :, :512] = dot_rows(scaled, n.dqkv_[...]).astype(BF16).reshape(8, 2, 48, 512)
-    n.mnl_c_s_[:, :, :, 512:768] = dot_rows(low(), n.att_[...]).astype(BF16).reshape(8, 2, 48, 256)
-    n.mnl_c_s_[:, :, :, 768:] = (
-        dot_rows(low(), n.slices_[:, :256]).astype(BF16).reshape(8, 2, 48, 256)
-    )
-    links.mnl_c.start()
+    def core_sum(name):
+        getattr(links, name + "_c").receive()
+        mine = getattr(n, name + "_c_s_")
+        far = getattr(n, name + "_c_r_")
+        target = getattr(n, name + "_s_")
+
+        def add(j):
+            target[j] = (mine[j, h].astype(F32) + far[0, j].astype(F32)).astype(BF16)
+
+        loop(8, add)
+        getattr(links, name).start()
 
     def first_hop(name):
         over_x, over_z = getattr(links, name + "A"), getattr(links, name + "B")
@@ -678,20 +688,16 @@
         getattr(links, name + "D").receive()
         return jnp.concatenate([left, total(getattr(links, name + "D").result, 4)], axis=1)
 
-    def core_sum(name):
-        getattr(links, name + "_c").receive()
-        mine = getattr(n, name + "_c_s_")
-        far = getattr(n, name + "_c_r_")
-        target = getattr(n, name + "_s_")
-
-        def add(j):
-            target[j] = (mine[j, h].astype(F32) + far[0, j].astype(F32)).astype(BF16)
-
-        loop(8, add)
-        getattr(links, name).start()
-
+    pick = n.select_down_[:, rows_of(b, 128)]
+    for half in range(2):
+        wide = slice(768 * half, 768 * half + 768)
+        n.slices_[:, 128 * half : 128 * half + 128] = dot(n.lifted_[:, wide], pick).astype(BF16)
+    core_sum("rows")
+    n.side_c_s_[...] = dot_rows(low(), n.slices_[:, :256]).astype(BF16).reshape(8, 2, 48, 256)
+    links.side_c.start()
     first_hop("lp")
-    core_sum("mnl")
+    first_hop("pd")
+    core_sum("side")
 
     here = rows_of(b, 64)
     n.conv_[...] = dot(n.emb_[b], n.conv_w_[...])
@@ -704,7 +710,6 @@
     behind = dot_cols(jnp.concatenate([lifted, d_updated], axis=0), n.down_w_[...])
     lowered = dot(lifted, n.up_w_[...])
     slope = gelu_grad(n.conv_[...])
-    first_hop("pd")
     lowered = lowered + second_hop("lp")
     features = n.tower_[...].astype(F32) + jnp.concatenate([lowered, lowered], axis=0)
     n.feat_s_[0] = dot_rows(order, features.astype(BF16)).astype(BF16)
@@ -735,9 +740,9 @@
     n.mean_s_[0] = jnp.broadcast_to(line, (8, 128))
     links.mean.start()
 
-    links.mnl.receive()
-    summed = total(n.mnl_r_, 8)
-    n.mn_s_[0] = summed[:, :768].astype(BF16)
+    links.rows.receive()
+    summed = total(n.rows_r_, 8).astype(BF16)
+    n.mn_s_[0] = summed
     links.mn.start()
 
     hots = one_hots(b)
@@ -753,11 +758,11 @@
         n.ds_s_[j] = moved[:, 128 * j : 128 * j + 128]
     links.ds.start()
 
-    wide = dot(summed[:, 512:768].astype(BF16), n.o_w_[...])
-    sides = [
-        dot_cols(summed[:, 768 + 128 * half : 896 + 128 * half].astype(BF16), pick)
-        for half in range(2)
-    ]
+    own = jnp.concatenate([summed[:, 448:], jnp.zeros((48, 64), BF16)], axis=1)
+    wide = dot(own, n.o_w_[...])
+    links.side.receive()
+    sides = total(n.side_r_, 8).astype(BF16)
+    sides = [dot_cols(sides[:, 128 * half : 128 * half + 128], pick) for half in range(2)]
     wide = (wide + jnp.concatenate(sides, axis=1)).astype(BF16)
     groups = iota((64, 48), 0)
     groups = jnp.where(groups % 8 < 6, 6 * (groups // 8) + groups % 8, -1)
@@ -828,7 +833,7 @@
     n.g_q[...] = inner[:, :128]
     n.g_k[...] = inner[:, 128:256]
     n.g_v[...] = inner[:, 256:448]
-    n.g_o[...] = dot(n.up_w_[rows, :], n.summed_[:, 512:])[:, :192]
+    n.g_o[...] = dot(n.up_w_[rows, :], n.summed_[:, 384:])[:, 64:]
 
     links.feat.receive()
     n.features[...] = n.feat_r_[0]

time: 108 us -> 108 us (level)
  no operation moved by 1% of the time
where the time goes in v6:
time: 108 us; the launch traced here: 107 us
  Pallas kernels  105 us (97%)
  local copies, waits for them, and re-layouts  1.12 us (1%)
    pallas_call x1, Pallas kernels, per_device(): pl.pallas_call(kernel_body, out_shape=out_shape, in_specs=[vmem] * 4 + [a...  103 us

profile of v6, /device:TPU:1, one launch (start us, length us, event | category | flops | bytes accessed | tf_op | source)
XLA Modules:
  0.0 106.8 jit_solution(9447161276446386594)
XLA Ops:
  0.6 103.0 %step.1 = (bf16[128,768]{1,0:T(8,128)(2,1)}, f32[6,4,15]{2,1,0:T(4,128)}, f32[3,6,768]{2,1,0:T(8,128)}, f32[12,768]{1,0:T(8,128)}, f32[1,128]{1,0:T(1,128)}, /*i...) custom-call(s32[1,128]{1,0:T(1,128)} %refs_0_.1, ...), custom_call_target="tpu_custom_call" | custom-call | tf_op jit(solution)/shard_map/step/pallas_call | solution.py:896
  103.7 2.1 %finish.1 = (bf16[128,768]{1,0:T(8,128)(2,1)}, f32[6,4,15]{2,1,0:T(4,128)}, f32[3,6,768]{2,1,0:T(8,128)}, f32[12,768]{1,0:T(8,128)}, f32[1,128]{1,0:T(1,128)}, /...) custom-call(bf16[128,768]{1,0:T(8,128)(2,1)} %get-tuple-element.30.refs_, ...), custom_call_target="tpu_custom_call" | custom-call | tf_op jit(solution)/shard_map/finish/pallas_call | solution.py:919
  105.7 1.1 %slice_bitcast_fusion = f32[12]{0:T(128)} fusion(f32[1,128]{1,0:T(1,128)} %get-tuple-element.44), kind=kLoop, calls=%fused_computation | loop fusion | bytes 96 | tf_op jit(solution)/shard_map/squeeze | solution.py:931

commit v7 on v6

--- a/solution.py
+++ b/solution.py
@@ -131,6 +131,20 @@
 
     def src(self, i, s, b):
         return i, i, s // 2
+
+
+class Neighbours:
+    count = 2
+
+    def dst(self, i, s, b):
+        target = s + 1 - 2 * i
+        inside = jnp.logical_and(target >= 0, target < SEQ)
+        return 0, jnp.where(inside, target, s), b, i
+
+    def src(self, i, s, b):
+        source = s - 1 + 2 * i
+        inside = jnp.logical_and(source >= 0, source < SEQ)
+        return i, jnp.where(inside, source, s), b
 
 
 class ToBlock:
@@ -288,8 +302,9 @@
     select_down=((768, 1024), BF16),
     codes_s=((1, 8, 128), F32),
     codes_r=((16, 8, 128), F32),
-    blk_s=((1, 128, 768), BF16),
-    blk_r=((1, 128, 768), BF16),
+    near_r=((2, 8, 128), F32),
+    blk_s=((1, 64, 768), BF16),
+    blk_r=((1, 64, 768), BF16),
     own_s=((1, 64, 768), BF16),
     own_r=((1, 64, 768), BF16),
     low_r=((8, 64, 768), BF16),
@@ -297,7 +312,9 @@
     picked=((2, 528, 128), F32),
     emb=((8, 128, 2304), BF16),
     conv=((128, 768), F32),
-    tower=((128, 768), BF16),
+    tower=((128, 768), F32),
+    own_code=((2, 192, 128), F32),
+    own_emb=((128, 2304), BF16),
     pooled=((512, 768), BF16),
     lifted=((512, 1536), BF16),
     factor=((512, 128), F32),
@@ -331,8 +348,8 @@
     pdC_r=((1, 64, 384), BF16),
     pdD_s=((4, 64, 384), BF16),
     pdD_r=((4, 64, 384), BF16),
-    feat_s=((1, 128, 768), BF16),
-    feat_r=((1, 128, 768), BF16),
+    feat_s=((1, 64, 768), BF16),
+    feat_r=((1, 64, 768), BF16),
     mean_s=((1, 8, 128), F32),
     mean_r=((8, 8, 128), F32),
     gain_s=((1, 8, 128), F32),
@@ -370,6 +387,7 @@
 )
 LINKS = dict(
     codes=Codes(),
+    near=Neighbours(),
     own=ToBlock(),
     blk=ToBlock(),
     low=Share(),
@@ -401,7 +419,7 @@
 )
 
 
-FORWARDED = dict(low="own_r", full="mn_r")
+FORWARDED = dict(near="codes_s", low="own_r", full="mn_r")
 
 
 class Namespace:
@@ -433,7 +451,7 @@
         setattr(links, name, link)
 
     barrier = pltpu.get_barrier_semaphore()
-    for link in (links.codes, links.low, links.rows, links.rows_c, links.feat):
+    for link in (links.codes, links.low, links.rows, links.rows_c, links.feat, links.near):
         pattern = link.pattern
 
         def greet(i, pattern=pattern):
@@ -448,7 +466,8 @@
         loop(pattern.count, greet)
     own_window = (b == s // 2).astype(jnp.int32)
     own_block = own_window * (s == BATCH * h + b).astype(jnp.int32)
-    expected = 16 + 7 + 7 + 1 + 1 - own_window - own_block
+    ends = (s == 0).astype(jnp.int32) + (s == SEQ - 1).astype(jnp.int32)
+    expected = 16 + 7 + 7 + 1 + 1 + 2 - own_window - own_block - ends
 
     weights = [
         pltpu.make_async_copy(source, target, weight_sems.at[k])
@@ -473,11 +492,12 @@
     n.codes_s_[0] = dot_cols(codes, order)
     cot = dot(order, n.cot[...])
     n.own_s_[0] = (cot[:64] + cot[64:]).astype(BF16)
-    n.blk_s_[0] = cot.astype(BF16)
+    n.blk_s_[0] = cot[:64].astype(BF16)
 
     pl.semaphore_wait(barrier, expected)
     links.codes.start()
     links.own.start()
+    links.near.each(links.near.start_one)
 
     def fill(c):
         within = iota((1, 128), 1)
@@ -506,30 +526,35 @@
 
     links.codes.receive()
     ones = jnp.ones((128, 128), BF16)
+    lane_tap = iota((1, 128), 1) // 4
+    lane_code = (iota((1, 128), 1) % 4 + 1).astype(F32)
+
+    def spread(line, target, i):
+        lines = dot(jnp.where(row == column, line, 0.0).astype(BF16), ones)
+        target[0, 64 * i : 64 * i + 64] = lines[:64]
+        target[1, 64 * i : 64 * i + 64] = lines[64:]
+
+    def pick_taps(source, parity, count, first):
+        picked = jnp.zeros((count, 128), F32)
+        for tap in range(15):
+            offset = parity + tap - 7
+            stream, shift = offset % 2, (offset - offset % 2) // 2
+            begin = 56 + shift
+            picked = jnp.where(lane_tap == tap, source[stream, begin : begin + count, :], picked)
+        where = iota((count, 128), 0) - 8 + first
+        inside = jnp.logical_and(where >= 0, where < 1024)
+        return jnp.where(inside, picked, 0.0)
+
     for i in range(10):
         place = BATCH * h + (i - 1)
         inside = jnp.logical_and(place >= 0, place < 16)
         line = n.codes_r_[jnp.clip(place, 0, 15)][0:1]
-        line = jnp.where(inside, line, 0.0)
-        spread = dot(jnp.where(row == column, line, 0.0).astype(BF16), ones)
-        n.code_[0, 64 * i : 64 * i + 64] = spread[:64]
-        n.code_[1, 64 * i : 64 * i + 64] = spread[64:]
-    lane_tap = iota((1, 128), 1) // 4
-    lane_code = (iota((1, 128), 1) % 4 + 1).astype(F32)
+        spread(jnp.where(inside, line, 0.0), n.code_, i)
     for parity in range(2):
-        picked = jnp.zeros((528, 128), F32)
-        for tap in range(15):
-            offset = parity + tap - 7
-            stream, shift = offset % 2, (offset - offset % 2) // 2
-            begin = 56 + shift
-            picked = jnp.where(lane_tap == tap, n.code_[stream, begin : begin + 528, :], picked)
-        where = iota((528, 128), 0) - 8 + 512 * h
-        inside = jnp.logical_and(where >= 0, where < 1024)
-        n.picked_[parity] = jnp.where(inside, picked, 0.0)
+        n.picked_[parity] = pick_taps(n.code_, parity, 528, 512 * h)
 
     links.own.receive()
     links.low.start()
-    links.blk.start()
 
     def one_hots(j):
         found = []
@@ -578,6 +603,7 @@
     swap.start()
     n.w_up_[...] = dot(n.o_w_[...], n.up_w_[...]).astype(BF16)
     links.low.receive()
+    links.blk.start()
 
     def low():
         return n.low_r_[...].reshape(512, 768)
@@ -701,8 +727,6 @@
 
     here = rows_of(b, 64)
     n.conv_[...] = dot(n.emb_[b], n.conv_w_[...])
-    center = n.emb_[b, :, 768:1536].astype(F32)
-    n.tower_[...] = (center + jax.nn.gelu(n.conv_[...])).astype(BF16)
     lifted = n.lifted_[here, :]
     factor = n.factor_[here, 0:1]
     cube = factor * factor * factor
@@ -711,8 +735,7 @@
     lowered = dot(lifted, n.up_w_[...])
     slope = gelu_grad(n.conv_[...])
     lowered = lowered + second_hop("lp")
-    features = n.tower_[...].astype(F32) + jnp.concatenate([lowered, lowered], axis=0)
-    n.feat_s_[0] = dot_rows(order, features.astype(BF16)).astype(BF16)
+    n.feat_s_[0] = lowered.astype(BF16)
     links.feat.start()
 
     lane, channel = iota((128, 1536), 0), iota((128, 1536), 1)
@@ -724,11 +747,30 @@
     hit = jnp.logical_and(channel == wanted, lane % 8 < 6)
     gained = (n.in_t_[...].astype(F32) * gain).astype(BF16)
     n.pick_in_[...] = dot_cols(zero_one(hit), gained).astype(BF16)
+
+    links.near.receive()
+    spread(jnp.where(s > 0, n.near_r_[0][0:1], 0.0), n.own_code_, 0)
+    spread(n.codes_s_[0][0:1], n.own_code_, 1)
+    spread(jnp.where(s < SEQ - 1, n.near_r_[1][0:1], 0.0), n.own_code_, 2)
+    for parity in range(2):
+        near = pick_taps(n.own_code_, parity, 80, 64 * s)
+        steps = [zero_one(near[8 + step : 72 + step] == lane_code) for step in (-4, 0, 4)]
+        value = dot(jnp.concatenate(steps, axis=0), n.stem_w_[...]).astype(BF16)
+        for step in range(3):
+            n.own_emb_[64 * parity : 64 * parity + 64, 768 * step : 768 * step + 768] = value[
+                64 * step : 64 * step + 64
+            ]
+    center = n.own_emb_[:, 768:1536].astype(F32)
+    tower = center + jax.nn.gelu(dot(n.own_emb_[...], n.conv_w_[...]))
+    n.tower_[...] = tower.astype(BF16).astype(F32)
+
     straight = second_hop("pd")
     mean = jnp.sum(straight * n.pooled_[here, :].astype(F32), axis=-1, keepdims=True) / 1536.0
     d_pooled = 0.5 * (factor * straight - cube * mean * behind[:64] + behind[64:])
     links.blk.receive()
-    d_tower = n.blk_r_[0].astype(F32) + jnp.concatenate([d_pooled, d_pooled], axis=0)
+    even = n.blk_r_[0].astype(F32)
+    odd = n.own_r_[0].astype(F32) - even
+    d_tower = jnp.concatenate([even + d_pooled, odd + d_pooled], axis=0)
     d_tower = d_tower.astype(BF16)
     d_conv = (d_tower.astype(F32) * slope).astype(BF16)
     moved = dot(d_conv, n.select_conv_[...]).astype(BF16)
@@ -836,7 +878,9 @@
     n.g_o[...] = dot(n.up_w_[rows, :], n.summed_[:, 384:])[:, 64:]
 
     links.feat.receive()
-    n.features[...] = n.feat_r_[0]
+    lowered = n.feat_r_[0].astype(F32)
+    features = n.tower_[...] + jnp.concatenate([lowered, lowered], axis=0)
+    n.features[...] = dot_rows(order, features.astype(BF16)).astype(BF16)
     links.up.receive()
     up = total(n.up_r_, 8)
     n.g_up[:, :768] = up[0:6]

time: 108 us -> 100 us (0.926)
  Pallas kernels: 105 us -> 98 us
    pallas_call x1, Pallas kernels: 103 us -> 96 us  [per_device(): pl.pallas_call(kernel_body, out_shape=out_shape, in_specs=[vmem] * 4 + [a...]
where the time goes in v7:
time: 100 us; the launch traced here: 99.8 us
  Pallas kernels  98 us (98%)
  local copies, waits for them, and re-layouts  1.12 us (1%)
    pallas_call x1, Pallas kernels, per_device(): pl.pallas_call(kernel_body, out_shape=out_shape, in_specs=[vmem] * 4 + [a...  96 us
    pallas_call x1, Pallas kernels, per_device(): pl.pallas_call(finish_body, out_shape=out_shape, in_specs=[vmem] * len(OU...  2.06 us

profile of v7, /device:TPU:1, one launch (start us, length us, event | category | flops | bytes accessed | tf_op | source)
XLA Modules:
  0.0 99.8 jit_solution(7215387012623954207)
XLA Ops:
  0.6 96.0 %step.1 = (bf16[128,768]{1,0:T(8,128)(2,1)}, f32[6,4,15]{2,1,0:T(4,128)}, f32[3,6,768]{2,1,0:T(8,128)}, f32[12,768]{1,0:T(8,128)}, f32[1,128]{1,0:T(1,128)}, /*i...) custom-call(s32[1,128]{1,0:T(1,128)} %refs_0_.1, ...), custom_call_target="tpu_custom_call" | custom-call | tf_op jit(solution)/shard_map/step/pallas_call | solution.py:940
  96.6 2.1 %finish.1 = (bf16[128,768]{1,0:T(8,128)(2,1)}, f32[6,4,15]{2,1,0:T(4,128)}, f32[3,6,768]{2,1,0:T(8,128)}, f32[12,768]{1,0:T(8,128)}, f32[1,128]{1,0:T(1,128)}, /...) custom-call(bf16[128,768]{1,0:T(8,128)(2,1)} %get-tuple-element.30.refs_, ...), custom_call_target="tpu_custom_call" | custom-call | tf_op jit(solution)/shard_map/finish/pallas_call | solution.py:963
  98.7 1.1 %slice_bitcast_fusion = f32[12]{0:T(128)} fusion(f32[1,128]{1,0:T(1,128)} %get-tuple-element.44), kind=kLoop, calls=%fused_computation | loop fusion | bytes 96 | tf_op jit(solution)/shard_map/squeeze | solution.py:975

commit v8 on v7

--- a/solution.py
+++ b/solution.py
@@ -51,16 +51,38 @@
         return j, 2 * j + lax.rem(s, 2), b
 
 
-class QuadShare:
-    count = SEQ // 2
-
-    def dst(self, i, s, b):
-        j = lax.rem(s // 2 + i, SEQ // 2)
-        return 0, 2 * j + lax.rem(s, 2), b, s // 2
-
-    def src(self, i, s, b):
-        j = lax.rem(s // 2 + SEQ // 2 - i, SEQ // 2)
-        return j, 2 * j + lax.rem(s, 2), b
+class OverY:
+    count = 4
+
+    def dst(self, i, s, b):
+        to = lax.rem(s // 4 + i, 4)
+        return to, 4 * to + lax.rem(s, 4), b, s // 4
+
+    def src(self, i, s, b):
+        at = lax.rem(s // 4 + 4 - i, 4)
+        return at, 4 * at + lax.rem(s, 4), b
+
+
+class ShareY(OverY):
+    def dst(self, i, s, b):
+        to = lax.rem(s // 4 + i, 4)
+        return 0, 4 * to + lax.rem(s, 4), b, s // 4
+
+
+class FarZ:
+    count = 1
+
+    def dst(self, i, s, b):
+        mine = lax.rem(s, 4) // 2
+        return 1 - mine, s + 2 - 4 * mine, b, 0
+
+    def src(self, i, s, b):
+        return 0, s + 2 - 4 * (lax.rem(s, 4) // 2), b
+
+
+class ShareFarZ(FarZ):
+    def dst(self, i, s, b):
+        return 0, s + 2 - 4 * (lax.rem(s, 4) // 2), b, 0
 
 
 class Core:
@@ -365,14 +387,18 @@
     rows_c_s=((8, 2, 48, 640), BF16),
     rows_c_r=((1, 8, 48, 640), BF16),
     rows_s=((8, 48, 640), BF16),
-    rows_r=((8, 48, 640), BF16),
+    rows_r=((4, 2, 48, 640), BF16),
+    far_s=((2, 48, 640), BF16),
+    far_r=((1, 48, 640), BF16),
     side_c_s=((8, 2, 48, 256), BF16),
     side_c_r=((1, 8, 48, 256), BF16),
     side_s=((8, 48, 256), BF16),
     side_r=((8, 48, 256), BF16),
-    mn_s=((1, 48, 640), BF16),
-    mn_r=((8, 48, 640), BF16),
-    full_r=((1, 8, 48, 640), BF16),
+    pair_s=((1, 48, 640), BF16),
+    pair_r=((1, 48, 640), BF16),
+    mn_s=((1, 2, 48, 640), BF16),
+    mn_r=((4, 2, 48, 640), BF16),
+    full_r=((1, 4, 2, 48, 640), BF16),
     summed=((768, 640), BF16),
     slices=((512, 512), BF16),
     rest=((512, 256), BF16),
@@ -407,10 +433,12 @@
     up=OverBatch(),
     first=OverBatch(),
     rows_c=Core(),
-    rows=OverQuads(),
+    rows=OverY(),
+    far=FarZ(),
+    pair=ShareFarZ(),
     side_c=Core(),
     side=OverQuads(),
-    mn=QuadShare(),
+    mn=ShareY(),
     full=Core(),
     down_c=Core(),
     down=OverQuads(),
@@ -442,6 +470,8 @@
         sent = getattr(n, FORWARDED.get(name, name + "_s") + "_")
         if name == "full":
             source = lambda piece, sent=sent: sent
+        elif name == "rows":
+            source = lambda piece, sent=sent: sent.at[pl.ds(2 * piece, 2)]
         elif name.endswith("_c"):
             source = lambda piece, sent=sent: sent.at[:, piece]
         else:
@@ -451,7 +481,7 @@
         setattr(links, name, link)
 
     barrier = pltpu.get_barrier_semaphore()
-    for link in (links.codes, links.low, links.rows, links.rows_c, links.feat, links.near):
+    for link in (links.codes, links.low, links.side, links.rows_c, links.feat, links.near):
         pattern = link.pattern
 
         def greet(i, pattern=pattern):
@@ -734,9 +764,12 @@
     behind = dot_cols(jnp.concatenate([lifted, d_updated], axis=0), n.down_w_[...])
     lowered = dot(lifted, n.up_w_[...])
     slope = gelu_grad(n.conv_[...])
+    links.rows.receive()
+    n.far_s_[...] = total(n.rows_r_, 4).astype(BF16)
+    links.far.start()
     lowered = lowered + second_hop("lp")
     n.feat_s_[0] = lowered.astype(BF16)
-    links.feat.start()
+
 
     lane, channel = iota((128, 1536), 0), iota((128, 1536), 1)
     wanted = jnp.where(lane < 96, 96 * s + lane, -1)
@@ -763,6 +796,16 @@
     center = n.own_emb_[:, 768:1536].astype(F32)
     tower = center + jax.nn.gelu(dot(n.own_emb_[...], n.conv_w_[...]))
     n.tower_[...] = tower.astype(BF16).astype(F32)
+
+    zf = lax.rem(s, 4) // 2
+    links.far.receive()
+    summed = n.far_r_[0].astype(F32)
+    for j in range(4):
+        summed = summed + n.rows_r_[j, zf].astype(F32)
+    summed = summed.astype(BF16)
+    n.pair_s_[0] = summed
+    n.mn_s_[0, zf] = summed
+    links.pair.start()
 
     straight = second_hop("pd")
     mean = jnp.sum(straight * n.pooled_[here, :].astype(F32), axis=-1, keepdims=True) / 1536.0
@@ -782,9 +825,8 @@
     n.mean_s_[0] = jnp.broadcast_to(line, (8, 128))
     links.mean.start()
 
-    links.rows.receive()
-    summed = total(n.rows_r_, 8).astype(BF16)
-    n.mn_s_[0] = summed
+    links.pair.receive()
+    n.mn_s_[0, 1 - zf] = n.pair_r_[0]
     links.mn.start()
 
     hots = one_hots(b)
@@ -799,6 +841,7 @@
     for j in range(8):
         n.ds_s_[j] = moved[:, 128 * j : 128 * j + 128]
     links.ds.start()
+    links.feat.start()
 
     own = jnp.concatenate([summed[:, 448:], jnp.zeros((48, 64), BF16)], axis=1)
     wide = dot(own, n.o_w_[...])
@@ -857,8 +900,8 @@
     def assemble(q):
         near = pl.ds(pl.multiple_of(96 * q + 48 * h, 16), 48)
         far = pl.ds(pl.multiple_of(96 * q + 48 * (1 - h), 16), 48)
-        n.summed_[near, :] = n.mn_r_[q]
-        n.summed_[far, :] = n.full_r_[0, q]
+        n.summed_[near, :] = n.mn_r_[q // 2, lax.rem(q, 2)]
+        n.summed_[far, :] = n.full_r_[0, q // 2, lax.rem(q, 2)]
 
     loop(8, assemble)
     first = dot_cols(n.pick_in_[...], n.summed_[:, :512])

time: 100 us -> 90.1 us (0.901)
  Pallas kernels: 98 us -> 88.1 us
    pallas_call x1, Pallas kernels: 96 us -> 86.1 us  [per_device(): pl.pallas_call(kernel_body, out_shape=out_shape, in_specs=[vmem] * 4 + [a...]
where the time goes in v8:
time: 90.1 us; the launch traced here: 89.9 us
  Pallas kernels  88.1 us (98%)
  local copies, waits for them, and re-layouts  1.12 us (1%)
    pallas_call x1, Pallas kernels, per_device(): pl.pallas_call(kernel_body, out_shape=out_shape, in_specs=[vmem] * 4 + [a...  86.1 us
    pallas_call x1, Pallas kernels, per_device(): pl.pallas_call(finish_body, out_shape=out_shape, in_specs=[vmem] * len(OU...  2.06 us

profile of v8, /device:TPU:1, one launch (start us, length us, event | category | flops | bytes accessed | tf_op | source)
XLA Modules:
  0.0 89.9 jit_solution(8055486766658191842)
XLA Ops:
  0.6 86.1 %step.1 = (bf16[128,768]{1,0:T(8,128)(2,1)}, f32[6,4,15]{2,1,0:T(4,128)}, f32[3,6,768]{2,1,0:T(8,128)}, f32[12,768]{1,0:T(8,128)}, f32[1,128]{1,0:T(1,128)}, /*i...) custom-call(s32[1,128]{1,0:T(1,128)} %refs_0_.1, ...), custom_call_target="tpu_custom_call" | custom-call | tf_op jit(solution)/shard_map/step/pallas_call | solution.py:983
  86.7 2.1 %finish.1 = (bf16[128,768]{1,0:T(8,128)(2,1)}, f32[6,4,15]{2,1,0:T(4,128)}, f32[3,6,768]{2,1,0:T(8,128)}, f32[12,768]{1,0:T(8,128)}, f32[1,128]{1,0:T(1,128)}, /...) custom-call(bf16[128,768]{1,0:T(8,128)(2,1)} %get-tuple-element.30.refs_, ...), custom_call_target="tpu_custom_call" | custom-call | tf_op jit(solution)/shard_map/finish/pallas_call | solution.py:1006
  88.8 1.1 %slice_bitcast_fusion = f32[12]{0:T(128)} fusion(f32[1,128]{1,0:T(1,128)} %get-tuple-element.44), kind=kLoop, calls=%fused_computation | loop fusion | bytes 96 | tf_op jit(solution)/shard_map/squeeze | solution.py:1018

commit v9 on v8

--- a/solution.py
+++ b/solution.py
@@ -658,7 +658,7 @@
                 getattr(links, name + "B").start_one(to)
 
     def attend(t):
-        here = rows_of(t, 128)
+        here = rows_of(t, 256)
         q, da = n.qkv_[here, :128], n.d_att_[here, :]
         blocks = (
             (n.qkv_[:, 128:256], n.qkv_[:, 256:], n.dkv_own_),
@@ -670,8 +670,8 @@
         probs = [jnp.exp(x - log_total) for x in scores]
         dprobs = [dot_cols(da, v) for _, v, _ in blocks]
         inner = sum(jnp.sum(p * d, axis=1, keepdims=True) for p, d in zip(probs, dprobs))
-        att = jnp.zeros((128, 256), F32)
-        dq = jnp.zeros((128, 128), F32)
+        att = jnp.zeros((256, 256), F32)
+        dq = jnp.zeros((256, 128), F32)
         for (k, v, total_ref), p, d in zip(blocks, probs, dprobs):
             ds = (p * (d - inner)).astype(BF16)
             pb = p.astype(BF16)
@@ -682,9 +682,11 @@
         att = att.astype(BF16)
         n.att_[here, :] = att
         n.dqkv_[here, :128] = (dq * scale).astype(BF16)
-        send_pair("lp", t, dot(att, n.w_up_[...]))
-
-    loop(4, attend)
+        part = dot(att, n.w_up_[...])
+        send_pair("lp", 2 * t, part[:128])
+        send_pair("lp", 2 * t + 1, part[128:])
+
+    loop(2, attend)
     n.dkv_s_[...] = n.dkv_far_[...].astype(BF16)
     swap_back = pltpu.make_async_remote_copy(
         src_ref=n.dkv_s_, dst_ref=n.dkv_r_, send_sem=swap_send.at[1], recv_sem=swap_recv.at[1],
@@ -876,6 +878,8 @@
     rest = jnp.concatenate([n.conv_acc_[:, 1280:], stem, jnp.zeros((128, 128), F32)], axis=1)
     n.conv_c_s_[:, :, 8:16, :] = rest.reshape(8, 2, 8, 1280).astype(BF16)
     links.conv_c.start()
+    links.mn.receive()
+    links.full.start()
 
     links.mean.receive()
 
@@ -891,9 +895,6 @@
     links.down_c.start()
 
     core_sum("conv")
-    links.mn.receive()
-    links.full.start()
-    core_sum("down")
 
     links.full.receive()
 
@@ -907,6 +908,7 @@
     first = dot_cols(n.pick_in_[...], n.summed_[:, :512])
     n.first_s_[...] = first.astype(BF16).reshape(8, 16, 768)
     links.first.start()
+    core_sum("down")
     inner = dot(n.pick_down_[...], n.summed_[:, :512])[:96]
     rows = pl.ds(pl.multiple_of(96 * s, 16), 96)
     part = jnp.sum(inner * n.in_w_[rows, :].astype(F32), axis=1, keepdims=True)
@@ -954,8 +956,8 @@
 
 def finish_body(*refs):
     number = len(OUTPUTS)
-    for source, target in zip(refs[:number], refs[number:]):
-        target[...] = source[...]
+    for name, source, target in zip(OUTPUTS, refs[:number], refs[number:]):
+        target[...] = source[0, :12] if name == "g_gain" else source[...]
 
 
 def per_device(
@@ -1005,7 +1007,7 @@
     )
     features, g_stem, g_conv, g_down, g_gain, g_up, g_q, g_k, g_v, g_o = pl.pallas_call(
         finish_body,
-        out_shape=out_shape,
+        out_shape=out_shape[:4] + [jax.ShapeDtypeStruct((12,), F32)] + out_shape[5:],
         in_specs=[vmem] * len(OUTPUTS),
         out_specs=[vmem] * len(OUTPUTS),
         name="finish",
@@ -1015,7 +1017,7 @@
         g_stem.transpose(2, 1, 0),
         g_conv.transpose(0, 2, 1),
         g_down.T,
-        g_gain[0, :12],
+        g_gain,
         g_up.T,
         g_q,
         g_k,

time: 90.1 us -> 87.8 us (0.974)
  Pallas kernels: 88.1 us -> 86.9 us
  local copies, waits for them, and re-layouts: 1.12 us -> 0 us
    pallas_call x1, Pallas kernels: 86.1 us -> 84.8 us  [per_device(): pl.pallas_call(kernel_body, out_shape=out_shape, in_specs=[vmem] * 4 + [a...]
    squeeze x1 -> x0, local copies, waits for them, and re-layouts: 1.12 us -> none  [per_device(): g_gain[0, :12]]
where the time goes in v9:
time: 87.8 us; the launch traced here: 87.6 us
  Pallas kernels  86.9 us (99%)
    pallas_call x1, Pallas kernels, per_device(): pl.pallas_call(kernel_body, out_shape=out_shape, in_specs=[vmem] * 4 + [a...  84.8 us
    pallas_call x1, Pallas kernels, per_device(): pl.pallas_call(finish_body, out_shape=out_shape[:4] + [jax.ShapeDtypeStru...  2.06 us

profile of v9, /device:TPU:1, one launch (start us, length us, event | category | flops | bytes accessed | tf_op | source)
XLA Modules:
  0.0 87.6 jit_solution(15039850155128559026)
XLA Ops:
  0.6 84.8 %step.1 = (bf16[128,768]{1,0:T(8,128)(2,1)}, f32[6,4,15]{2,1,0:T(4,128)}, f32[3,6,768]{2,1,0:T(8,128)}, f32[12,768]{1,0:T(8,128)}, f32[1,128]{1,0:T(1,128)}, /*i...) custom-call(s32[1,128]{1,0:T(1,128)} %refs_0_.1, ...), custom_call_target="tpu_custom_call" | custom-call | tf_op jit(solution)/shard_map/step/pallas_call | solution.py:985
  85.5 2.1 %finish.1 = (bf16[128,768]{1,0:T(8,128)(2,1)}, f32[6,4,15]{2,1,0:T(4,128)}, f32[3,6,768]{2,1,0:T(8,128)}, f32[12,768]{1,0:T(8,128)}, f32[12]{0:T(128)}, /*index=...) custom-call(bf16[128,768]{1,0:T(8,128)(2,1)} %get-tuple-element.30.refs_0_, ...), custom_call_target="tpu_custom_call" | custom-call | tf_op jit(solution)/shard_map/finish/pallas_call | solution.py:1008

commit v10 on v9

--- a/solution.py
+++ b/solution.py
@@ -26,6 +26,19 @@
     def src(self, i, s, b):
         j = lax.rem(b + BATCH - i, BATCH)
         return j, s, j
+
+
+class ShareX:
+    count = 4
+
+    def dst(self, i, s, b):
+        z, x = b // 4, lax.rem(b, 4)
+        return 0, s, 4 * z + lax.rem(x + i, 4), x
+
+    def src(self, i, s, b):
+        z, x = b // 4, lax.rem(b, 4)
+        at = lax.rem(x + 4 - i, 4)
+        return at, s, 4 * z + at
 
 
 class Share:
@@ -329,7 +342,14 @@
     blk_r=((1, 64, 768), BF16),
     own_s=((1, 64, 768), BF16),
     own_r=((1, 64, 768), BF16),
-    low_r=((8, 64, 768), BF16),
+    low=((8, 64, 768), BF16),
+    low_z_s=((1, 64, 384), BF16),
+    low_z_r=((1, 64, 384), BF16),
+    low_zx_s=((1, 2, 64, 384), BF16),
+    low_zx_r=((4, 2, 64, 384), BF16),
+    low_x_s=((1, 64, 384), BF16),
+    low_x_r=((4, 64, 384), BF16),
+    low_xz_r=((1, 4, 64, 384), BF16),
     code=((2, 640, 128), F32),
     picked=((2, 528, 128), F32),
     emb=((8, 128, 2304), BF16),
@@ -416,7 +436,10 @@
     near=Neighbours(),
     own=ToBlock(),
     blk=ToBlock(),
-    low=Share(),
+    low_z=ZOne(),
+    low_zx=ShareX(),
+    low_x=ShareX(),
+    low_xz=ZOne(),
     lpA=XBlocks(),
     lpB=ZBlocks(),
     lpC=ZOne(),
@@ -447,7 +470,7 @@
 )
 
 
-FORWARDED = dict(near="codes_s", low="own_r", full="mn_r")
+FORWARDED = dict(near="codes_s", low_xz="low_x_r", full="mn_r")
 
 
 class Namespace:
@@ -468,7 +491,7 @@
     links = Namespace()
     for k, (name, pattern) in enumerate(LINKS.items()):
         sent = getattr(n, FORWARDED.get(name, name + "_s") + "_")
-        if name == "full":
+        if name in ("full", "low_xz"):
             source = lambda piece, sent=sent: sent
         elif name == "rows":
             source = lambda piece, sent=sent: sent.at[pl.ds(2 * piece, 2)]
@@ -481,7 +504,7 @@
         setattr(links, name, link)
 
     barrier = pltpu.get_barrier_semaphore()
-    for link in (links.codes, links.low, links.side, links.rows_c, links.feat, links.near):
+    for link in (links.codes, links.mean, links.side, links.rows_c, links.feat, links.near):
         pattern = link.pattern
 
         def greet(i, pattern=pattern):
@@ -584,7 +607,10 @@
         n.picked_[parity] = pick_taps(n.code_, parity, 528, 512 * h)
 
     links.own.receive()
-    links.low.start()
+    n.low_z_s_[0] = n.own_r_[0, :, :384]
+    n.low_x_s_[0] = n.own_r_[0, :, 384:]
+    links.low_z.start()
+    links.low_x.start()
 
     def one_hots(j):
         found = []
@@ -604,6 +630,12 @@
                 ]
 
     loop(8, embed)
+    links.low_x.receive()
+    links.low_xz.start()
+    links.low_z.receive()
+    n.low_zx_s_[0, z] = n.low_z_s_[0]
+    n.low_zx_s_[0, 1 - z] = n.low_z_r_[0]
+    links.low_zx.start()
     for copy in weights[4:]:
         copy.wait()
     gain = n.gain[...].reshape(1, 1536)
@@ -632,11 +664,20 @@
     )
     swap.start()
     n.w_up_[...] = dot(n.o_w_[...], n.up_w_[...]).astype(BF16)
-    links.low.receive()
+    links.low_zx.receive()
+    links.low_xz.receive()
     links.blk.start()
 
+    def gather(x):
+        n.low_[x, :, :384] = n.low_zx_r_[x, 0]
+        n.low_[4 + x, :, :384] = n.low_zx_r_[x, 1]
+        n.low_[4 * z + x, :, 384:] = n.low_x_r_[x]
+        n.low_[4 * (1 - z) + x, :, 384:] = n.low_xz_r_[0, x]
+
+    loop(4, gather)
+
     def low():
-        return n.low_r_[...].reshape(512, 768)
+        return n.low_[...].reshape(512, 768)
 
     n.d_att_[...] = dot_cols(low(), n.w_up_[...]).astype(BF16)
     n.dkv_own_[...] = jnp.zeros((512, 384), F32)

time: 87.8 us -> 90.3 us (1.028)
  Pallas kernels: 86.9 us -> 89.4 us
    pallas_call x1, Pallas kernels: 84.8 us -> 87.3 us  [per_device(): pl.pallas_call(kernel_body, out_shape=out_shape, in_specs=[vmem] * 4 + [a...]
where the time goes in v10:
time: 90.3 us; the launch traced here: 90.1 us
  Pallas kernels  89.4 us (99%)
    pallas_call x1, Pallas kernels, per_device(): pl.pallas_call(kernel_body, out_shape=out_shape, in_specs=[vmem] * 4 + [a...  87.3 us
    pallas_call x1, Pallas kernels, per_device(): pl.pallas_call(finish_body, out_shape=out_shape[:4] + [jax.ShapeDtypeStru...  2.06 us

profile of v10, /device:TPU:1, one launch (start us, length us, event | category | flops | bytes accessed | tf_op | source)
XLA Modules:
  0.0 90.1 jit_solution(3514705689950264972)
XLA Ops:
  0.6 87.3 %step.1 = (bf16[128,768]{1,0:T(8,128)(2,1)}, f32[6,4,15]{2,1,0:T(4,128)}, f32[3,6,768]{2,1,0:T(8,128)}, f32[12,768]{1,0:T(8,128)}, f32[1,128]{1,0:T(1,128)}, /*i...) custom-call(s32[1,128]{1,0:T(1,128)} %refs_0_.1, ...), custom_call_target="tpu_custom_call" | custom-call | tf_op jit(solution)/shard_map/step/pallas_call | solution.py:1026
  87.9 2.1 %finish.1 = (bf16[128,768]{1,0:T(8,128)(2,1)}, f32[6,4,15]{2,1,0:T(4,128)}, f32[3,6,768]{2,1,0:T(8,128)}, f32[12,768]{1,0:T(8,128)}, f32[12]{0:T(128)}, /*index=...) custom-call(bf16[128,768]{1,0:T(8,128)(2,1)} %get-tuple-element.30.refs_0_, ...), custom_call_target="tpu_custom_call" | custom-call | tf_op jit(solution)/shard_map/finish/pallas_call | solution.py:1049
